TPU v7x, 32 devices: a whole 2x2x4 slice. The times are simulated.
32 devices in a mesh: groups: 2 (over y), out: 8 (over z, x), inp: 2 (over core).
Axes of the slice: x: 2, y: 2, z: 4, core: 2. Of those that a mesh axis runs over, the one named last changes fastest.
Arguments:
- grads: bfloat16 [1024, 28672], P('groups', ('inp', 'out')), parts along dimension 0, may hold values from -6 to 6
- basis_out: bfloat16 [28672, 14336], P('inp', 'out'), may hold values from -0.03125 to 0.03125
- acts: bfloat16 [1024, 8192], P('groups', 'out'), parts along dimension 0, may hold values from -6 to 6
- basis_in: bfloat16 [8192, 8192], P('out', 'inp'), may hold values from -0.09375 to 0.09375
Outputs:
- correction: float32 [28672, 8192], P(('groups', 'out'), 'inp'), parts along dimension 0
There are 2 independent parts, one for each index of `groups`. A program takes and returns all parts, laid end to end along the dimension named above; an argument that names none is the same for every part. Nothing has to cross between parts.
All inputs are finite; a program needn't handle non-finite values.
Results may differ from a plain program's by a relative error of at most 0.0047.
Values may be sent and summed in bfloat16 or wider, within the bound.
No kernel may reach another device: no remote copies, remote signals or barrier semaphores. Data moves between devices by JAX's collectives and lax.ppermute only.
A program may use at most 256 MiB of HBM per device.

v0:
```python
import jax
import jax.numpy as jnp
from jax import lax
from jax.sharding import PartitionSpec as P


def on_device(grads, basis_out, acts, basis_in):
    partial_grad = jnp.dot(
        lax.all_gather(grads, "out", axis=1, tiled=True),
        basis_out,
        preferred_element_type=jnp.float32,
    )
    rot_grad = lax.psum(partial_grad, "inp").astype(jnp.bfloat16)
    contract = (((0,), (1,)), ((), ()))
    act_full = lax.dot_general(basis_in, acts, contract, preferred_element_type=jnp.float32)
    rot_act = lax.psum(act_full, "out").astype(jnp.bfloat16)
    tile = lax.dot_general(rot_grad, rot_act, contract, preferred_element_type=jnp.float32)
    return tile * tile / jnp.float32(rot_grad.shape[0])


def solution(mesh):
    return jax.shard_map(
        on_device,
        mesh=mesh,
        in_specs=(
            P("groups", ("inp", "out")),
            P("inp", "out"),
            P("groups", "out"),
            P("out", "inp"),
        ),
        out_specs=P(("groups", "out"), "inp"),
        check_vma=False,
    )
```

profile of v0, /device:TPU:0, one launch (start us, length us, event | category | flops | bytes accessed | tf_op | source)
XLA Modules:
  0.0 512.5 jit_solution(11791586790338032972)
XLA Ops:
  6.5 0.0 copy-start
  6.5 0.0 all-gather.2.cloned.1.call-start
  6.5 0.7 all-gather.2.cloned.1.call-update
  7.3 0.5 copy-done
  7.8 10.3 %fusion.3 = f32[4096,512]{1,0:T(8,128)} fusion(bf16[1024,4096]{1,0:T(8,128)(2,1)} %param.7, bf16[512,1024]{1,0:T(8,128)(2,1)S(1)} %copy-done), kind=kOutput, calls=%fused_computation.4 | convolution fusion | flops 4294967296 | bytes 17825792 | tf_op jit(solution)/shard_map/dot_general | solution.py:15
  18.1 422.3 %all-reduce.3 = bf16[4096,512]{1,0:T(8,128)(2,1)} all-reduce(f32[4096,512]{1,0:T(8,128)} %fusion.3), channel_id=1, replica_groups=mesh['groups'=2,'out'=8,'inp'=2] {'out'}, use_global_device_ids=true, to_apply=%region_1.0 | all-reduce | flops 2097152 | bytes 12582912 | tf_op jit(solution)/shard_map/psum | solution.py:16
  440.3 0.1 all-gather.2.cloned.1.call-done
  440.5 34.8 %fusion.2 = f32[512,1792]{1,0:T(8,128)} fusion(bf16[512,14336]{1,0:T(8,128)(2,1)} %all-gather.2.cloned.1.call-done, bf16[14336,1792]{1,0:T(8,128)(2,1)} %param.5), kind=kOutput, calls=%fused_computation.3 | convolution fusion | flops 26306674688 | bytes 69730304 | tf_op jit(solution)/shard_map/dot_general | solution.py:8
  475.2 13.7 %all-reduce.2 = bf16[512,1792]{1,0:T(8,128)(2,1)S(1)} all-reduce(f32[512,1792]{1,0:T(8,128)} %fusion.2), channel_id=1, replica_groups=mesh['groups'=2,'out'=8,'inp'=2] {'inp'}, use_global_device_ids=true, to_apply=%region_0.0 | all-reduce | flops 917504 | bytes 5505024 | tf_op jit(solution)/shard_map/psum | solution.py:13
  489.0 0.0 copy-start.1
  489.0 16.6 %multiply_multiply_fusion = f32[1792,4096]{1,0:T(8,128)} fusion(bf16[4096,512]{1,0:T(8,128)(2,1)} %all-reduce.3, bf16[512,1792]{1,0:T(8,128)(2,1)S(1)} %all-reduce.2), kind=kOutput, calls=%fused_computation | convolution fusion | flops 7530872832 | bytes 35389440 | tf_op jit(solution)/shard_map/dot_general | solution.py:17
  505.6 0.0 copy-done.1
Async XLA Ops:
  6.5 1.2 copy-start
  6.5 433.9 %all-gather.2.cloned.1.call-start = ((), (), s32[]{:S(2)}) async-start(), calls=%async_computation | async-start | bytes 16515072 | tf_op jit(solution)/shard_map/all_gather | solution.py:9
  489.0 16.6 %copy-start.1 = (bf16[512,1024]{1,0:T(8,128)(2,1)S(1)}, bf16[512,1024]{1,0:T(8,128)(2,1)}, u32[]{:S(2)}) copy-start(bf16[512,1024]{1,0:T(8,128)(2,1)} %param.6) | copy-start | bytes 3145732
Sparse Core Ops, SparseCore 0:
  9.6 430.8 all-gather.1
where the time goes:
time: 520 us; the launch traced here: 512 us
  blocking collectives  436 us (84%)
  matrix products  61.7 us (12%)
  between operations  13.4 us (3%)
    psum x1, blocking collectives, on_device(): rot_act = lax.psum(act_full, 'out').astype(jnp.bfloat16)  422 us
    dot_general x1, matrix products, on_device(): jnp.dot(lax.all_gather(grads, 'out', axis=1, tiled=True), basis_out, pref...  34.8 us
    dot_general x1, matrix products, on_device(): lax.dot_general(rot_grad, rot_act, contract, preferred_element_type=jnp.f...  16.6 us
    psum x1, blocking collectives, on_device(): rot_grad = lax.psum(partial_grad, 'inp').astype(jnp.bfloat16)  13.7 us
  transfers between devices with their start and end apart: 1, of which 1 were waited for; matrix products, arithmetic and copies ran while one was open for 2% of the time, Pallas kernels for 0%

commit v1 on v0

v1 whole, which is shorter than its diff:
```python
import functools

import jax
import jax.numpy as jnp
from jax import lax
from jax.experimental import pallas as pl
from jax.experimental.pallas import tpu as pltpu
from jax.sharding import PartitionSpec as P

F32, BF16 = jnp.float32, jnp.bfloat16
TN = (((0,), (0,)), ((), ()))
VMEM = 44 * 1024 * 1024
CHEAP = pl.CostEstimate(flops=1000, bytes_accessed=1000, transcendentals=0)


def plain(grads, basis_out, acts, basis_in):
    partial_grad = jnp.dot(
        lax.all_gather(grads, "out", axis=1, tiled=True),
        basis_out,
        preferred_element_type=F32,
    )
    rot_grad = lax.psum(partial_grad, "inp").astype(BF16)
    contract = (((0,), (1,)), ((), ()))
    act_full = lax.dot_general(basis_in, acts, contract, preferred_element_type=F32)
    rot_act = lax.psum(act_full, "out").astype(BF16)
    tile = lax.dot_general(rot_grad, rot_act, contract, preferred_element_type=F32)
    return tile * tile / F32(rot_grad.shape[0])


def pairs(fn):
    out = []
    for z in range(4):
        for x in range(2):
            to = fn(z, x)
            if to is not None:
                out.append((z * 2 + x, to[0] * 2 + to[1]))
    return out


def is_end(z):
    return z in (0, 3)


X_ALL = pairs(lambda z, x: (z, 1 - x))
X_END = pairs(lambda z, x: (z, 1 - x) if is_end(z) else None)
X_MID = pairs(lambda z, x: None if is_end(z) else (z, 1 - x))
Z_NEAR = pairs(lambda z, x: (z ^ 1, x))
Z_MID = pairs(lambda z, x: None if is_end(z) else (3 - z, x))
Z_OUT = pairs(lambda z, x: (z ^ 1, x) if is_end(z) else None)
Z_IN = pairs(lambda z, x: None if is_end(z) else (z ^ 1, x))


def send(name, value, way, axis="out"):
    with jax.named_scope(name):
        return lax.ppermute(value, axis, way)


def after(value, *events):
    return lax.optimization_barrier((value, *events))[0]


def act_kernel(place_ref, acts_ref, basis_ref, wide_ref, narrow_ref):
    part = jnp.dot(acts_ref[...], basis_ref[...], preferred_element_type=F32)
    wide_ref[...] = part
    narrow_ref[...] = part.astype(BF16)


def act_parts(columns, acts, basis_in):
    tokens, depth = acts.shape
    width = basis_in.shape[1]
    step = width // len(columns)
    out_spec = pl.BlockSpec((tokens, step), lambda j, p: (0, j))
    return pl.pallas_call(
        act_kernel,
        grid_spec=pltpu.PrefetchScalarGridSpec(
            num_scalar_prefetch=1,
            grid=(len(columns),),
            in_specs=[
                pl.BlockSpec((tokens, depth), lambda j, p: (0, 0)),
                pl.BlockSpec((depth, step), lambda j, p: (0, p[j])),
            ],
            out_specs=[out_spec, out_spec],
        ),
        out_shape=[
            jax.ShapeDtypeStruct((tokens, width), F32),
            jax.ShapeDtypeStruct((tokens, width), BF16),
        ],
        compiler_params=pltpu.CompilerParams(vmem_limit_bytes=VMEM),
        cost_estimate=CHEAP,
        name="act_parts",
    )(jnp.stack(columns).astype(jnp.int32), acts, basis_in)


def grad_kernel(end_cuts, mid_cuts, place_ref, basis_ref, *refs):
    refs, total_ref, out_ref = refs[:-2], refs[-2], refs[-1]

    def add(cuts):
        acc = total_ref[...]
        row = 0
        for n, width in cuts:
            acc = acc + jnp.dot(refs[n][:, :width], basis_ref[row : row + width], preferred_element_type=F32)
            row += width
        out_ref[...] = acc

    pl.when(place_ref[0] == 1)(lambda: add(end_cuts))
    pl.when(place_ref[0] == 0)(lambda: add(mid_cuts))


def grad_pieces(end, at_end, at_mid, place, basis_out, total):
    arrays = []
    cuts = []
    for sources in (at_end, at_mid):
        cuts.append([])
        for array, width in sources:
            known = [n for n, other in enumerate(arrays) if other is array]
            if not known:
                arrays.append(array)
            cuts[-1].append((known[0] if known else len(arrays) - 1, width))
    depth = sum(width for _, width in cuts[0])
    tokens, width = total.shape
    step = width // 2
    out_spec = pl.BlockSpec((tokens, step), lambda j, s: (0, j))
    return pl.pallas_call(
        functools.partial(grad_kernel, *cuts),
        grid_spec=pltpu.PrefetchScalarGridSpec(
            num_scalar_prefetch=1,
            grid=(width // step,),
            in_specs=[pl.BlockSpec((depth, step), lambda j, s: (s[1], j))]
            + [pl.BlockSpec(array.shape, lambda j, s: (0, 0)) for array in arrays]
            + [out_spec],
            out_specs=out_spec,
        ),
        out_shape=jax.ShapeDtypeStruct((tokens, width), F32),
        compiler_params=pltpu.CompilerParams(vmem_limit_bytes=VMEM),
        cost_estimate=CHEAP,
        name="grad_pieces",
    )(jnp.stack([end.astype(jnp.int32), place.astype(jnp.int32)]), basis_out, *arrays, total)


def grad_sum_kernel(has_total, place_ref, *refs):
    out_ref, refs = refs[-1], refs[:-1]
    acc = None
    if has_total:
        acc, refs = refs[-1][...], refs[:-1]
    count = len(refs) // 2
    for block, basis in zip(refs[:count], refs[count:]):
        part = jnp.dot(block[...], basis[...], preferred_element_type=F32)
        acc = part if acc is None else acc + part
    out_ref[...] = acc


def grad_blocks(pieces, places, basis_out, total):
    tokens, depth = pieces[0].shape
    width = basis_out.shape[1]
    step = width // 2
    whole = pl.BlockSpec((tokens, depth), lambda j, s: (0, 0))
    out_spec = pl.BlockSpec((tokens, step), lambda j, s: (0, j))

    def rows_of(n):
        return pl.BlockSpec((depth, step), lambda j, s: (s[n], j))

    totals = [] if total is None else [total]
    return pl.pallas_call(
        functools.partial(grad_sum_kernel, total is not None),
        grid_spec=pltpu.PrefetchScalarGridSpec(
            num_scalar_prefetch=1,
            grid=(width // step,),
            in_specs=[whole] * len(pieces) + [rows_of(n) for n in range(len(pieces))] + [out_spec] * len(totals),
            out_specs=out_spec,
        ),
        out_shape=jax.ShapeDtypeStruct((tokens, width), F32),
        compiler_params=pltpu.CompilerParams(vmem_limit_bytes=VMEM),
        cost_estimate=CHEAP,
        name="grad_blocks",
    )(jnp.stack(places).astype(jnp.int32), *pieces, *[basis_out] * len(pieces), *totals)


def pick_kernel(place_ref, first_ref, second_ref, out_ref):
    @pl.when(place_ref[0] == 1)
    def _():
        out_ref[...] = first_ref[...]

    @pl.when(place_ref[0] == 0)
    def _():
        out_ref[...] = second_ref[...]


def pick(end, first, first_at, second, second_at, width):
    tokens = first.shape[0]
    step = tokens // 4
    return pl.pallas_call(
        pick_kernel,
        grid_spec=pltpu.PrefetchScalarGridSpec(
            num_scalar_prefetch=1,
            grid=(tokens // step,),
            in_specs=[
                pl.BlockSpec((step, width), lambda i, p: (i * p[0], first_at)),
                pl.BlockSpec((step, width), lambda i, p: (i * (1 - p[0]), second_at)),
            ],
            out_specs=pl.BlockSpec((step, width), lambda i, p: (i, 0)),
        ),
        out_shape=jax.ShapeDtypeStruct((tokens, width), first.dtype),
        compiler_params=pltpu.CompilerParams(vmem_limit_bytes=VMEM),
        cost_estimate=CHEAP,
        name="pick",
    )(end.astype(jnp.int32).reshape(1), first, second)


def lay_kernel(spans, place_ref, *refs):
    out_ref = refs[-1]
    j = pl.program_id(0)
    for ref, (flag, start, count) in zip(refs, spans):

        @pl.when((place_ref[0] == flag) & (j >= start) & (j < start + count))
        def _(ref=ref):
            out_ref[...] = ref[...]


def lay(end, at_end, at_mid, unit):
    tokens = at_mid[0][0].shape[0]
    (one, one_at, count), (two, two_at, other) = at_end[0], at_mid[0]
    if len(at_end) == len(at_mid) == 1 and count == other and one_at % count == two_at % count == 0:
        return pick(end, one, one_at // count, two, two_at // count, count * unit)
    spans, arrays, specs = [], [], []
    units = 0
    for flag, sources in ((1, at_end), (0, at_mid)):
        start = 0
        for array, first, count in sources:

            def index(j, p, flag=flag, start=start, first=first, count=count):
                mine = p[0] if flag else 1 - p[0]
                return 0, first + mine * jnp.clip(j - start, 0, count - 1)

            spans.append((flag, start, count))
            arrays.append(array)
            specs.append(pl.BlockSpec((tokens, unit), index))
            start += count
        units = max(units, start)
    return pl.pallas_call(
        functools.partial(lay_kernel, spans),
        grid_spec=pltpu.PrefetchScalarGridSpec(
            num_scalar_prefetch=1,
            grid=(units,),
            in_specs=specs,
            out_specs=pl.BlockSpec((tokens, unit), lambda j, p: (0, j)),
        ),
        out_shape=jax.ShapeDtypeStruct((tokens, units * unit), arrays[0].dtype),
        compiler_params=pltpu.CompilerParams(vmem_limit_bytes=VMEM),
        cost_estimate=CHEAP,
        name="lay",
    )(end.astype(jnp.int32).reshape(1), *arrays)


def sum_kernel(cut, count, place_ref, *refs):
    out_ref, refs = refs[-1], refs[:-1]
    j = pl.program_id(0)

    def add():
        if cut:
            blocks = [jnp.where(j < cut, refs[0][...], refs[1][...])] + [r[...] for r in refs[2 : len(refs) - 1]]
        else:
            blocks = [r[...] for r in refs[:-1]]
        total = blocks[0].astype(F32)
        for block in blocks[1:]:
            total = total + block.astype(F32)
        out_ref[...] = total.astype(out_ref.dtype)

    if count:
        pl.when((place_ref[0] == 1) & (j < count))(lambda: out_ref.__setitem__(..., refs[-1][...]))
        pl.when((place_ref[0] == 0) | (j >= count))(add)
    else:
        add()


def add_parts(end, sources, units, unit, cut=0, rider=None):
    tokens = sources[0][0].shape[0]

    def spec(n, first):
        if cut and n < 2:
            low, high = (0, cut - 1) if n == 0 else (cut, units - 1)
            return pl.BlockSpec((tokens, unit), lambda j, p: (0, first + jnp.clip(j, low, high) - low))
        return pl.BlockSpec((tokens, unit), lambda j, p: (0, first + j))

    array, first, count = rider or (sources[-1][0], sources[-1][1], 0)
    return pl.pallas_call(
        functools.partial(sum_kernel, cut, count),
        grid_spec=pltpu.PrefetchScalarGridSpec(
            num_scalar_prefetch=1,
            grid=(units,),
            in_specs=[spec(n, f) for n, (_, f) in enumerate(sources)]
            + [pl.BlockSpec((tokens, unit), lambda j, p: (0, first + jnp.clip(j, 0, max(count - 1, 0))))],
            out_specs=pl.BlockSpec((tokens, unit), lambda j, p: (0, j)),
        ),
        out_shape=jax.ShapeDtypeStruct((tokens, units * unit), BF16),
        compiler_params=pltpu.CompilerParams(vmem_limit_bytes=VMEM),
        cost_estimate=CHEAP,
        name="add_parts",
    )(end.astype(jnp.int32).reshape(1), *[source for source, _ in sources], array)


def tile_kernel(tokens, place_ref, grad_ref, first_ref, second_ref, *refs):
    def put(act_ref):
        tile = lax.dot_general(grad_ref[...], act_ref[...], TN, preferred_element_type=F32)
        refs[-1][...] = tile * tile / F32(tokens)

    pl.when(pl.program_id(1) == 0)(lambda: put(first_ref))
    pl.when(pl.program_id(1) == 1)(lambda: put(second_ref))


def tile_part(rot_grad, acts, columns, out, shape):
    tokens, rows = rot_grad.shape
    width = acts[0].shape[1]
    step = rows // 2
    outs = [] if out is None else [out]
    return pl.pallas_call(
        functools.partial(tile_kernel, tokens),
        grid_spec=pltpu.PrefetchScalarGridSpec(
            num_scalar_prefetch=1,
            grid=(rows // step, 2),
            in_specs=[pl.BlockSpec((tokens, step), lambda i, j, p: (0, i))]
            + [pl.BlockSpec((tokens, width), lambda i, j, p: (0, 0))] * 2
            + [pl.BlockSpec(memory_space=pl.ANY)] * len(outs),
            out_specs=pl.BlockSpec((step, width), lambda i, j, p: (i, p[j])),
        ),
        out_shape=jax.ShapeDtypeStruct(shape, F32),
        input_output_aliases={4: 0} if outs else {},
        compiler_params=pltpu.CompilerParams(vmem_limit_bytes=VMEM),
        cost_estimate=CHEAP,
        name="tile_part",
    )(jnp.stack(columns).astype(jnp.int32), rot_grad, *acts, *outs)


def barrier(*values):
    return lax.optimization_barrier(values)


def grid_of_eight(grads, basis_out, acts, basis_in):
    o = lax.axis_index("out")
    z, x = o // 2, o % 2
    side = z // 2
    end = (z == 0) | (z == 3)
    near, far, farthest = z ^ 1, 2 - side, 3 - 3 * side
    eighth = basis_in.shape[1] // 8
    half = grads.shape[1] // 2

    def either(at_end, at_mid):
        return jnp.where(end, at_end, at_mid)

    def z_block(zb, xb):
        return zb * 2 + xb

    def column(ds, dx, h):
        return ((side ^ ds) * 2 + (x ^ dx)) * 2 + h

    unit = eighth // 2

    def blocks(pieces, places, total):
        return grad_blocks(pieces, places, basis_out, total)

    def block_of(at_end, at_mid, place, total):
        at_end = [(array, units * unit) for array, units in at_end]
        at_mid = [(array, units * unit) for array, units in at_mid]
        return grad_pieces(end, at_end, at_mid, place, basis_out, total)

    def put(at_end, at_mid):
        return lay(end, at_end, at_mid, unit)

    def summed(sources, units, **more):
        return add_parts(end, sources, units, unit, **more)

    a = send("near", grads, Z_NEAR)
    x0 = send("own_x", grads, X_ALL)
    b1 = send("mid_own", grads, Z_MID)
    order = [(1, 1, 0), (1, 0, 0), (0, 1, 0), (0, 0, 0), (1, 1, 1), (1, 0, 1), (0, 1, 1), (0, 0, 1)]
    wide, narrow = act_parts([column(*e) for e in order], acts, basis_in)
    total = blocks([after(grads, wide)], [z_block(z, x)], None)

    b1, total = barrier(b1, total)
    a, total = barrier(a, total)
    b2 = send("mid_near", a, Z_MID)
    y1 = put([(narrow, 0, 7)], [(b1, 0, 7)])
    r1 = send("r1", y1, Z_NEAR)
    x1 = send("x1", put([(after(a, y1), 0, 7)], [(b1, 0, 7)]), X_ALL)
    total = blocks([a, x0], [z_block(near, x), z_block(z, 1 - x)], total)

    b2, total = barrier(b2, total)
    y2 = put([(narrow, 7, 5)], [(b2, 0, 5)])
    r2_h = send("r2_h", y2, Z_NEAR)
    r1, y2, total = barrier(r1, y2, total)
    y3 = put([(r1, 0, 7)], [(b2, 0, 7)])
    x2 = send("x2", y3, X_ALL)
    y4 = summed([(after(wide, y3), 0), (r1, 0)], 4)
    m_a = send("mid_a", y4, Z_MID)
    y5 = put([(after(narrow, y4), 12, 4)], [(b2, 5, 2)])
    r2_t = send("r2_t", y5, Z_NEAR)
    x1, total = barrier(x1, total)
    total = blocks([x1], [z_block(either(near, far), 1 - x)], after(total, y5))

    r2_h, total = barrier(r2_h, total)
    y6 = summed([(wide, 8), (r2_h, 1)], 4)
    m_b = send("mid_b", y6, Z_MID)
    x3_h = send("x3_h", after(r2_h, y6), X_END)
    m_a, y6, total = barrier(m_a, y6, total)
    y7 = summed([(wide, 4), (r1, 4), (m_a, 0)], 2)
    xm_a = send("sum_x_a", y7, X_MID)
    total = block_of([(r1, 7)], [(b1, 7)], z_block(far, x), after(total, y7))

    x2, total = barrier(x2, total)
    r2_t, total = barrier(r2_t, total)
    xm_a, total = barrier(xm_a, total)
    t00_a = summed([(r1, 6), (r2_h, 0), (wide, 6), (m_a, 2), (xm_a, 0)], 2, cut=1, rider=(x0, 3, 2))
    t10_a = send("all_mid_a", t00_a, Z_MID)
    e00_a = send("all_in_0a", t00_a, Z_NEAR)
    m_b, t00_a = barrier(m_b, t00_a)
    y9 = summed([(after(wide, t00_a), 12), (r2_t, 0), (m_b, 0)], 2)
    xm_b = send("sum_x_b", y9, X_MID)
    total = blocks([x2], [z_block(either(far, farthest), 1 - x)], after(total, y9))

    x3_h, total = barrier(x3_h, total)
    y8 = put([(r2_t, 0, 2)], [(after(a, total), 0, 3)])
    x3_t = send("x3_t", y8, X_ALL)
    t10_a, e00_a, y8 = barrier(t10_a, e00_a, y8)
    y10 = put([(x0, 5, 2)], [(t10_a, 0, 2)])
    e10_a = send("all_in_1a", y10, Z_NEAR)
    u00_a = put([(after(e00_a, y10), 0, 2)], [(t00_a, 0, 2)])
    s01_a = send("all_x_0a", u00_a, X_ALL)
    xm_b, u00_a = barrier(xm_b, u00_a)
    t00_b = summed([(after(wide, u00_a), 14), (r2_t, 2), (m_b, 2), (xm_b, 0)], 2)
    t10_b = send("all_mid_b", t00_b, Z_MID)
    e00_b = send("all_in_0b", t00_b, Z_IN)

    e10_a, t00_b = barrier(e10_a, t00_b)
    u10_a = put([(e10_a, 0, 2)], [(after(t10_a, t00_b), 0, 2)])
    s11_a = send("all_x_1a", u10_a, X_ALL)
    total = block_of([(r2_h, 5), (r2_t, 2)], [(b2, 7)], z_block(farthest, x), after(total, u10_a))
    x3_t, total = barrier(x3_t, total)
    s01_a, total = barrier(s01_a, total)
    total = block_of([(x3_h, 5), (x3_t, 2)], [(x3_t, 3), (e00_a, 2), (e10_a, 2)], z_block(either(farthest, near), 1 - x), total)

    t10_b, e00_b, total = barrier(t10_b, e00_b, total)
    s11_a, total = barrier(s11_a, total)
    other = [send("core", piece, [(0, 1), (1, 0)], "inp") for piece in jnp.split(total, 8)]
    e10_b = send("all_in_1b", t10_b, Z_IN)
    u00_b = put([(e00_b, 0, 2)], [(t00_b, 0, 2)])
    s01_b = send("all_x_0b", u00_b, X_ALL)
    rot_grad = (after(total, u00_b) + jnp.concatenate(other)).astype(BF16)
    shape = (basis_out.shape[1], basis_in.shape[1])

    def tile(parts, dx, h, out):
        return tile_part(rot_grad, parts, [column(0, dx, h), column(1, dx, h)], out, shape)

    out = tile((u00_a, u10_a), 0, 0, None)
    out = tile((s01_a, s11_a), 1, 0, out)
    s01_b, out = barrier(s01_b, out)

    e10_b, out = barrier(e10_b, out)
    u10_b = put([(e10_b, 0, 2)], [(t10_b, 0, 2)])
    s11_b = send("all_x_1b", u10_b, X_ALL)
    out = tile((u00_b, u10_b), 0, 1, out)
    return tile((s01_b, s11_b), 1, 1, out)


def solution(mesh):
    return jax.shard_map(
        grid_of_eight if mesh.shape["out"] == 8 and mesh.shape["inp"] == 2 else plain,
        mesh=mesh,
        in_specs=(
            P("groups", ("inp", "out")),
            P("inp", "out"),
            P("groups", "out"),
            P("out", "inp"),
        ),
        out_specs=P(("groups", "out"), "inp"),
        check_vma=False,
    )
```

time: 520 us -> 260 us (0.50); the launches traced: 512 us -> 258 us
  blocking collectives: 436 us -> 0 us
  Pallas kernels: 0 us -> 131 us
  starting transfers between devices: 0.01 us -> 62.3 us
  matrix products: 61.7 us -> 0 us
  waiting for transfers between devices: 0.84 us -> 41.3 us
  local copies, waits for them, and re-layouts: 0.51 us -> 22.1 us
  between operations: 13.4 us -> 0.38 us
    psum x2 -> x0, blocking collectives: 436 us -> none  [the longest x1 422 us: on_device(): rot_act = lax.psum(act_full, 'out').astype(jnp.bfloat16)]
    pallas_call x0 -> x29, Pallas kernels: none -> 131 us  [the longest x4 34.5 us: grad_blocks(): pl.pallas_call(functools.partial(grad_sum_kernel, total is not None), gri...]
    ppermute x0 -> x33, starting transfers between devices: none -> 62.3 us  [send(): return lax.ppermute(value, axis, way)]
    dot_general x3 -> x0, matrix products: 61.7 us -> none  [the longest x1 34.8 us: on_device(): jnp.dot(lax.all_gather(grads, 'out', axis=1, tiled=True), basis_out, pref...]
    ppermute x0 -> x33, waiting for transfers between devices: none -> 41.3 us  [send(): return lax.ppermute(value, axis, way)]
    unnamed x4 -> x47, local copies, waits for them, and re-layouts: 0.51 us -> 21.6 us
  transfers between devices with their start and end apart: 1 -> 33, of which waited for: 1 -> 13; matrix products, arithmetic and copies ran while one was open for 2% -> 1% of each run, Pallas kernels for 0% -> 48%
where the time goes in v1:
time: 260 us; the launch traced here: 258 us
  Pallas kernels  131 us (50%)
  starting transfers between devices  62.3 us (24%)
  waiting for transfers between devices  41.3 us (16%)
  local copies, waits for them, and re-layouts  22.1 us (8%)
    ppermute x33, starting transfers between devices, send(): return lax.ppermute(value, axis, way)  62.3 us
    ppermute x33, waiting for transfers between devices, send(): return lax.ppermute(value, axis, way)  41.3 us
    pallas_call x4, Pallas kernels, grad_blocks(): pl.pallas_call(functools.partial(grad_sum_kernel, total is not None), gri...  34.5 us
    pallas_call x3, Pallas kernels, grad_pieces(): pl.pallas_call(functools.partial(grad_kernel, *cuts), grid_spec=pltpu.Pre...  23.9 us
    pallas_call x4, Pallas kernels, tile_part(): pl.pallas_call(functools.partial(tile_kernel, tokens), grid_spec=pltpu.Pr...  22.2 us
    unnamed x47, local copies, waits for them, and re-layouts  21.6 us
    pallas_call x6, Pallas kernels, add_parts(): pl.pallas_call(functools.partial(sum_kernel, cut, count), grid_spec=pltpu...  16.4 us
    pallas_call x7, Pallas kernels, pick(): pl.pallas_call(pick_kernel, grid_spec=pltpu.PrefetchScalarGridSpec(num_sc...  12.6 us
  transfers between devices with their start and end apart: 33, of which 13 were waited for; matrix products, arithmetic and copies ran while one was open for 1% of the time, Pallas kernels for 48%

profile of v1, /device:TPU:0, one launch (start us, length us, event | category | flops | bytes accessed | tf_op | source)
XLA Modules:
  0.0 258.0 jit_solution(3375523996588266271)
XLA Ops:
  0.8 5.8 %collective-permute-start.3 = (bf16[512,1792]{1,0:T(8,128)(2,1)}, bf16[512,1792]{1,0:T(8,128)(2,1)}, u32[]{:S(2)}, u32[]{:S(2)}) collective-permute-start(bf16[512,1792]{1,0:T(8,128)(2,1)} %refs_0_), channel_id=1, source_target_pairs={{0,4},{2,6},{4,0},{6,2},{8,12},{10,14},{12,8},{14,10},{1,5},{3,7},... | collective-permute-start | bytes 5505032 | tf_op jit(solution)/shard_map/near/ppermute | solution.py:55
  9.4 11.5 %act_parts.1 = (f32[512,4096]{1,0:T(8,128)}, bf16[512,4096]{1,0:T(8,128)(2,1)S(1)}) custom-call(s32[8]{0:T(128)S(1)} %stack.95.place_ref, bf16[512,1024]{1,0:T(8,128)(2,1)S(1)} %copy-done.19, bf16[1024,4096]{1,0:T(8,128)(2,1)} %basis_ref.4), custom_call_target="tpu_custom_call" | custom-call | flops 1000 | bytes 1000 | tf_op jit(solution)/shard_map/act_parts/pallas_call | solution.py:73
  20.8 2.1 copy-done
  24.4 6.3 %grad_blocks.4.refs_4_ = f32[512,1792]{1,0:T(8,128)S(1)} custom-call(s32[1]{0:T(128)} %bitcast.9.place_ref, bf16[512,1792]{1,0:T(8,128)(2,1)S(1)} %copy-done.18, bf16[14336,1792]{1,0:T(8,128)(2,1)} %basis_ref.7), custom_call_target="tpu_custom_call" | custom-call | flops 1000 | bytes 1000 | tf_op jit(solution)/shard_map/grad_blocks/pallas_call | solution.py:163
  30.7 1.8 copy-done.6
  32.5 14.1 %collective-permute-done.3.refs_0_.first_ref.refs_1_ = bf16[512,1792]{1,0:T(8,128)(2,1)} collective-permute-done((bf16[512,1792]{1,0:T(8,128)(2,1)}, bf16[512,1792]{1,0:T(8,128)(2,1)}, u32[]{:S(2)}, u32[]{:S(2)}) %collective-permute-start.3) | collective-permute-done | bytes 1835040 | tf_op jit(solution)/shard_map/near/ppermute | solution.py:55
  46.6 1.9 collective-permute-start.4
  48.5 2.2 copy-done.1
  50.7 1.9 pick.7
  53.9 2.1 collective-permute-start.2
  57.5 3.7 %pick.8 = bf16[512,1792]{1,0:T(8,128)(2,1)} custom-call(s32[1]{0:T(128)} %bitcast.2.place_ref, bf16[512,1792]{1,0:T(8,128)(2,1)} %collective-permute-done.3.refs_0_.first_ref.refs_1_, bf16[512,1792]{1,0:T(8,128)(2,1)S(1)} %copy-done.4), custom_call_target="tpu_custom_call" | custom-call | flops 1000 | bytes 1000 | tf_op jit(solution)/shard_map/pick/pallas_call | solution.py:191
  62.8 14.4 %grad_blocks.5.refs_2_ = f32[512,1792]{1,0:T(8,128)S(1)} custom-call(s32[2]{0:T(128)S(1)} %pad_add_fusion.1.place_ref, bf16[512,1792]{1,0:T(8,128)(2,1)} %collective-permute-done.3.refs_0_.first_ref.refs_1_, bf16[512,1792]{1,0:T(8,128)(2,1)} %collective-permute-done.refs_1_.refs_5_.refs_0_, bf16[14336,1792]{1,0:T(8,128)(2,1)} %basis_ref.7, ...), custom_call_target="tpu_custom_call" | custom-call | flops 1000 | bytes 1000 | tf_op jit(solution)/shard_map/grad_blocks/pallas_call | solution.py:163
  77.2 1.9 copy-done.10
  79.1 3.3 %lay.4 = bf16[512,1280]{1,0:T(8,128)(2,1)} custom-call(s32[1]{0:T(128)} %bitcast.2.place_ref, bf16[512,4096]{1,0:T(8,128)(2,1)S(1)} %copy-done.2, bf16[512,1792]{1,0:T(8,128)(2,1)} %collective-permute-done.4.refs_1_.second_ref.refs_2_), custom_call_target="tpu_custom_call" | custom-call | flops 1000 | bytes 1000 | tf_op jit(solution)/shard_map/lay/pallas_call | solution.py:239
  82.4 12.7 %collective-permute-start.5 = (bf16[512,1280]{1,0:T(8,128)(2,1)}, bf16[512,1280]{1,0:T(8,128)(2,1)S(1)}, u32[]{:S(2)}, u32[]{:S(2)}) collective-permute-start(bf16[512,1280]{1,0:T(8,128)(2,1)} %lay.4), channel_id=1, source_target_pairs={{0,4},{2,6},{4,0},{6,2},{8,12},{10,14},{12,8},{14,10},{1,5},{3,7},... | collective-permute-start | bytes 3932168 | tf_op jit(solution)/shard_map/r2_h/ppermute | solution.py:55
  96.0 2.8 %pick.9 = bf16[512,1792]{1,0:T(8,128)(2,1)} custom-call(s32[1]{0:T(128)} %bitcast.2.place_ref, bf16[512,1792]{1,0:T(8,128)(2,1)S(1)} %collective-permute-done.2.first_ref.refs_1_.refs_2_.refs_0_, bf16[512,1792]{1,0:T(8,128)(2,1)} %collective-permute-done.4.refs_1_.second_ref.refs_2_), custom_call_target="tpu_custom_call" | custom-call | flops 1000 | bytes 1000 | tf_op jit(solution)/shard_map/pick/pallas_call | solution.py:191
  100.3 3.7 %add_parts.6 = bf16[512,1024]{1,0:T(8,128)(2,1)} custom-call(s32[1]{0:T(128)} %bitcast.2.place_ref, f32[512,4096]{1,0:T(8,128)} %get-tuple-element.104.refs_0_.refs_2_, bf16[512,1792]{1,0:T(8,128)(2,1)S(1)} %collective-permute-done.2.first_ref.refs_1_.refs_2_.refs_0_, bf16[512,1792]{1,0:T(8,128)(2,1)S(1)} %collective-permute-done.2.first_ref.refs_1_.refs_2_.refs_0_), custom_call_target="tpu_custom_call" | custom-call | flops 1000 | bytes 1000 | tf_op jit(solution)/shard_map/add_parts/pallas_call | solution.py:285
  104.0 1.6 collective-permute-start.7
  105.6 2.7 %lay.5 = bf16[512,1024]{1,0:T(8,128)(2,1)} custom-call(s32[1]{0:T(128)} %bitcast.2.place_ref, bf16[512,4096]{1,0:T(8,128)(2,1)S(1)} %copy-done.2, bf16[512,1792]{1,0:T(8,128)(2,1)} %collective-permute-done.4.refs_1_.second_ref.refs_2_), custom_call_target="tpu_custom_call" | custom-call | flops 1000 | bytes 1000 | tf_op jit(solution)/shard_map/lay/pallas_call | solution.py:239
  108.3 5.0 %collective-permute-start.9 = (bf16[512,1024]{1,0:T(8,128)(2,1)}, bf16[512,1024]{1,0:T(8,128)(2,1)}, u32[]{:S(2)}, u32[]{:S(2)}) collective-permute-start(bf16[512,1024]{1,0:T(8,128)(2,1)} %lay.5), channel_id=1, source_target_pairs={{0,4},{2,6},{4,0},{6,2},{8,12},{10,14},{12,8},{14,10},{1,5},{3,7},... | collective-permute-start | bytes 3145736 | tf_op jit(solution)/shard_map/r2_t/ppermute | solution.py:55
  113.3 2.0 copy-done.11
  115.3 6.9 %grad_blocks.6.refs_2_ = f32[512,1792]{1,0:T(8,128)S(1)} custom-call(s32[1]{0:T(128)} %bitcast.12.place_ref, bf16[512,1792]{1,0:T(8,128)(2,1)} %collective-permute-done.6.refs_0_, bf16[14336,1792]{1,0:T(8,128)(2,1)} %basis_ref.7, f32[512,1792]{1,0:T(8,128)S(1)} %copy-done.11), custom_call_target="tpu_custom_call" | custom-call | flops 1000 | bytes 1000 | tf_op jit(solution)/shard_map/grad_blocks/pallas_call | solution.py:163
  122.3 2.8 %collective-permute-done.5.refs_1_.refs_2_.refs_0_ = bf16[512,1280]{1,0:T(8,128)(2,1)S(1)} collective-permute-done((bf16[512,1280]{1,0:T(8,128)(2,1)}, bf16[512,1280]{1,0:T(8,128)(2,1)S(1)}, u32[]{:S(2)}, u32[]{:S(2)}) %collective-permute-start.5) | collective-permute-done | bytes 1310752 | tf_op jit(solution)/shard_map/r2_h/ppermute | solution.py:55
  125.1 3.6 %add_parts.7 = bf16[512,1024]{1,0:T(8,128)(2,1)} custom-call(s32[1]{0:T(128)} %bitcast.2.place_ref, f32[512,4096]{1,0:T(8,128)} %get-tuple-element.104.refs_0_.refs_2_, bf16[512,1280]{1,0:T(8,128)(2,1)S(1)} %collective-permute-done.5.refs_1_.refs_2_.refs_0_, bf16[512,1280]{1,0:T(8,128)(2,1)S(1)} %collective-permute-done.5.refs_1_.refs_2_.refs_0_), custom_call_target="tpu_custom_call" | custom-call | flops 1000 | bytes 1000 | tf_op jit(solution)/shard_map/add_parts/pallas_call | solution.py:285
  128.7 3.4 %collective-permute-start.13 = (bf16[512,1280]{1,0:T(8,128)(2,1)S(1)}, bf16[512,1280]{1,0:T(8,128)(2,1)}, u32[]{:S(2)}, u32[]{:S(2)}) collective-permute-start(bf16[512,1280]{1,0:T(8,128)(2,1)S(1)} %collective-permute-done.5.refs_1_.refs_2_.refs_0_), channel_id=1, source_target_pairs={{0,2},{2,0},{12,14},{14,12},{1,3},{3,1},{13,15},{15,13},{16,18},{1... | collective-permute-start | bytes 3932168 | tf_op jit(solution)/shard_map/x3_h/ppermute | solution.py:55
  132.1 1.7 collective-permute-start.14
  133.8 2.3 add_parts.8
  139.1 7.5 %grad_pieces.3.refs_2_ = f32[512,1792]{1,0:T(8,128)S(1)} custom-call(s32[2]{0:T(128)S(1)} %pad_add_fusion.2.place_ref, bf16[14336,1792]{1,0:T(8,128)(2,1)} %basis_ref.7, bf16[512,1792]{1,0:T(8,128)(2,1)S(1)} %collective-permute-done.2.first_ref.refs_1_.refs_2_.refs_0_, bf16[512,1792]{1,0:T(8,128)(2,1)S(1)} %copy-done.5, f32[512,1792]{1,0:T(8,128)} %copy-done.12), custom_call_target="tpu_custom_call" | custom-call | flops 1000 | bytes 1000 | tf_op jit(solution)/shard_map/grad_pieces/pallas_call | solution.py:123
  146.6 1.8 copy-done.8
  148.5 2.5 add_parts.9.second_ref
  151.7 6.0 %collective-permute-start.12 = (bf16[512,512]{1,0:T(8,128)(2,1)}, bf16[512,512]{1,0:T(8,128)(2,1)S(1)}, u32[]{:S(2)}, u32[]{:S(2)}) collective-permute-start(bf16[512,512]{1,0:T(8,128)(2,1)} %add_parts.9.second_ref), channel_id=1, source_target_pairs={{0,4},{2,6},{4,0},{6,2},{8,12},{10,14},{12,8},{14,10},{1,5},{3,7},... | collective-permute-start | bytes 1572872 | tf_op jit(solution)/shard_map/all_in_0a/ppermute | solution.py:55
  157.7 1.9 add_parts.10
  160.5 6.9 %grad_blocks.7.refs_3_ = f32[512,1792]{1,0:T(8,128)S(1)} custom-call(s32[1]{0:T(128)} %bitcast.14.place_ref, bf16[512,1792]{1,0:T(8,128)(2,1)} %collective-permute-done.10.refs_0_, bf16[14336,1792]{1,0:T(8,128)(2,1)} %basis_ref.7, f32[512,1792]{1,0:T(8,128)S(1)} %copy-done.9), custom_call_target="tpu_custom_call" | custom-call | flops 1000 | bytes 1000 | tf_op jit(solution)/shard_map/grad_blocks/pallas_call | solution.py:163
  167.4 1.6 collective-permute-done.13.refs_0_
  169.0 2.5 lay.6
  172.9 2.0 collective-permute-start.15
  178.1 2.4 add_parts.11.second_ref
  183.2 1.7 collective-permute-done.15.first_ref.refs_3_
  187.4 8.3 %grad_pieces.4.refs_4_ = f32[512,1792]{1,0:T(8,128)S(1)} custom-call(s32[2]{0:T(128)S(1)} %get-tuple-element.134.place_ref, bf16[14336,1792]{1,0:T(8,128)(2,1)} %basis_ref.7, bf16[512,1280]{1,0:T(8,128)(2,1)S(1)} %collective-permute-done.5.refs_1_.refs_2_.refs_0_, bf16[512,1024]{1,0:T(8,128)(2,1)} %collective-permute-done.9.refs_1_.refs_0_, ...), custom_call_target="tpu_custom_call" | custom-call | flops 1000 | bytes 1000 | tf_op jit(solution)/shard_map/grad_pieces/pallas_call | solution.py:123
  195.8 1.8 copy-done.13
  197.6 9.3 %collective-permute-done.21.first_ref = bf16[512,512]{1,0:T(8,128)(2,1)} collective-permute-done((bf16[512,512]{1,0:T(8,128)(2,1)S(1)}, bf16[512,512]{1,0:T(8,128)(2,1)}, u32[]{:S(2)}, u32[]{:S(2)}) %collective-permute-start.21) | collective-permute-done | bytes 524320 | tf_op jit(solution)/shard_map/all_x_0a/ppermute | solution.py:55
  206.9 8.1 %grad_pieces.5 = f32[512,1792]{1,0:T(8,128)S(1)} custom-call(s32[2]{0:T(128)S(1)} %get-tuple-element.133.place_ref, bf16[14336,1792]{1,0:T(8,128)(2,1)} %basis_ref.7, bf16[512,1280]{1,0:T(8,128)(2,1)} %collective-permute-done.13.refs_0_, bf16[512,768]{1,0:T(8,128)(2,1)} %collective-permute-done.20.refs_1_, ...), custom_call_target="tpu_custom_call" | custom-call | flops 1000 | bytes 1000 | tf_op jit(solution)/shard_map/grad_pieces/pallas_call | solution.py:123
  216.1 2.0 pick.12.first_ref
  226.0 5.2 %tile_part.4.refs_0_ = f32[1792,4096]{1,0:T(8,128)} custom-call(s32[2]{0:T(128)S(1)} %pad_add_fusion.6.place_ref, bf16[512,1792]{1,0:T(8,128)(2,1)S(1)} %add_convert_fusion.grad_ref, bf16[512,512]{1,0:T(8,128)(2,1)S(1)} %pick.10.first_ref, bf16[512,512]{1,0:T(8,128)(2,1)S(1)} %pick.11.second_ref), custom_call_target="tpu_custom_call" | custom-call | flops 1000 | bytes 1000 | tf_op jit(solution)/shard_map/tile_part/pallas_call | solution.py:315
  231.2 6.4 %tile_part.5.refs_0_ = f32[1792,4096]{1,0:T(8,128)} custom-call(s32[2]{0:T(128)S(1)} %pad_add_fusion.5.place_ref, bf16[512,1792]{1,0:T(8,128)(2,1)S(1)} %add_convert_fusion.grad_ref, bf16[512,512]{1,0:T(8,128)(2,1)} %collective-permute-done.21.first_ref, bf16[512,512]{1,0:T(8,128)(2,1)} %collective-permute-done.17.second_ref, ...), custom_call_target="tpu_custom_call", output_to_operand_aliasing={{}: (4, {})} | custom-call | flops 1000 | bytes 1000 | tf_op jit(solution)/shard_map/tile_part/pallas_call | solution.py:315
  240.4 5.3 %tile_part.6.refs_0_ = f32[1792,4096]{1,0:T(8,128)} custom-call(s32[2]{0:T(128)S(1)} %pad_add_fusion.7.place_ref, bf16[512,1792]{1,0:T(8,128)(2,1)S(1)} %add_convert_fusion.grad_ref, bf16[512,512]{1,0:T(8,128)(2,1)S(1)} %pick.12.first_ref, bf16[512,512]{1,0:T(8,128)(2,1)S(1)} %pick.13.second_ref, ...), custom_call_target="tpu_custom_call", output_to_operand_aliasing={{}: (4, {})} | custom-call | flops 1000 | bytes 1000 | tf_op jit(solution)/shard_map/tile_part/pallas_call | solution.py:315
  245.7 7.1 %collective-permute-done.32.second_ref = bf16[512,512]{1,0:T(8,128)(2,1)S(1)} collective-permute-done((bf16[512,512]{1,0:T(8,128)(2,1)S(1)}, bf16[512,512]{1,0:T(8,128)(2,1)S(1)}, u32[]{:S(2)}, u32[]{:S(2)}) %collective-permute-start.32) | collective-permute-done | bytes 524320 | tf_op jit(solution)/shard_map/all_x_1b/ppermute | solution.py:55
  252.7 5.3 %tile_part.7 = f32[1792,4096]{1,0:T(8,128)} custom-call(s32[2]{0:T(128)S(1)} %pad_add_fusion.place_ref, bf16[512,1792]{1,0:T(8,128)(2,1)S(1)} %add_convert_fusion.grad_ref, bf16[512,512]{1,0:T(8,128)(2,1)S(1)} %collective-permute-done.30.first_ref, bf16[512,512]{1,0:T(8,128)(2,1)S(1)} %collective-permute-done.32.second_ref, ...), custom_call_target="tpu_custom_call", output_to_operand_aliasing={{}: (4, {})} | custom-call | flops 1000 | bytes 1000 | tf_op jit(solution)/shard_map/tile_part/pallas_call | solution.py:315
  (105 shorter events, 37.7 us)
Async XLA Ops:
  0.0 32.5 %collective-permute-start.1 = (bf16[512,1792]{1,0:T(8,128)(2,1)}, bf16[512,1792]{1,0:T(8,128)(2,1)S(1)}, u32[]{:S(2)}, u32[]{:S(2)}) collective-permute-start(bf16[512,1792]{1,0:T(8,128)(2,1)} %refs_0_), channel_id=1, source_target_pairs={{4,8},{6,10},{8,4},{10,6},{5,9},{7,11},{9,5},{11,7},{20,24},{22,26... | collective-permute-start | bytes 5505032 | tf_op jit(solution)/shard_map/mid_own/ppermute | solution.py:55
  0.8 45.8 %collective-permute-start.3 = (bf16[512,1792]{1,0:T(8,128)(2,1)}, bf16[512,1792]{1,0:T(8,128)(2,1)}, u32[]{:S(2)}, u32[]{:S(2)}) collective-permute-start(bf16[512,1792]{1,0:T(8,128)(2,1)} %refs_0_), channel_id=1, source_target_pairs={{0,4},{2,6},{4,0},{6,2},{8,12},{10,14},{12,8},{14,10},{1,5},{3,7},... | collective-permute-start | bytes 5505032 | tf_op jit(solution)/shard_map/near/ppermute | solution.py:55
  6.6 56.3 %collective-permute-start = (bf16[512,1792]{1,0:T(8,128)(2,1)}, bf16[512,1792]{1,0:T(8,128)(2,1)}, u32[]{:S(2)}, u32[]{:S(2)}) collective-permute-start(bf16[512,1792]{1,0:T(8,128)(2,1)} %refs_0_), channel_id=1, source_target_pairs={{0,2},{2,0},{4,6},{6,4},{8,10},{10,8},{12,14},{14,12},{1,3},{3,1},... | collective-permute-start | bytes 5505032 | tf_op jit(solution)/shard_map/own_x/ppermute | solution.py:55
  20.8 2.1 copy-start
  22.9 1.5 copy-start.18
  30.7 1.8 copy-start.6
  46.6 32.5 %collective-permute-start.4 = (bf16[512,1792]{1,0:T(8,128)(2,1)}, bf16[512,1792]{1,0:T(8,128)(2,1)}, u32[]{:S(2)}, u32[]{:S(2)}) collective-permute-start(bf16[512,1792]{1,0:T(8,128)(2,1)} %collective-permute-done.3.refs_0_.first_ref.refs_1_), channel_id=1, source_target_pairs={{4,8},{6,10},{8,4},{10,6},{5,9},{7,11},{9,5},{11,7},{20,24},{22,26... | collective-permute-start | bytes 5505032 | tf_op jit(solution)/shard_map/mid_near/ppermute | solution.py:55
  48.5 2.2 copy-start.1
  53.9 42.1 %collective-permute-start.2 = (bf16[512,1792]{1,0:T(8,128)(2,1)}, bf16[512,1792]{1,0:T(8,128)(2,1)S(1)}, u32[]{:S(2)}, u32[]{:S(2)}) collective-permute-start(bf16[512,1792]{1,0:T(8,128)(2,1)} %pick.7), channel_id=1, source_target_pairs={{0,4},{2,6},{4,0},{6,2},{8,12},{10,14},{12,8},{14,10},{1,5},{3,7},... | collective-permute-start | bytes 5505032 | tf_op jit(solution)/shard_map/r1/ppermute | solution.py:55
  61.3 52.1 %collective-permute-start.6 = (bf16[512,1792]{1,0:T(8,128)(2,1)}, bf16[512,1792]{1,0:T(8,128)(2,1)}, u32[]{:S(2)}, u32[]{:S(2)}) collective-permute-start(bf16[512,1792]{1,0:T(8,128)(2,1)} %pick.8), channel_id=1, source_target_pairs={{0,2},{2,0},{4,6},{6,4},{8,10},{10,8},{12,14},{14,12},{1,3},{3,1},... | collective-permute-start | bytes 5505032 | tf_op jit(solution)/shard_map/x1/ppermute | solution.py:55
  62.8 16.3 %copy-start.2 = (bf16[512,4096]{1,0:T(8,128)(2,1)S(1)}, bf16[512,4096]{1,0:T(8,128)(2,1)}, u32[]{:S(2)}) copy-start(bf16[512,4096]{1,0:T(8,128)(2,1)} %copy-done) | copy-start | bytes 12582916
  77.2 1.9 copy-start.10
  82.4 42.6 %collective-permute-start.5 = (bf16[512,1280]{1,0:T(8,128)(2,1)}, bf16[512,1280]{1,0:T(8,128)(2,1)S(1)}, u32[]{:S(2)}, u32[]{:S(2)}) collective-permute-start(bf16[512,1280]{1,0:T(8,128)(2,1)} %lay.4), channel_id=1, source_target_pairs={{0,4},{2,6},{4,0},{6,2},{8,12},{10,14},{12,8},{14,10},{1,5},{3,7},... | collective-permute-start | bytes 3932168 | tf_op jit(solution)/shard_map/r2_h/ppermute | solution.py:55
  98.8 49.6 %collective-permute-start.10 = (bf16[512,1792]{1,0:T(8,128)(2,1)}, bf16[512,1792]{1,0:T(8,128)(2,1)}, u32[]{:S(2)}, u32[]{:S(2)}) collective-permute-start(bf16[512,1792]{1,0:T(8,128)(2,1)} %pick.9), channel_id=1, source_target_pairs={{0,2},{2,0},{4,6},{6,4},{8,10},{10,8},{12,14},{14,12},{1,3},{3,1},... | collective-permute-start | bytes 5505032 | tf_op jit(solution)/shard_map/x2/ppermute | solution.py:55
  104.0 29.8 %collective-permute-start.7 = (bf16[512,1024]{1,0:T(8,128)(2,1)}, bf16[512,1024]{1,0:T(8,128)(2,1)}, u32[]{:S(2)}, u32[]{:S(2)}) collective-permute-start(bf16[512,1024]{1,0:T(8,128)(2,1)} %add_parts.6), channel_id=1, source_target_pairs={{4,8},{6,10},{8,4},{10,6},{5,9},{7,11},{9,5},{11,7},{20,24},{22,26... | collective-permute-start | bytes 3145736 | tf_op jit(solution)/shard_map/mid_a/ppermute | solution.py:55
  108.3 40.2 %collective-permute-start.9 = (bf16[512,1024]{1,0:T(8,128)(2,1)}, bf16[512,1024]{1,0:T(8,128)(2,1)}, u32[]{:S(2)}, u32[]{:S(2)}) collective-permute-start(bf16[512,1024]{1,0:T(8,128)(2,1)} %lay.5), channel_id=1, source_target_pairs={{0,4},{2,6},{4,0},{6,2},{8,12},{10,14},{12,8},{14,10},{1,5},{3,7},... | collective-permute-start | bytes 3145736 | tf_op jit(solution)/shard_map/r2_t/ppermute | solution.py:55
  113.3 2.0 copy-start.11
  122.3 6.4 %copy-start.12 = (f32[512,1792]{1,0:T(8,128)}, f32[512,1792]{1,0:T(8,128)S(1)}, u32[]{:S(2)}) copy-start(f32[512,1792]{1,0:T(8,128)S(1)} %grad_blocks.6.refs_2_) | copy-start | bytes 11010052
  128.7 40.4 %collective-permute-start.13 = (bf16[512,1280]{1,0:T(8,128)(2,1)S(1)}, bf16[512,1280]{1,0:T(8,128)(2,1)}, u32[]{:S(2)}, u32[]{:S(2)}) collective-permute-start(bf16[512,1280]{1,0:T(8,128)(2,1)S(1)} %collective-permute-done.5.refs_1_.refs_2_.refs_0_), channel_id=1, source_target_pairs={{0,2},{2,0},{12,14},{14,12},{1,3},{3,1},{13,15},{15,13},{16,18},{1... | collective-permute-start | bytes 3932168 | tf_op jit(solution)/shard_map/x3_h/ppermute | solution.py:55
  132.1 25.6 %collective-permute-start.14 = (bf16[512,1024]{1,0:T(8,128)(2,1)}, bf16[512,1024]{1,0:T(8,128)(2,1)}, u32[]{:S(2)}, u32[]{:S(2)}) collective-permute-start(bf16[512,1024]{1,0:T(8,128)(2,1)} %add_parts.7), channel_id=1, source_target_pairs={{4,8},{6,10},{8,4},{10,6},{5,9},{7,11},{9,5},{11,7},{20,24},{22,26... | collective-permute-start | bytes 3145736 | tf_op jit(solution)/shard_map/mid_b/ppermute | solution.py:55
  136.1 12.4 %collective-permute-start.8 = (bf16[512,512]{1,0:T(8,128)(2,1)}, bf16[512,512]{1,0:T(8,128)(2,1)}, u32[]{:S(2)}, u32[]{:S(2)}) collective-permute-start(bf16[512,512]{1,0:T(8,128)(2,1)} %add_parts.8), channel_id=1, source_target_pairs={{4,6},{6,4},{8,10},{10,8},{5,7},{7,5},{9,11},{11,9},{20,22},{22,20... | collective-permute-start | bytes 1572872 | tf_op jit(solution)/shard_map/sum_x_a/ppermute | solution.py:55
  146.6 1.9 copy-start.8
  151.0 20.6 %collective-permute-start.11 = (bf16[512,512]{1,0:T(8,128)(2,1)}, bf16[512,512]{1,0:T(8,128)(2,1)S(1)}, u32[]{:S(2)}, u32[]{:S(2)}) collective-permute-start(bf16[512,512]{1,0:T(8,128)(2,1)} %add_parts.9.second_ref), channel_id=1, source_target_pairs={{4,8},{6,10},{8,4},{10,6},{5,9},{7,11},{9,5},{11,7},{20,24},{22,26... | collective-permute-start | bytes 1572872 | tf_op jit(solution)/shard_map/all_mid_a/ppermute | solution.py:55
  151.7 19.9 %collective-permute-start.12 = (bf16[512,512]{1,0:T(8,128)(2,1)}, bf16[512,512]{1,0:T(8,128)(2,1)S(1)}, u32[]{:S(2)}, u32[]{:S(2)}) collective-permute-start(bf16[512,512]{1,0:T(8,128)(2,1)} %add_parts.9.second_ref), channel_id=1, source_target_pairs={{0,4},{2,6},{4,0},{6,2},{8,12},{10,14},{12,8},{14,10},{1,5},{3,7},... | collective-permute-start | bytes 1572872 | tf_op jit(solution)/shard_map/all_in_0a/ppermute | solution.py:55
  157.7 2.8 %copy-start.9 = (f32[512,1792]{1,0:T(8,128)S(1)}, f32[512,1792]{1,0:T(8,128)}, u32[]{:S(2)}) copy-start(f32[512,1792]{1,0:T(8,128)} %copy-done.8) | copy-start | bytes 11010052
  159.6 18.5 %collective-permute-start.16 = (bf16[512,512]{1,0:T(8,128)(2,1)S(1)}, bf16[512,512]{1,0:T(8,128)(2,1)S(1)}, u32[]{:S(2)}, u32[]{:S(2)}) collective-permute-start(bf16[512,512]{1,0:T(8,128)(2,1)S(1)} %add_parts.10), channel_id=1, source_target_pairs={{4,6},{6,4},{8,10},{10,8},{5,7},{7,5},{9,11},{11,9},{20,22},{22,20... | collective-permute-start | bytes 1572872 | tf_op jit(solution)/shard_map/sum_x_b/ppermute | solution.py:55
  167.4 9.1 %copy-start.7 = (f32[512,1792]{1,0:T(8,128)}, f32[512,1792]{1,0:T(8,128)S(1)}, u32[]{:S(2)}) copy-start(f32[512,1792]{1,0:T(8,128)S(1)} %grad_blocks.7.refs_3_) | copy-start | bytes 11010052
  171.6 3.3 %copy-start.16 = (bf16[512,512]{1,0:T(8,128)(2,1)}, bf16[512,512]{1,0:T(8,128)(2,1)S(1)}, u32[]{:S(2)}) copy-start(bf16[512,512]{1,0:T(8,128)(2,1)S(1)} %collective-permute-done.11.refs_1_.second_ref) | copy-start | bytes 1572868
  172.9 12.0 %collective-permute-start.15 = (bf16[512,512]{1,0:T(8,128)(2,1)S(1)}, bf16[512,512]{1,0:T(8,128)(2,1)S(1)}, u32[]{:S(2)}, u32[]{:S(2)}) collective-permute-start(bf16[512,512]{1,0:T(8,128)(2,1)S(1)} %lay.7), channel_id=1, source_target_pairs={{0,4},{2,6},{4,0},{6,2},{8,12},{10,14},{12,8},{14,10},{1,5},{3,7},... | collective-permute-start | bytes 1572872 | tf_op jit(solution)/shard_map/all_in_1a/ppermute | solution.py:55
  174.9 22.7 %collective-permute-start.20 = (bf16[512,768]{1,0:T(8,128)(2,1)}, bf16[512,768]{1,0:T(8,128)(2,1)}, u32[]{:S(2)}, u32[]{:S(2)}) collective-permute-start(bf16[512,768]{1,0:T(8,128)(2,1)} %lay.6), channel_id=1, source_target_pairs={{0,2},{2,0},{4,6},{6,4},{8,10},{10,8},{12,14},{14,12},{1,3},{3,1},... | collective-permute-start | bytes 2359304 | tf_op jit(solution)/shard_map/x3_t/ppermute | solution.py:55
  176.5 8.4 %copy-start.17 = (bf16[512,512]{1,0:T(8,128)(2,1)S(1)}, bf16[512,512]{1,0:T(8,128)(2,1)}, u32[]{:S(2)}) copy-start(bf16[512,512]{1,0:T(8,128)(2,1)} %copy-done.16) | copy-start | bytes 1572868
  176.5 30.4 %collective-permute-start.21 = (bf16[512,512]{1,0:T(8,128)(2,1)S(1)}, bf16[512,512]{1,0:T(8,128)(2,1)}, u32[]{:S(2)}, u32[]{:S(2)}) collective-permute-start(bf16[512,512]{1,0:T(8,128)(2,1)S(1)} %pick.10.first_ref), channel_id=1, source_target_pairs={{0,2},{2,0},{4,6},{6,4},{8,10},{10,8},{12,14},{14,12},{1,3},{3,1},... | collective-permute-start | bytes 1572872 | tf_op jit(solution)/shard_map/all_x_0a/ppermute | solution.py:55
  180.5 34.6 %collective-permute-start.18 = (bf16[512,512]{1,0:T(8,128)(2,1)}, bf16[512,512]{1,0:T(8,128)(2,1)}, u32[]{:S(2)}, u32[]{:S(2)}) collective-permute-start(bf16[512,512]{1,0:T(8,128)(2,1)} %add_parts.11.second_ref), channel_id=1, source_target_pairs={{4,8},{6,10},{8,4},{10,6},{5,9},{7,11},{9,5},{11,7},{20,24},{22,26... | collective-permute-start | bytes 1572872 | tf_op jit(solution)/shard_map/all_mid_b/ppermute | solution.py:55
  181.9 33.1 %collective-permute-start.19 = (bf16[512,512]{1,0:T(8,128)(2,1)}, bf16[512,512]{1,0:T(8,128)(2,1)}, u32[]{:S(2)}, u32[]{:S(2)}) collective-permute-start(bf16[512,512]{1,0:T(8,128)(2,1)} %add_parts.11.second_ref), channel_id=1, source_target_pairs={{4,0},{6,2},{8,12},{10,14},{5,1},{7,3},{9,13},{11,15},{20,16},{22,... | collective-permute-start | bytes 1572872 | tf_op jit(solution)/shard_map/all_in_0b/ppermute | solution.py:55
  185.9 29.2 %collective-permute-start.17 = (bf16[512,512]{1,0:T(8,128)(2,1)S(1)}, bf16[512,512]{1,0:T(8,128)(2,1)}, u32[]{:S(2)}, u32[]{:S(2)}) collective-permute-start(bf16[512,512]{1,0:T(8,128)(2,1)S(1)} %pick.11.second_ref), channel_id=1, source_target_pairs={{0,2},{2,0},{4,6},{6,4},{8,10},{10,8},{12,14},{14,12},{1,3},{3,1},... | collective-permute-start | bytes 1572872 | tf_op jit(solution)/shard_map/all_x_1a/ppermute | solution.py:55
  187.4 19.5 %copy-start.15 = (bf16[512,512]{1,0:T(8,128)(2,1)S(1)}, bf16[512,512]{1,0:T(8,128)(2,1)}, u32[]{:S(2)}) copy-start(bf16[512,512]{1,0:T(8,128)(2,1)} %copy-done.14) | copy-start | bytes 1572868
  195.8 1.8 copy-start.13
  215.4 4.8 %collective-permute-start.22 = (f32[64,1792]{1,0:T(8,128)S(1)}, f32[64,1792]{1,0:T(8,128)S(1)}, u32[]{:S(2)}, u32[]{:S(2)}) collective-permute-start(f32[64,1792]{1,0:T(8,128)S(1)} %get-tuple-element.132), channel_id=1, source_target_pairs={{0,1},{1,0},{2,3},{3,2},{4,5},{5,4},{6,7},{7,6},{8,9},{9,8},{10,11... | collective-permute-start | bytes 1376264 | tf_op jit(solution)/shard_map/core/ppermute | solution.py:55
  215.5 5.3 %collective-permute-start.23 = (f32[64,1792]{1,0:T(8,128)S(1)}, f32[64,1792]{1,0:T(8,128)S(1)}, u32[]{:S(2)}, u32[]{:S(2)}) collective-permute-start(f32[64,1792]{1,0:T(8,128)S(1)} %get-tuple-element.131), channel_id=1, source_target_pairs={{0,1},{1,0},{2,3},{3,2},{4,5},{5,4},{6,7},{7,6},{8,9},{9,8},{10,11... | collective-permute-start | bytes 1376264 | tf_op jit(solution)/shard_map/core/ppermute | solution.py:55
  218.1 19.6 %collective-permute-start.30 = (bf16[512,512]{1,0:T(8,128)(2,1)S(1)}, bf16[512,512]{1,0:T(8,128)(2,1)S(1)}, u32[]{:S(2)}, u32[]{:S(2)}) collective-permute-start(bf16[512,512]{1,0:T(8,128)(2,1)S(1)} %pick.12.first_ref), channel_id=1, source_target_pairs={{0,2},{2,0},{4,6},{6,4},{8,10},{10,8},{12,14},{14,12},{1,3},{3,1},... | collective-permute-start | bytes 1572872 | tf_op jit(solution)/shard_map/all_x_0b/ppermute | solution.py:55
  218.7 19.0 %collective-permute-start.31 = (bf16[512,512]{1,0:T(8,128)(2,1)}, bf16[512,512]{1,0:T(8,128)(2,1)S(1)}, u32[]{:S(2)}, u32[]{:S(2)}) collective-permute-start(bf16[512,512]{1,0:T(8,128)(2,1)} %collective-permute-done.18.second_ref), channel_id=1, source_target_pairs={{4,0},{6,2},{8,12},{10,14},{5,1},{7,3},{9,13},{11,15},{20,16},{22,... | collective-permute-start | bytes 1572872 | tf_op jit(solution)/shard_map/all_in_1b/ppermute | solution.py:55
  220.2 1.9 collective-permute-start.24
  220.3 2.4 collective-permute-start.25
  220.8 2.6 collective-permute-start.26
  222.1 2.0 collective-permute-start.27
  222.8 2.0 collective-permute-start.28
  223.4 2.0 collective-permute-start.29
  238.7 14.0 %collective-permute-start.32 = (bf16[512,512]{1,0:T(8,128)(2,1)S(1)}, bf16[512,512]{1,0:T(8,128)(2,1)S(1)}, u32[]{:S(2)}, u32[]{:S(2)}) collective-permute-start(bf16[512,512]{1,0:T(8,128)(2,1)S(1)} %pick.13.second_ref), channel_id=1, source_target_pairs={{0,2},{2,0},{4,6},{6,4},{8,10},{10,8},{12,14},{14,12},{1,3},{3,1},... | collective-permute-start | bytes 1572872 | tf_op jit(solution)/shard_map/all_x_1b/ppermute | solution.py:55
  (5 other events, 6.3 us)

commit v2 on v0

v2 whole, which is shorter than its diff:
```python
import functools

import jax
import jax.numpy as jnp
from jax import lax
from jax.experimental import pallas as pl
from jax.experimental.pallas import tpu as pltpu
from jax.sharding import PartitionSpec as P

F32, BF16 = jnp.float32, jnp.bfloat16
TN = (((0,), (0,)), ((), ()))
VMEM = 44 * 1024 * 1024
CHEAP = pl.CostEstimate(flops=1000, bytes_accessed=1000, transcendentals=0)


def plain(grads, basis_out, acts, basis_in):
    partial_grad = jnp.dot(
        lax.all_gather(grads, "out", axis=1, tiled=True),
        basis_out,
        preferred_element_type=F32,
    )
    rot_grad = lax.psum(partial_grad, "inp").astype(BF16)
    contract = (((0,), (1,)), ((), ()))
    act_full = lax.dot_general(basis_in, acts, contract, preferred_element_type=F32)
    rot_act = lax.psum(act_full, "out").astype(BF16)
    tile = lax.dot_general(rot_grad, rot_act, contract, preferred_element_type=F32)
    return tile * tile / F32(rot_grad.shape[0])


def pairs(fn):
    out = []
    for z in range(4):
        for x in range(2):
            to = fn(z, x)
            if to is not None:
                out.append((z * 2 + x, to[0] * 2 + to[1]))
    return out


def is_end(z):
    return z in (0, 3)


X_ALL = pairs(lambda z, x: (z, 1 - x))
X_END = pairs(lambda z, x: (z, 1 - x) if is_end(z) else None)
X_MID = pairs(lambda z, x: None if is_end(z) else (z, 1 - x))
Z_NEAR = pairs(lambda z, x: (z ^ 1, x))
Z_MID = pairs(lambda z, x: None if is_end(z) else (3 - z, x))
X_END_Z_MID = pairs(lambda z, x: (z, 1 - x) if is_end(z) else (3 - z, x))
Z_IN = pairs(lambda z, x: None if is_end(z) else (z ^ 1, x))


def send(name, value, way, axis="out"):
    with jax.named_scope(name):
        return lax.ppermute(value, axis, way)


def after(value, *events):
    return lax.optimization_barrier((value, *events))[0]


def pinned(*arrays):
    return [pltpu.with_memory_space_constraint(array, pltpu.HBM) for array in arrays]


def act_kernel(spans, place_ref, acts_ref, basis_ref, wide_ref, *narrow_refs):
    part = jnp.dot(acts_ref[...], basis_ref[...], preferred_element_type=F32)
    wide_ref[...] = part
    narrow = part.astype(BF16)
    for j, pieces in enumerate(spans):

        @pl.when(pl.program_id(0) == j)
        def _(pieces=pieces):
            for n, into, first, width in pieces:
                narrow_refs[n][:, into : into + width] = narrow[:, first : first + width]


def act_parts(columns, sent, unit, acts, basis_in):
    tokens, depth = acts.shape
    width = basis_in.shape[1]
    step = 2 * unit
    spans = [[] for _ in columns]
    for n, units in enumerate(sent):
        for at, u in enumerate(units):
            spans[u // 2].append((n, at * unit, (u % 2) * unit, unit))
    return pl.pallas_call(
        functools.partial(act_kernel, spans),
        grid_spec=pltpu.PrefetchScalarGridSpec(
            num_scalar_prefetch=1,
            grid=(len(columns),),
            in_specs=[
                pl.BlockSpec((tokens, depth), lambda j, p: (0, 0)),
                pl.BlockSpec((depth, step), lambda j, p: (0, p[j])),
            ],
            out_specs=[pl.BlockSpec((tokens, step), lambda j, p: (0, j))]
            + [pl.BlockSpec((tokens, len(units) * unit), lambda j, p: (0, 0)) for units in sent],
        ),
        out_shape=[pltpu.HBM((tokens, width), F32)] + [pltpu.HBM((tokens, len(units) * unit), BF16) for units in sent],
        compiler_params=pltpu.CompilerParams(vmem_limit_bytes=VMEM),
        cost_estimate=CHEAP,
        name="act_parts",
    )(jnp.stack(columns).astype(jnp.int32), *pinned(acts, basis_in))


def grad_kernel(end_cuts, mid_cuts, outs, place_ref, basis_ref, *refs):
    refs, total_ref, out_refs = refs[: -outs - 1], refs[-outs - 1], refs[-outs:]

    def add(cuts):
        acc = total_ref[...]
        row = 0
        for n, first, width in cuts:
            piece = refs[n][:, first : first + width]
            acc = acc + jnp.dot(piece, basis_ref[row : row + width], preferred_element_type=F32)
            row += width
        if outs == 1:
            out_refs[0][...] = acc
            return
        for n, out_ref in enumerate(out_refs):

            @pl.when(pl.program_id(0) == n)
            def _(out_ref=out_ref):
                out_ref[...] = acc

    pl.when(place_ref[0] == 1)(lambda: add(end_cuts))
    pl.when(place_ref[0] == 0)(lambda: add(mid_cuts))


def grad_pieces(end, at_end, at_mid, place, basis_out, total, halves=False):
    arrays = []
    cuts = []
    for sources in (at_end, at_mid):
        cuts.append([])
        for array, first, width in sources:
            known = [n for n, other in enumerate(arrays) if other is array]
            if not known:
                arrays.append(array)
            cuts[-1].append((known[0] if known else len(arrays) - 1, first, width))
    depth = sum(width for _, _, width in cuts[0])
    tokens, width = total.shape
    step = width // 2
    out_spec = pl.BlockSpec((tokens, step), lambda j, s: (0, j))
    half_spec = pl.BlockSpec((tokens, step), lambda j, s: (0, 0))
    return pl.pallas_call(
        functools.partial(grad_kernel, *cuts, 2 if halves else 1),
        grid_spec=pltpu.PrefetchScalarGridSpec(
            num_scalar_prefetch=1,
            grid=(2,),
            in_specs=[pl.BlockSpec((depth, step), lambda j, s: (s[1], j))]
            + [pl.BlockSpec(array.shape, lambda j, s: (0, 0)) for array in arrays]
            + [out_spec],
            out_specs=[half_spec] * 2 if halves else out_spec,
        ),
        out_shape=[pltpu.HBM((tokens, step), F32)] * 2 if halves else pltpu.HBM((tokens, width), F32),
        compiler_params=pltpu.CompilerParams(vmem_limit_bytes=VMEM),
        cost_estimate=CHEAP,
        name="grad_pieces",
    )(jnp.stack([end.astype(jnp.int32), place.astype(jnp.int32)]), *pinned(basis_out), *arrays, *pinned(total))


def grad_sum_kernel(has_total, place_ref, *refs):
    out_ref, refs = refs[-1], refs[:-1]
    acc = None
    if has_total:
        acc, refs = refs[-1][...], refs[:-1]
    count = len(refs) // 2
    for block, basis in zip(refs[:count], refs[count:]):
        part = jnp.dot(block[...], basis[...], preferred_element_type=F32)
        acc = part if acc is None else acc + part
    out_ref[...] = acc


def grad_blocks(pieces, places, basis_out, total):
    tokens, depth = pieces[0].shape
    width = basis_out.shape[1]
    step = width // 2 if len(pieces) == 1 else 256
    whole = pl.BlockSpec((tokens, depth), lambda j, s: (0, 0))
    out_spec = pl.BlockSpec((tokens, step), lambda j, s: (0, j))

    def rows_of(n):
        return pl.BlockSpec((depth, step), lambda j, s: (s[n], j))

    totals = [] if total is None else [total]
    return pl.pallas_call(
        functools.partial(grad_sum_kernel, total is not None),
        grid_spec=pltpu.PrefetchScalarGridSpec(
            num_scalar_prefetch=1,
            grid=(width // step,),
            in_specs=[whole] * len(pieces) + [rows_of(n) for n in range(len(pieces))] + [out_spec] * len(totals),
            out_specs=out_spec,
        ),
        out_shape=pltpu.HBM((tokens, width), F32),
        compiler_params=pltpu.CompilerParams(vmem_limit_bytes=VMEM),
        cost_estimate=CHEAP,
        name="grad_blocks",
    )(jnp.stack(places).astype(jnp.int32), *pinned(*pieces, *[basis_out] * len(pieces), *totals))


def make_kernel(plans, place_ref, *refs):
    out_ref = refs[-1]

    def write(layers):
        at = 0
        for columns in layers:
            total = None
            for n, first, width in columns:
                block = refs[n][:, first : first + width]
                if len(columns) > 1:
                    block = block.astype(F32)
                total = block if total is None else total + block
            out_ref[:, at : at + columns[0][2]] = total.astype(out_ref.dtype)
            at += columns[0][2]

    for flag, layers in plans:
        if layers is not None:
            pl.when(place_ref[0] == flag)(lambda layers=layers: write(layers))


def make(end, at_end, at_mid, units, unit):
    arrays, specs, keys, plans = [], [], [], []
    small = units <= 2
    rows = (at_mid or at_end)[0][0][0].shape[0]
    steps = 1 if small else 2
    rows //= steps
    for flag, ranges in ((1, at_end), (0, at_mid)):
        if ranges is None:
            plans.append((flag, None))
            continue
        plan = []
        for sources in ranges:
            columns = []
            for array, first, count in sources:
                aligned = first % count == 0
                width = count * unit if aligned else array.shape[1]
                column = first // count if aligned else 0
                key = (id(array), width, column, flag)
                if key not in keys:
                    keys.append(key)
                    arrays.append(array)
                    specs.append(
                        pl.BlockSpec(
                            (rows, width),
                            lambda i, p, flag=flag, column=column: (i * (p[0] if flag else 1 - p[0]), column),
                        )
                    )
                columns.append((keys.index(key), 0 if aligned else first * unit, count * unit))
            plan.append(columns)
        plans.append((flag, plan))
    return pl.pallas_call(
        functools.partial(make_kernel, plans),
        grid_spec=pltpu.PrefetchScalarGridSpec(
            num_scalar_prefetch=1,
            grid=(steps,),
            in_specs=specs,
            out_specs=pl.BlockSpec((rows, units * unit), lambda i, p: (i, 0)),
        ),
        out_shape=(jax.ShapeDtypeStruct if small else pltpu.HBM)((steps * rows, units * unit), BF16),
        compiler_params=pltpu.CompilerParams(vmem_limit_bytes=VMEM),
        cost_estimate=CHEAP,
        name="make",
    )(end.astype(jnp.int32).reshape(1), *[a if a.shape[1] <= 2 * unit else pinned(a)[0] for a in arrays])


def tile_kernel(tokens, count, place_ref, low_ref, high_ref, *refs):
    out_ref = refs[-1]
    rows = low_ref.shape[1]
    for n in range(count):

        @pl.when(pl.program_id(0) == n)
        def _(n=n):
            for at, grad_ref in ((0, low_ref), (rows, high_ref)):
                tile = lax.dot_general(grad_ref[...], refs[n][...], TN, preferred_element_type=F32)
                out_ref[at : at + rows] = tile * tile / F32(tokens)


def tile_part(rot_grad, acts, columns, out, shape):
    tokens, rows = rot_grad[0].shape
    count = len(acts)
    width = acts[0].shape[1]
    outs = [] if out is None else [out]
    return pl.pallas_call(
        functools.partial(tile_kernel, tokens, count),
        grid_spec=pltpu.PrefetchScalarGridSpec(
            num_scalar_prefetch=1,
            grid=(count,),
            in_specs=[pl.BlockSpec((tokens, rows), lambda j, p: (0, 0))] * 2
            + [pl.BlockSpec((tokens, width), lambda j, p: (0, 0))] * count
            + [pl.BlockSpec(memory_space=pl.ANY)] * len(outs),
            out_specs=pl.BlockSpec((2 * rows, width), lambda j, p: (0, p[j])),
        ),
        out_shape=jax.ShapeDtypeStruct(shape, F32),
        input_output_aliases={3 + count: 0} if outs else {},
        compiler_params=pltpu.CompilerParams(vmem_limit_bytes=VMEM),
        cost_estimate=CHEAP,
        name="tile_part",
    )(jnp.stack(columns).astype(jnp.int32), *rot_grad, *acts, *outs)


def barrier(*values):
    return lax.optimization_barrier(values)


def grid_of_eight(grads, basis_out, acts, basis_in):
    o = lax.axis_index("out")
    z, x = o // 2, o % 2
    side = z // 2
    end = (z == 0) | (z == 3)
    near, far, farthest = z ^ 1, 2 - side, 3 - 3 * side
    eighth = basis_in.shape[1] // 8
    half = grads.shape[1] // 2

    def either(at_end, at_mid):
        return jnp.where(end, at_end, at_mid)

    def z_block(zb, xb):
        return zb * 2 + xb

    def column(ds, dx, h):
        return ((side ^ ds) * 2 + (x ^ dx)) * 2 + h

    unit = eighth // 2

    def blocks(pieces, places, total):
        return grad_blocks(pieces, places, basis_out, total)

    def block_of(at_end, at_mid, place, total, halves=False):
        at_end = [(array, first * unit, units * unit) for array, first, units in at_end]
        at_mid = [(array, first * unit, units * unit) for array, first, units in at_mid]
        return grad_pieces(end, at_end, at_mid, place, basis_out, total, halves)

    def put(at_end, at_mid, units):
        return make(end, at_end, at_mid, units, unit)

    def one(array, first, units):
        return [[(array, first, units)]]

    a = send("near", grads, Z_NEAR)
    x0 = send("own_x", grads, X_ALL)
    b1 = send("mid_own", grads, Z_MID)
    order = [(1, 1, 0), (1, 0, 0), (0, 1, 0), (0, 0, 0), (1, 1, 1), (1, 0, 1), (0, 1, 1), (0, 0, 1)]
    sent = [0, 1, 2, 3, 4, 5, 6], [8, 9, 10, 11, 7], [12, 13, 14, 15]
    wide, n1, n2, n3 = act_parts([column(*e) for e in order], sent, unit, acts, basis_in)
    total = blocks([after(grads, wide)], [z_block(z, x)], None)

    a, total = barrier(a, total)
    c1 = send("near_on", a, X_END_Z_MID)
    b1, total = barrier(b1, total)
    y1 = put(one(n1, 0, 7), one(b1, 0, 7), 7)
    r1 = send("r1", y1, Z_NEAR)
    xb1 = send("mid_own_x", after(b1, y1), X_MID)
    total = blocks([a, x0], [z_block(near, x), z_block(z, 1 - x)], total)

    b2, total = barrier(c1, total)
    y2 = put(one(n2, 0, 5), one(b2, 0, 5), 5)
    r2_h = send("r2_h", y2, Z_NEAR)
    r1, y2, total = barrier(r1, y2, total)
    y3 = put(one(r1, 0, 7), one(b2, 0, 7), 7)
    x2 = send("x2", y3, X_ALL)
    y4 = put(None, [[(after(wide, y3), 0, 4), (r1, 0, 4)]], 4)
    m_a = send("mid_a", y4, Z_MID)
    y5 = put(one(after(n3, y4), 0, 4), one(b2, 5, 2), 4)
    r2_t = send("r2_t", y5, Z_NEAR)
    xb1, total = barrier(xb1, total)
    total = block_of([(b2, 0, 7)], [(xb1, 0, 7)], z_block(either(near, far), 1 - x), after(total, y5))
    total = block_of([(r1, 0, 7)], [(b1, 0, 7)], z_block(far, x), total)

    r2_h, total = barrier(r2_h, total)
    y6 = put(None, [[(wide, 8, 4), (r2_h, 0, 4)]], 4)
    m_b = send("mid_b", y6, Z_MID)
    x3_h = send("x3_h", after(r2_h, y6), X_END)
    m_a, y6, total = barrier(m_a, y6, total)
    y7 = put(None, [[(wide, 4, 2), (r1, 4, 2), (m_a, 0, 2)]], 2)
    xm_a = send("sum_x_a", y7, X_MID)
    x2, total = barrier(x2, after(total, y7))
    total = blocks([x2], [z_block(either(far, farthest), 1 - x)], total)

    r2_t, total = barrier(r2_t, total)
    xm_a, total = barrier(xm_a, total)
    sums = [
        [(r1, 6, 1), (wide, 6, 1), (m_a, 2, 1), (xm_a, 0, 1)],
        [(r2_h, 4, 1), (wide, 7, 1), (m_a, 3, 1), (xm_a, 1, 1)],
    ]
    t00_a = put(one(x0, 2, 2), sums, 2)
    t10_a = send("all_mid_a", t00_a, Z_MID)
    e00_a = send("all_in_0a", t00_a, Z_NEAR)
    m_b, t00_a = barrier(m_b, t00_a)
    y9 = put(None, [[(after(wide, t00_a), 12, 2), (r2_t, 0, 2), (m_b, 0, 2)]], 2)
    xm_b = send("sum_x_b", y9, X_MID)
    y8 = put(one(after(r2_t, y9), 0, 2), [[(a, 0, 2)], [(a, 6, 1)]], 3)

    t10_a, e00_a, y8 = barrier(t10_a, e00_a, y8)
    y10 = put(one(x0, 4, 2), one(t10_a, 0, 2), 2)
    e10_a = send("all_in_1a", y10, Z_NEAR)
    x3_h, y10 = barrier(x3_h, y10)
    x3_t = send("x3_t", after(y8, y10), X_ALL)
    xm_b, y10 = barrier(xm_b, y10)
    sums = [[(after(wide, y10), 14, 2), (r2_t, 2, 2), (m_b, 2, 2), (xm_b, 0, 2)]]
    t00_b = put(None, sums, 2)
    t10_b = send("all_mid_b", t00_b, Z_MID)
    e00_b = send("all_in_0b", t00_b, Z_IN)
    u00_a = put(one(after(e00_a, t00_b), 0, 2), one(t00_a, 0, 2), 2)
    s01_a = send("all_x_0a", u00_a, X_ALL)

    e10_a, u00_a = barrier(e10_a, u00_a)
    u10_a = put(one(e10_a, 0, 2), one(after(t10_a, u00_a), 0, 2), 2)
    s11_a = send("all_x_1a", u10_a, X_ALL)
    total = block_of([(r2_h, 0, 5), (r2_t, 0, 2)], [(b2, 0, 7)], z_block(farthest, x), after(total, u10_a))
    x3_t, total = barrier(x3_t, total)

    t10_b, e00_b, total = barrier(t10_b, e00_b, total)
    e10_b = send("all_in_1b", t10_b, Z_IN)
    u00_b = put(one(e00_b, 0, 2), one(t00_b, 0, 2), 2)
    s01_b = send("all_x_0b", u00_b, X_ALL)
    s01_a, total = barrier(s01_a, after(total, u00_b))
    at_end = [(x3_h, 0, 5), (x3_t, 0, 2)]
    at_mid = [(x3_t, 0, 2), (e00_a, 0, 2), (e10_a, 0, 2), (x3_t, 2, 1)]
    low, high = block_of(at_end, at_mid, z_block(either(farthest, near), 1 - x), total, halves=True)

    s11_a, e10_b, low, high = barrier(s11_a, e10_b, low, high)
    low_other = send("core_low", low, [(0, 1), (1, 0)], "inp")
    high_other = send("core_high", high, [(0, 1), (1, 0)], "inp")
    u10_b = put(one(e10_b, 0, 2), one(t10_b, 0, 2), 2)
    s11_b = send("all_x_1b", u10_b, X_ALL)
    rot_grad = [
        (mine + theirs).astype(BF16) for mine, theirs in ((after(low, u10_b), low_other), (after(high, u10_b), high_other))
    ]
    shape = (basis_out.shape[1], basis_in.shape[1])
    places = [column(0, 0, 0), column(1, 0, 0), column(0, 1, 0), column(1, 1, 0)]
    out = tile_part(rot_grad, [u00_a, u10_a, s01_a, s11_a], places, None, shape)
    s01_b, out = barrier(s01_b, out)
    out = tile_part(rot_grad, [u00_b, u10_b, s01_b], [column(0, 0, 1), column(1, 0, 1), column(0, 1, 1)], out, shape)
    return tile_part(rot_grad, [s11_b], [column(1, 1, 1)], out, shape)


def solution(mesh):
    return jax.shard_map(
        grid_of_eight if mesh.shape["out"] == 8 and mesh.shape["inp"] == 2 else plain,
        mesh=mesh,
        in_specs=(
            P("groups", ("inp", "out")),
            P("inp", "out"),
            P("groups", "out"),
            P("out", "inp"),
        ),
        out_specs=P(("groups", "out"), "inp"),
        check_vma=False,
    )
```

time: 520 us -> 237 us (0.46); the launches traced: 512 us -> 235 us
  blocking collectives: 436 us -> 0 us
  Pallas kernels: 0 us -> 133 us
  matrix products: 61.7 us -> 0 us
  waiting for transfers between devices: 0.84 us -> 49.5 us
  starting transfers between devices: 0.01 us -> 44 us
  between operations: 13.4 us -> 0.24 us
  local copies, waits for them, and re-layouts: 0.51 us -> 6.19 us
    psum x2 -> x0, blocking collectives: 436 us -> none  [the longest x1 422 us: on_device(): rot_act = lax.psum(act_full, 'out').astype(jnp.bfloat16)]
    pallas_call x0 -> x27, Pallas kernels: none -> 133 us  [the longest x4 37.7 us: grad_pieces(): pl.pallas_call(functools.partial(grad_kernel, *cuts, 2 if halves else 1),...]
    dot_general x3 -> x0, matrix products: 61.7 us -> none  [the longest x1 34.8 us: on_device(): jnp.dot(lax.all_gather(grads, 'out', axis=1, tiled=True), basis_out, pref...]
    ppermute x0 -> x27, waiting for transfers between devices: none -> 49.5 us  [send(): return lax.ppermute(value, axis, way)]
    ppermute x0 -> x27, starting transfers between devices: none -> 44 us  [send(): return lax.ppermute(value, axis, way)]
    unnamed x4 -> x24, local copies, waits for them, and re-layouts: 0.51 us -> 6.11 us
  transfers between devices with their start and end apart: 1 -> 27, of which waited for: 1 -> 8; matrix products, arithmetic and copies ran while one was open for 2% -> 1% of each run, Pallas kernels for 0% -> 55%
where the time goes in v2:
time: 237 us; the launch traced here: 235 us
  Pallas kernels  133 us (56%)
  waiting for transfers between devices  49.5 us (21%)
  starting transfers between devices  44 us (19%)
  local copies, waits for them, and re-layouts  6.19 us (3%)
  other arithmetic  2.51 us (1%)
    ppermute x27, waiting for transfers between devices, send(): return lax.ppermute(value, axis, way)  49.5 us
    ppermute x27, starting transfers between devices, send(): return lax.ppermute(value, axis, way)  44 us
    pallas_call x4, Pallas kernels, grad_pieces(): pl.pallas_call(functools.partial(grad_kernel, *cuts, 2 if halves else 1),...  37.7 us
    pallas_call x16, Pallas kernels, make(): pl.pallas_call(functools.partial(make_kernel, plans), grid_spec=pltpu.Pre...  31.8 us
    pallas_call x3, Pallas kernels, grad_blocks(): pl.pallas_call(functools.partial(grad_sum_kernel, total is not None), gri...  30.9 us
    pallas_call x3, Pallas kernels, tile_part(): pl.pallas_call(functools.partial(tile_kernel, tokens, count), grid_spec=p...  18.6 us
    pallas_call x1, Pallas kernels, act_parts(): pl.pallas_call(functools.partial(act_kernel, spans), grid_spec=pltpu.Pref...  13.6 us
    unnamed x24, local copies, waits for them, and re-layouts  6.11 us
  transfers between devices with their start and end apart: 27, of which 8 were waited for; matrix products, arithmetic and copies ran while one was open for 1% of the time, Pallas kernels for 55%

profile of v2, /device:TPU:0, one launch (start us, length us, event | category | flops | bytes accessed | tf_op | source)
XLA Modules:
  0.0 235.2 jit_solution(26410716666024262)
XLA Ops:
  0.0 3.0 %collective-permute-start.2 = (bf16[512,1792]{1,0:T(8,128)(2,1)}, bf16[512,1792]{1,0:T(8,128)(2,1)}, u32[]{:S(2)}, u32[]{:S(2)}) collective-permute-start(bf16[512,1792]{1,0:T(8,128)(2,1)} %refs_0_), channel_id=1, source_target_pairs={{0,4},{2,6},{4,0},{6,2},{8,12},{10,14},{12,8},{14,10},{1,5},{3,7},... | collective-permute-start | bytes 5505032 | tf_op jit(solution)/shard_map/near/ppermute | solution.py:55
  3.0 1.9 collective-permute-start.1
  4.9 1.5 collective-permute-start
  6.5 13.6 %act_parts.1 = (f32[512,4096]{1,0:T(8,128)}, bf16[512,1792]{1,0:T(8,128)(2,1)}, bf16[512,1280]{1,0:T(8,128)(2,1)}, bf16[512,1024]{1,0:T(8,128)(2,1)}) custom-call(s32[8]{0:T(128)S(1)} %stack.92.place_ref, bf16[512,1024]{1,0:T(8,128)(2,1)} %acts_ref.1, bf16[1024,4096]{1,0:T(8,128)(2,1)} %basis_ref.5), custom_call_target="tpu_custom_call" | custom-call | flops 1000 | bytes 1000 | tf_op jit(solution)/shard_map/act_parts/pallas_call | solution.py:86
  20.1 7.9 %grad_blocks.3.refs_4_ = f32[512,1792]{1,0:T(8,128)} custom-call(s32[1]{0:T(128)} %bitcast.9.place_ref, bf16[512,1792]{1,0:T(8,128)(2,1)} %refs_0_, bf16[14336,1792]{1,0:T(8,128)(2,1)} %basis_ref.9), custom_call_target="tpu_custom_call" | custom-call | flops 1000 | bytes 1000 | tf_op jit(solution)/shard_map/grad_blocks/pallas_call | solution.py:183
  28.0 15.3 %collective-permute-done.2.refs_0_.refs_1_.refs_2_ = bf16[512,1792]{1,0:T(8,128)(2,1)} collective-permute-done((bf16[512,1792]{1,0:T(8,128)(2,1)}, bf16[512,1792]{1,0:T(8,128)(2,1)}, u32[]{:S(2)}, u32[]{:S(2)}) %collective-permute-start.2) | collective-permute-done | bytes 1835040 | tf_op jit(solution)/shard_map/near/ppermute | solution.py:55
  43.3 1.7 collective-permute-start.4
  45.0 2.7 %make.16 = bf16[512,1792]{1,0:T(8,128)(2,1)} custom-call(s32[1]{0:T(128)} %bitcast.1.place_ref, bf16[512,1792]{1,0:T(8,128)(2,1)} %get-tuple-element.70.refs_0_, bf16[512,1792]{1,0:T(8,128)(2,1)} %collective-permute-done.1.refs_1_), custom_call_target="tpu_custom_call" | custom-call | flops 1000 | bytes 1000 | tf_op jit(solution)/shard_map/make/pallas_call | solution.py:248
  47.7 4.2 %collective-permute-start.3 = (bf16[512,1792]{1,0:T(8,128)(2,1)}, bf16[512,1792]{1,0:T(8,128)(2,1)}, u32[]{:S(2)}, u32[]{:S(2)}) collective-permute-start(bf16[512,1792]{1,0:T(8,128)(2,1)} %make.16), channel_id=1, source_target_pairs={{0,4},{2,6},{4,0},{6,2},{8,12},{10,14},{12,8},{14,10},{1,5},{3,7},... | collective-permute-start | bytes 5505032 | tf_op jit(solution)/shard_map/r1/ppermute | solution.py:55
  51.9 1.9 collective-permute-start.7
  53.9 14.6 %grad_blocks.4.refs_2_ = f32[512,1792]{1,0:T(8,128)} custom-call(s32[2]{0:T(128)S(1)} %pad_add_fusion.place_ref, bf16[512,1792]{1,0:T(8,128)(2,1)} %collective-permute-done.2.refs_0_.refs_1_.refs_2_, bf16[512,1792]{1,0:T(8,128)(2,1)} %collective-permute-done.refs_1_.refs_0_, bf16[14336,1792]{1,0:T(8,128)(2,1)} %basis_ref.9, bf16[14336,1792]{1,0:T(8,128)(2,1)} %basis_ref.9, ...), custom_call_target="tpu_custom_call" | custom-call | flops 1000 | bytes 1000 | tf_op jit(solution)/shard_map/grad_blocks/pallas_call | solution.py:183
  68.5 17.4 %collective-permute-done.4.refs_1_.refs_0_.refs_2_ = bf16[512,1792]{1,0:T(8,128)(2,1)S(1)} collective-permute-done((bf16[512,1792]{1,0:T(8,128)(2,1)}, bf16[512,1792]{1,0:T(8,128)(2,1)S(1)}, u32[]{:S(2)}, u32[]{:S(2)}) %collective-permute-start.4) | collective-permute-done | bytes 1835040 | tf_op jit(solution)/shard_map/near_on/ppermute | solution.py:55
  87.3 2.4 %make.17 = bf16[512,1280]{1,0:T(8,128)(2,1)} custom-call(s32[1]{0:T(128)} %bitcast.1.place_ref, bf16[512,1280]{1,0:T(8,128)(2,1)} %get-tuple-element.75.refs_0_, bf16[512,1792]{1,0:T(8,128)(2,1)} %copy-done), custom_call_target="tpu_custom_call" | custom-call | flops 1000 | bytes 1000 | tf_op jit(solution)/shard_map/make/pallas_call | solution.py:248
  91.1 2.7 %make.18 = bf16[512,1792]{1,0:T(8,128)(2,1)} custom-call(s32[1]{0:T(128)} %bitcast.1.place_ref, bf16[512,1792]{1,0:T(8,128)(2,1)} %collective-permute-done.3.refs_0_.refs_1_, bf16[512,1792]{1,0:T(8,128)(2,1)} %copy-done), custom_call_target="tpu_custom_call" | custom-call | flops 1000 | bytes 1000 | tf_op jit(solution)/shard_map/make/pallas_call | solution.py:248
  93.8 1.5 collective-permute-start.10
  95.3 2.4 %make.19 = bf16[512,1024]{1,0:T(8,128)(2,1)} custom-call(s32[1]{0:T(128)} %bitcast.1.place_ref, f32[512,4096]{1,0:T(8,128)} %get-tuple-element.100.refs_0_.refs_2_.refs_6_, bf16[512,1792]{1,0:T(8,128)(2,1)} %collective-permute-done.3.refs_0_.refs_1_), custom_call_target="tpu_custom_call" | custom-call | flops 1000 | bytes 1000 | tf_op jit(solution)/shard_map/make/pallas_call | solution.py:248
  97.7 1.7 collective-permute-start.5
  99.3 2.5 %make.20 = bf16[512,1024]{1,0:T(8,128)(2,1)} custom-call(s32[1]{0:T(128)} %bitcast.1.place_ref, bf16[512,1024]{1,0:T(8,128)(2,1)} %get-tuple-element.87.refs_0_, bf16[512,1792]{1,0:T(8,128)(2,1)} %copy-done), custom_call_target="tpu_custom_call" | custom-call | flops 1000 | bytes 1000 | tf_op jit(solution)/shard_map/make/pallas_call | solution.py:248
  101.8 3.1 %collective-permute-start.9 = (bf16[512,1024]{1,0:T(8,128)(2,1)}, bf16[512,1024]{1,0:T(8,128)(2,1)S(1)}, u32[]{:S(2)}, u32[]{:S(2)}) collective-permute-start(bf16[512,1024]{1,0:T(8,128)(2,1)} %make.20), channel_id=1, source_target_pairs={{0,4},{2,6},{4,0},{6,2},{8,12},{10,14},{12,8},{14,10},{1,5},{3,7},... | collective-permute-start | bytes 3145736 | tf_op jit(solution)/shard_map/r2_t/ppermute | solution.py:55
  105.1 9.1 %grad_pieces.4.refs_2_ = f32[512,1792]{1,0:T(8,128)} custom-call(s32[2]{0:T(128)S(1)} %pad_add_fusion.2.place_ref, bf16[14336,1792]{1,0:T(8,128)(2,1)} %basis_ref.9, bf16[512,1792]{1,0:T(8,128)(2,1)S(1)} %copy-done.1, bf16[512,1792]{1,0:T(8,128)(2,1)} %collective-permute-done.7.refs_1_, f32[512,1792]{1,0:T(8,128)} %grad_blocks.4.refs_2_), custom_call_target="tpu_custom_call" | custom-call | flops 1000 | bytes 1000 | tf_op jit(solution)/shard_map/grad_pieces/pallas_call | solution.py:143
  114.2 9.7 %grad_pieces.5.refs_2_ = f32[512,1792]{1,0:T(8,128)} custom-call(s32[2]{0:T(128)S(1)} %pad_add_fusion.1.place_ref, bf16[14336,1792]{1,0:T(8,128)(2,1)} %basis_ref.9, bf16[512,1792]{1,0:T(8,128)(2,1)} %collective-permute-done.3.refs_0_.refs_1_, bf16[512,1792]{1,0:T(8,128)(2,1)} %collective-permute-done.1.refs_1_, f32[512,1792]{1,0:T(8,128)} %grad_pieces.4.refs_2_), custom_call_target="tpu_custom_call" | custom-call | flops 1000 | bytes 1000 | tf_op jit(solution)/shard_map/grad_pieces/pallas_call | solution.py:143
  123.8 2.4 %make.21 = bf16[512,1024]{1,0:T(8,128)(2,1)} custom-call(s32[1]{0:T(128)} %bitcast.1.place_ref, f32[512,4096]{1,0:T(8,128)} %get-tuple-element.100.refs_0_.refs_2_.refs_6_, bf16[512,1280]{1,0:T(8,128)(2,1)} %collective-permute-done.6.refs_1_.refs_5_.refs_0_), custom_call_target="tpu_custom_call" | custom-call | flops 1000 | bytes 1000 | tf_op jit(solution)/shard_map/make/pallas_call | solution.py:248
  126.2 1.6 collective-permute-start.13
  127.8 2.4 %collective-permute-start.16 = (bf16[512,1280]{1,0:T(8,128)(2,1)}, bf16[512,1280]{1,0:T(8,128)(2,1)}, u32[]{:S(2)}, u32[]{:S(2)}) collective-permute-start(bf16[512,1280]{1,0:T(8,128)(2,1)} %collective-permute-done.6.refs_1_.refs_5_.refs_0_), channel_id=1, source_target_pairs={{0,2},{2,0},{12,14},{14,12},{1,3},{3,1},{13,15},{15,13},{16,18},{1... | collective-permute-start | bytes 3932168 | tf_op jit(solution)/shard_map/x3_h/ppermute | solution.py:55
  130.2 2.3 make.22
  133.4 3.6 %collective-permute-done.10.refs_0_ = bf16[512,1792]{1,0:T(8,128)(2,1)} collective-permute-done((bf16[512,1792]{1,0:T(8,128)(2,1)}, bf16[512,1792]{1,0:T(8,128)(2,1)}, u32[]{:S(2)}, u32[]{:S(2)}) %collective-permute-start.10) | collective-permute-done | bytes 1835040 | tf_op jit(solution)/shard_map/x2/ppermute | solution.py:55
  137.1 8.5 %grad_blocks.5.refs_3_ = f32[512,1792]{1,0:T(8,128)} custom-call(s32[1]{0:T(128)} %bitcast.14.place_ref, bf16[512,1792]{1,0:T(8,128)(2,1)} %collective-permute-done.10.refs_0_, bf16[14336,1792]{1,0:T(8,128)(2,1)} %basis_ref.9, f32[512,1792]{1,0:T(8,128)} %grad_pieces.5.refs_2_), custom_call_target="tpu_custom_call" | custom-call | flops 1000 | bytes 1000 | tf_op jit(solution)/shard_map/grad_blocks/pallas_call | solution.py:183
  145.6 2.1 make.23.refs_1_
  148.4 3.6 %collective-permute-start.12 = (bf16[512,512]{1,0:T(8,128)(2,1)S(1)}, bf16[512,512]{1,0:T(8,128)(2,1)S(1)}, u32[]{:S(2)}, u32[]{:S(2)}) collective-permute-start(bf16[512,512]{1,0:T(8,128)(2,1)S(1)} %make.23.refs_1_), channel_id=1, source_target_pairs={{0,4},{2,6},{4,0},{6,2},{8,12},{10,14},{12,8},{14,10},{1,5},{3,7},... | collective-permute-start | bytes 1572872 | tf_op jit(solution)/shard_map/all_in_0a/ppermute | solution.py:55
  152.0 1.5 make.24
  154.2 2.0 make.25
  156.3 4.3 %collective-permute-done.12.refs_0_.refs_2_ = bf16[512,512]{1,0:T(8,128)(2,1)S(1)} collective-permute-done((bf16[512,512]{1,0:T(8,128)(2,1)S(1)}, bf16[512,512]{1,0:T(8,128)(2,1)S(1)}, u32[]{:S(2)}, u32[]{:S(2)}) %collective-permute-start.12) | collective-permute-done | bytes 524320 | tf_op jit(solution)/shard_map/all_in_0a/ppermute | solution.py:55
  161.3 1.9 make.26
  164.1 1.8 collective-permute-start.20
  165.9 1.7 collective-permute-start.14
  167.7 2.3 make.27.refs_1_
  170.0 1.6 collective-permute-start.18
  175.8 4.6 %collective-permute-done.14.refs_0_.refs_3_ = bf16[512,512]{1,0:T(8,128)(2,1)} collective-permute-done((bf16[512,512]{1,0:T(8,128)(2,1)}, bf16[512,512]{1,0:T(8,128)(2,1)}, u32[]{:S(2)}, u32[]{:S(2)}) %collective-permute-start.14) | collective-permute-done | bytes 524320 | tf_op jit(solution)/shard_map/all_in_1a/ppermute | solution.py:55
  181.5 1.9 make.29.refs_1_
  184.5 8.8 %grad_pieces.6.refs_4_ = f32[512,1792]{1,0:T(8,128)} custom-call(s32[2]{0:T(128)S(1)} %pad_add_fusion.3.place_ref, bf16[14336,1792]{1,0:T(8,128)(2,1)} %basis_ref.9, bf16[512,1280]{1,0:T(8,128)(2,1)} %collective-permute-done.6.refs_1_.refs_5_.refs_0_, bf16[512,1024]{1,0:T(8,128)(2,1)S(1)} %copy-done.3, bf16[512,1792]{1,0:T(8,128)(2,1)S(1)} %copy-done.1, ...), custom_call_target="tpu_custom_call" | custom-call | flops 1000 | bytes 1000 | tf_op jit(solution)/shard_map/grad_pieces/pallas_call | solution.py:143
  193.3 1.4 collective-permute-start.21
  196.1 10.1 %grad_pieces.7 = (f32[512,896]{1,0:T(8,128)}, f32[512,896]{1,0:T(8,128)}) custom-call(s32[2]{0:T(128)S(1)} %pad_add_fusion.4.place_ref, bf16[14336,1792]{1,0:T(8,128)(2,1)} %basis_ref.9, bf16[512,1280]{1,0:T(8,128)(2,1)} %collective-permute-done.16.refs_0_, bf16[512,768]{1,0:T(8,128)(2,1)} %collective-permute-done.20.refs_1_, ...), custom_call_target="tpu_custom_call" | custom-call | flops 1000 | bytes 1000 | tf_op jit(solution)/shard_map/grad_pieces/pallas_call | solution.py:143
  207.0 1.7 collective-permute-start.26
  210.4 1.8 add_convert_fusion.high_ref
  213.2 9.1 %tile_part.3.refs_3_ = f32[1792,4096]{1,0:T(8,128)} custom-call(s32[4]{0:T(128)S(1)} %pad_add_fusion.6.place_ref, bf16[512,896]{1,0:T(8,128)(2,1)S(1)} %add_convert_fusion.1.low_ref, bf16[512,896]{1,0:T(8,128)(2,1)S(1)} %add_convert_fusion.high_ref, bf16[512,512]{1,0:T(8,128)(2,1)S(1)} %make.28.refs_0_, bf16[512,512]{1,0:T(8,128)(2,1)} %make.29.refs_1_, ...), custom_call_target="tpu_custom_call" | custom-call | flops 1000 | bytes 1000 | tf_op jit(solution)/shard_map/tile_part/pallas_call | solution.py:280
  222.3 6.6 %tile_part.4.refs_1_ = f32[1792,4096]{1,0:T(8,128)} custom-call(s32[3]{0:T(128)S(1)} %pad_add_fusion.5.place_ref, bf16[512,896]{1,0:T(8,128)(2,1)S(1)} %add_convert_fusion.1.low_ref, bf16[512,896]{1,0:T(8,128)(2,1)S(1)} %add_convert_fusion.high_ref, bf16[512,512]{1,0:T(8,128)(2,1)S(1)} %make.30.refs_0_, ...), custom_call_target="tpu_custom_call", output_to_operand_aliasing={{}: (6, {})} | custom-call | flops 1000 | bytes 1000 | tf_op jit(solution)/shard_map/tile_part/pallas_call | solution.py:280
  228.8 3.3 %collective-permute-done.25.refs_0_ = bf16[512,512]{1,0:T(8,128)(2,1)S(1)} collective-permute-done((bf16[512,512]{1,0:T(8,128)(2,1)S(1)}, bf16[512,512]{1,0:T(8,128)(2,1)S(1)}, u32[]{:S(2)}, u32[]{:S(2)}) %collective-permute-start.25) | collective-permute-done | bytes 524320 | tf_op jit(solution)/shard_map/all_x_1b/ppermute | solution.py:55
  232.2 3.0 %tile_part.5 = f32[1792,4096]{1,0:T(8,128)} custom-call(s32[1]{0:T(128)} %bitcast.place_ref, bf16[512,896]{1,0:T(8,128)(2,1)S(1)} %add_convert_fusion.1.low_ref, bf16[512,896]{1,0:T(8,128)(2,1)S(1)} %add_convert_fusion.high_ref, bf16[512,512]{1,0:T(8,128)(2,1)S(1)} %collective-permute-done.25.refs_0_, ...), custom_call_target="tpu_custom_call", output_to_operand_aliasing={{}: (4, {})} | custom-call | flops 1000 | bytes 1000 | tf_op jit(solution)/shard_map/tile_part/pallas_call | solution.py:280
  (67 shorter events, 18.0 us)
Async XLA Ops:
  0.0 43.3 %collective-permute-start.2 = (bf16[512,1792]{1,0:T(8,128)(2,1)}, bf16[512,1792]{1,0:T(8,128)(2,1)}, u32[]{:S(2)}, u32[]{:S(2)}) collective-permute-start(bf16[512,1792]{1,0:T(8,128)(2,1)} %refs_0_), channel_id=1, source_target_pairs={{0,4},{2,6},{4,0},{6,2},{8,12},{10,14},{12,8},{14,10},{1,5},{3,7},... | collective-permute-start | bytes 5505032 | tf_op jit(solution)/shard_map/near/ppermute | solution.py:55
  3.0 42.0 %collective-permute-start.1 = (bf16[512,1792]{1,0:T(8,128)(2,1)}, bf16[512,1792]{1,0:T(8,128)(2,1)}, u32[]{:S(2)}, u32[]{:S(2)}) collective-permute-start(bf16[512,1792]{1,0:T(8,128)(2,1)} %refs_0_), channel_id=1, source_target_pairs={{4,8},{6,10},{8,4},{10,6},{5,9},{7,11},{9,5},{11,7},{20,24},{22,26... | collective-permute-start | bytes 5505032 | tf_op jit(solution)/shard_map/mid_own/ppermute | solution.py:55
  4.9 49.0 %collective-permute-start = (bf16[512,1792]{1,0:T(8,128)(2,1)}, bf16[512,1792]{1,0:T(8,128)(2,1)}, u32[]{:S(2)}, u32[]{:S(2)}) collective-permute-start(bf16[512,1792]{1,0:T(8,128)(2,1)} %refs_0_), channel_id=1, source_target_pairs={{0,2},{2,0},{4,6},{6,4},{8,10},{10,8},{12,14},{14,12},{1,3},{3,1},... | collective-permute-start | bytes 5505032 | tf_op jit(solution)/shard_map/own_x/ppermute | solution.py:55
  43.3 42.6 %collective-permute-start.4 = (bf16[512,1792]{1,0:T(8,128)(2,1)}, bf16[512,1792]{1,0:T(8,128)(2,1)S(1)}, u32[]{:S(2)}, u32[]{:S(2)}) collective-permute-start(bf16[512,1792]{1,0:T(8,128)(2,1)} %collective-permute-done.2.refs_0_.refs_1_.refs_2_), channel_id=1, source_target_pairs={{0,2},{2,0},{4,8},{6,10},{8,4},{10,6},{12,14},{14,12},{1,3},{3,1},... | collective-permute-start | bytes 5505032 | tf_op jit(solution)/shard_map/near_on/ppermute | solution.py:55
  47.7 43.3 %collective-permute-start.3 = (bf16[512,1792]{1,0:T(8,128)(2,1)}, bf16[512,1792]{1,0:T(8,128)(2,1)}, u32[]{:S(2)}, u32[]{:S(2)}) collective-permute-start(bf16[512,1792]{1,0:T(8,128)(2,1)} %make.16), channel_id=1, source_target_pairs={{0,4},{2,6},{4,0},{6,2},{8,12},{10,14},{12,8},{14,10},{1,5},{3,7},... | collective-permute-start | bytes 5505032 | tf_op jit(solution)/shard_map/r1/ppermute | solution.py:55
  51.9 53.1 %collective-permute-start.7 = (bf16[512,1792]{1,0:T(8,128)(2,1)}, bf16[512,1792]{1,0:T(8,128)(2,1)}, u32[]{:S(2)}, u32[]{:S(2)}) collective-permute-start(bf16[512,1792]{1,0:T(8,128)(2,1)} %collective-permute-done.1.refs_1_), channel_id=1, source_target_pairs={{4,6},{6,4},{8,10},{10,8},{5,7},{7,5},{9,11},{11,9},{20,22},{22,20... | collective-permute-start | bytes 5505032 | tf_op jit(solution)/shard_map/mid_own_x/ppermute | solution.py:55
  85.9 1.3 copy-start
  89.7 34.1 %collective-permute-start.6 = (bf16[512,1280]{1,0:T(8,128)(2,1)}, bf16[512,1280]{1,0:T(8,128)(2,1)}, u32[]{:S(2)}, u32[]{:S(2)}) collective-permute-start(bf16[512,1280]{1,0:T(8,128)(2,1)} %make.17), channel_id=1, source_target_pairs={{0,4},{2,6},{4,0},{6,2},{8,12},{10,14},{12,8},{14,10},{1,5},{3,7},... | collective-permute-start | bytes 3932168 | tf_op jit(solution)/shard_map/r2_h/ppermute | solution.py:55
  93.8 43.3 %collective-permute-start.10 = (bf16[512,1792]{1,0:T(8,128)(2,1)}, bf16[512,1792]{1,0:T(8,128)(2,1)}, u32[]{:S(2)}, u32[]{:S(2)}) collective-permute-start(bf16[512,1792]{1,0:T(8,128)(2,1)} %make.18), channel_id=1, source_target_pairs={{0,2},{2,0},{4,6},{6,4},{8,10},{10,8},{12,14},{14,12},{1,3},{3,1},... | collective-permute-start | bytes 5505032 | tf_op jit(solution)/shard_map/x2/ppermute | solution.py:55
  97.7 32.6 %collective-permute-start.5 = (bf16[512,1024]{1,0:T(8,128)(2,1)}, bf16[512,1024]{1,0:T(8,128)(2,1)}, u32[]{:S(2)}, u32[]{:S(2)}) collective-permute-start(bf16[512,1024]{1,0:T(8,128)(2,1)} %make.19), channel_id=1, source_target_pairs={{4,8},{6,10},{8,4},{10,6},{5,9},{7,11},{9,5},{11,7},{20,24},{22,26... | collective-permute-start | bytes 3145736 | tf_op jit(solution)/shard_map/mid_a/ppermute | solution.py:55
  99.3 5.8 %copy-start.1 = (bf16[512,1792]{1,0:T(8,128)(2,1)S(1)}, bf16[512,1792]{1,0:T(8,128)(2,1)}, u32[]{:S(2)}) copy-start(bf16[512,1792]{1,0:T(8,128)(2,1)} %copy-done) | copy-start | bytes 5505028
  101.8 43.8 %collective-permute-start.9 = (bf16[512,1024]{1,0:T(8,128)(2,1)}, bf16[512,1024]{1,0:T(8,128)(2,1)S(1)}, u32[]{:S(2)}, u32[]{:S(2)}) collective-permute-start(bf16[512,1024]{1,0:T(8,128)(2,1)} %make.20), channel_id=1, source_target_pairs={{0,4},{2,6},{4,0},{6,2},{8,12},{10,14},{12,8},{14,10},{1,5},{3,7},... | collective-permute-start | bytes 3145736 | tf_op jit(solution)/shard_map/r2_t/ppermute | solution.py:55
  126.2 25.8 %collective-permute-start.13 = (bf16[512,1024]{1,0:T(8,128)(2,1)}, bf16[512,1024]{1,0:T(8,128)(2,1)}, u32[]{:S(2)}, u32[]{:S(2)}) collective-permute-start(bf16[512,1024]{1,0:T(8,128)(2,1)} %make.21), channel_id=1, source_target_pairs={{4,8},{6,10},{8,4},{10,6},{5,9},{7,11},{9,5},{11,7},{20,24},{22,26... | collective-permute-start | bytes 3145736 | tf_op jit(solution)/shard_map/mid_b/ppermute | solution.py:55
  127.8 36.3 %collective-permute-start.16 = (bf16[512,1280]{1,0:T(8,128)(2,1)}, bf16[512,1280]{1,0:T(8,128)(2,1)}, u32[]{:S(2)}, u32[]{:S(2)}) collective-permute-start(bf16[512,1280]{1,0:T(8,128)(2,1)} %collective-permute-done.6.refs_1_.refs_5_.refs_0_), channel_id=1, source_target_pairs={{0,2},{2,0},{12,14},{14,12},{1,3},{3,1},{13,15},{15,13},{16,18},{1... | collective-permute-start | bytes 3932168 | tf_op jit(solution)/shard_map/x3_h/ppermute | solution.py:55
  132.5 13.0 %collective-permute-start.8 = (bf16[512,512]{1,0:T(8,128)(2,1)}, bf16[512,512]{1,0:T(8,128)(2,1)S(1)}, u32[]{:S(2)}, u32[]{:S(2)}) collective-permute-start(bf16[512,512]{1,0:T(8,128)(2,1)} %make.22), channel_id=1, source_target_pairs={{4,6},{6,4},{8,10},{10,8},{5,7},{7,5},{9,11},{11,9},{20,22},{22,20... | collective-permute-start | bytes 1572872 | tf_op jit(solution)/shard_map/sum_x_a/ppermute | solution.py:55
  145.6 2.1 copy-start.2
  147.7 5.8 %copy-start.7 = (bf16[512,512]{1,0:T(8,128)(2,1)}, bf16[512,512]{1,0:T(8,128)(2,1)S(1)}, u32[]{:S(2)}) copy-start(bf16[512,512]{1,0:T(8,128)(2,1)S(1)} %make.23.refs_1_) | copy-start | bytes 1572868
  147.7 8.5 %collective-permute-start.11 = (bf16[512,512]{1,0:T(8,128)(2,1)S(1)}, bf16[512,512]{1,0:T(8,128)(2,1)S(1)}, u32[]{:S(2)}, u32[]{:S(2)}) collective-permute-start(bf16[512,512]{1,0:T(8,128)(2,1)S(1)} %make.23.refs_1_), channel_id=1, source_target_pairs={{4,8},{6,10},{8,4},{10,6},{5,9},{7,11},{9,5},{11,7},{20,24},{22,26... | collective-permute-start | bytes 1572872 | tf_op jit(solution)/shard_map/all_mid_a/ppermute | solution.py:55
  148.4 12.1 %collective-permute-start.12 = (bf16[512,512]{1,0:T(8,128)(2,1)S(1)}, bf16[512,512]{1,0:T(8,128)(2,1)S(1)}, u32[]{:S(2)}, u32[]{:S(2)}) collective-permute-start(bf16[512,512]{1,0:T(8,128)(2,1)S(1)} %make.23.refs_1_), channel_id=1, source_target_pairs={{0,4},{2,6},{4,0},{6,2},{8,12},{10,14},{12,8},{14,10},{1,5},{3,7},... | collective-permute-start | bytes 1572872 | tf_op jit(solution)/shard_map/all_in_0a/ppermute | solution.py:55
  153.6 14.1 %collective-permute-start.15 = (bf16[512,512]{1,0:T(8,128)(2,1)S(1)}, bf16[512,512]{1,0:T(8,128)(2,1)S(1)}, u32[]{:S(2)}, u32[]{:S(2)}) collective-permute-start(bf16[512,512]{1,0:T(8,128)(2,1)S(1)} %make.24), channel_id=1, source_target_pairs={{4,6},{6,4},{8,10},{10,8},{5,7},{7,5},{9,11},{11,9},{20,22},{22,20... | collective-permute-start | bytes 1572872 | tf_op jit(solution)/shard_map/sum_x_b/ppermute | solution.py:55
  160.5 0.8 copy-start.4
  163.3 0.8 copy-start.9
  164.1 29.2 %collective-permute-start.20 = (bf16[512,768]{1,0:T(8,128)(2,1)}, bf16[512,768]{1,0:T(8,128)(2,1)}, u32[]{:S(2)}, u32[]{:S(2)}) collective-permute-start(bf16[512,768]{1,0:T(8,128)(2,1)} %make.25), channel_id=1, source_target_pairs={{0,2},{2,0},{4,6},{6,4},{8,10},{10,8},{12,14},{14,12},{1,3},{3,1},... | collective-permute-start | bytes 2359304 | tf_op jit(solution)/shard_map/x3_t/ppermute | solution.py:55
  165.9 14.5 %collective-permute-start.14 = (bf16[512,512]{1,0:T(8,128)(2,1)}, bf16[512,512]{1,0:T(8,128)(2,1)}, u32[]{:S(2)}, u32[]{:S(2)}) collective-permute-start(bf16[512,512]{1,0:T(8,128)(2,1)} %make.26), channel_id=1, source_target_pairs={{0,4},{2,6},{4,0},{6,2},{8,12},{10,14},{12,8},{14,10},{1,5},{3,7},... | collective-permute-start | bytes 1572872 | tf_op jit(solution)/shard_map/all_in_1a/ppermute | solution.py:55
  170.0 14.5 %copy-start.3 = (bf16[512,1024]{1,0:T(8,128)(2,1)S(1)}, bf16[512,1024]{1,0:T(8,128)(2,1)}, u32[]{:S(2)}) copy-start(bf16[512,1024]{1,0:T(8,128)(2,1)} %copy-done.2) | copy-start | bytes 3145732
  170.0 23.3 %collective-permute-start.18 = (bf16[512,512]{1,0:T(8,128)(2,1)}, bf16[512,512]{1,0:T(8,128)(2,1)}, u32[]{:S(2)}, u32[]{:S(2)}) collective-permute-start(bf16[512,512]{1,0:T(8,128)(2,1)} %make.27.refs_1_), channel_id=1, source_target_pairs={{4,8},{6,10},{8,4},{10,6},{5,9},{7,11},{9,5},{11,7},{20,24},{22,26... | collective-permute-start | bytes 1572872 | tf_op jit(solution)/shard_map/all_mid_b/ppermute | solution.py:55
  171.6 21.7 %collective-permute-start.19 = (bf16[512,512]{1,0:T(8,128)(2,1)}, bf16[512,512]{1,0:T(8,128)(2,1)}, u32[]{:S(2)}, u32[]{:S(2)}) collective-permute-start(bf16[512,512]{1,0:T(8,128)(2,1)} %make.27.refs_1_), channel_id=1, source_target_pairs={{4,0},{6,2},{8,12},{10,14},{5,1},{7,3},{9,13},{11,15},{20,16},{22,... | collective-permute-start | bytes 1572872 | tf_op jit(solution)/shard_map/all_in_0b/ppermute | solution.py:55
  172.9 1.0 copy-start.5
  174.0 1.0 copy-start.8
  175.1 21.1 %collective-permute-start.22 = (bf16[512,512]{1,0:T(8,128)(2,1)S(1)}, bf16[512,512]{1,0:T(8,128)(2,1)}, u32[]{:S(2)}, u32[]{:S(2)}) collective-permute-start(bf16[512,512]{1,0:T(8,128)(2,1)S(1)} %make.28.refs_0_), channel_id=1, source_target_pairs={{0,2},{2,0},{4,6},{6,4},{8,10},{10,8},{12,14},{14,12},{1,3},{3,1},... | collective-permute-start | bytes 1572872 | tf_op jit(solution)/shard_map/all_x_0a/ppermute | solution.py:55
  180.4 1.0 copy-start.10
  183.4 22.9 %collective-permute-start.17 = (bf16[512,512]{1,0:T(8,128)(2,1)}, bf16[512,512]{1,0:T(8,128)(2,1)}, u32[]{:S(2)}, u32[]{:S(2)}) collective-permute-start(bf16[512,512]{1,0:T(8,128)(2,1)} %make.29.refs_1_), channel_id=1, source_target_pairs={{0,2},{2,0},{4,6},{6,4},{8,10},{10,8},{12,14},{14,12},{1,3},{3,1},... | collective-permute-start | bytes 1572872 | tf_op jit(solution)/shard_map/all_x_1a/ppermute | solution.py:55
  193.3 2.9 %copy-start.6 = (bf16[512,512]{1,0:T(8,128)(2,1)S(1)}, bf16[512,512]{1,0:T(8,128)(2,1)}, u32[]{:S(2)}) copy-start(bf16[512,512]{1,0:T(8,128)(2,1)} %copy-done.4) | copy-start | bytes 1572868
  193.3 13.0 %collective-permute-start.21 = (bf16[512,512]{1,0:T(8,128)(2,1)}, bf16[512,512]{1,0:T(8,128)(2,1)S(1)}, u32[]{:S(2)}, u32[]{:S(2)}) collective-permute-start(bf16[512,512]{1,0:T(8,128)(2,1)} %collective-permute-done.18.refs_1_), channel_id=1, source_target_pairs={{4,0},{6,2},{8,12},{10,14},{5,1},{7,3},{9,13},{11,15},{20,16},{22,... | collective-permute-start | bytes 1572872 | tf_op jit(solution)/shard_map/all_in_1b/ppermute | solution.py:55
  206.3 4.1 %collective-permute-start.24 = (f32[512,896]{1,0:T(8,128)}, f32[512,896]{1,0:T(8,128)S(1)}, u32[]{:S(2)}, u32[]{:S(2)}) collective-permute-start(f32[512,896]{1,0:T(8,128)} %get-tuple-element.130), channel_id=1, source_target_pairs={{0,1},{1,0},{2,3},{3,2},{4,5},{5,4},{6,7},{7,6},{8,9},{9,8},{10,11... | collective-permute-start | bytes 5505032 | tf_op jit(solution)/shard_map/core_high/ppermute | solution.py:55
  206.4 6.6 %collective-permute-start.23 = (f32[512,896]{1,0:T(8,128)}, f32[512,896]{1,0:T(8,128)S(1)}, u32[]{:S(2)}, u32[]{:S(2)}) collective-permute-start(f32[512,896]{1,0:T(8,128)} %get-tuple-element.128), channel_id=1, source_target_pairs={{0,1},{1,0},{2,3},{3,2},{4,5},{5,4},{6,7},{7,6},{8,9},{9,8},{10,11... | collective-permute-start | bytes 5505032 | tf_op jit(solution)/shard_map/core_low/ppermute | solution.py:55
  207.0 15.3 %collective-permute-start.26 = (bf16[512,512]{1,0:T(8,128)(2,1)S(1)}, bf16[512,512]{1,0:T(8,128)(2,1)S(1)}, u32[]{:S(2)}, u32[]{:S(2)}) collective-permute-start(bf16[512,512]{1,0:T(8,128)(2,1)S(1)} %make.30.refs_0_), channel_id=1, source_target_pairs={{0,2},{2,0},{4,6},{6,4},{8,10},{10,8},{12,14},{14,12},{1,3},{3,1},... | collective-permute-start | bytes 1572872 | tf_op jit(solution)/shard_map/all_x_0b/ppermute | solution.py:55
  210.0 3.0 %copy-start.11 = (f32[512,896]{1,0:T(8,128)S(1)}, f32[512,896]{1,0:T(8,128)}, u32[]{:S(2)}) copy-start(f32[512,896]{1,0:T(8,128)} %get-tuple-element.128) | copy-start | bytes 5505028
  210.0 22.1 %collective-permute-start.25 = (bf16[512,512]{1,0:T(8,128)(2,1)S(1)}, bf16[512,512]{1,0:T(8,128)(2,1)S(1)}, u32[]{:S(2)}, u32[]{:S(2)}) collective-permute-start(bf16[512,512]{1,0:T(8,128)(2,1)S(1)} %make.31.refs_1_), channel_id=1, source_target_pairs={{0,2},{2,0},{4,6},{6,4},{8,10},{10,8},{12,14},{14,12},{1,3},{3,1},... | collective-permute-start | bytes 1572872 | tf_op jit(solution)/shard_map/all_x_1b/ppermute | solution.py:55

commit v3 on v2

--- a/solution.py
+++ b/solution.py
@@ -380,14 +380,15 @@
         [(r2_h, 4, 1), (wide, 7, 1), (m_a, 3, 1), (xm_a, 1, 1)],
     ]
     t00_a = put(one(x0, 2, 2), sums, 2)
+    e00_a = send("all_in_0a", t00_a, Z_NEAR)
     t10_a = send("all_mid_a", t00_a, Z_MID)
-    e00_a = send("all_in_0a", t00_a, Z_NEAR)
     m_b, t00_a = barrier(m_b, t00_a)
     y9 = put(None, [[(after(wide, t00_a), 12, 2), (r2_t, 0, 2), (m_b, 0, 2)]], 2)
     xm_b = send("sum_x_b", y9, X_MID)
     y8 = put(one(after(r2_t, y9), 0, 2), [[(a, 0, 2)], [(a, 6, 1)]], 3)
 
-    t10_a, e00_a, y8 = barrier(t10_a, e00_a, y8)
+    e00_a, y8 = barrier(e00_a, y8)
+    t10_a, y8 = barrier(t10_a, y8)
     y10 = put(one(x0, 4, 2), one(t10_a, 0, 2), 2)
     e10_a = send("all_in_1a", y10, Z_NEAR)
     x3_h, y10 = barrier(x3_h, y10)

time: 237 us -> 235 us (level)
  waiting for transfers between devices: 49.5 us -> 54.2 us
  local copies, waits for them, and re-layouts: 6.19 us -> 2.47 us
  starting transfers between devices: 44 us -> 40.7 us
    ppermute x27, waiting for transfers between devices: 49.5 us -> 54.2 us  [send(): return lax.ppermute(value, axis, way)]
    unnamed x24 -> x18, local copies, waits for them, and re-layouts: 6.11 us -> 2.39 us
    ppermute x27, starting transfers between devices: 44 us -> 40.7 us  [send(): return lax.ppermute(value, axis, way)]
  transfers between devices with their start and end apart: 27 -> 27, of which waited for: 8 -> 9; matrix products, arithmetic and copies ran while one was open for 1% -> 1% of each run, Pallas kernels for 55% -> 56%
where the time goes in v3:
time: 235 us; the launch traced here: 234 us
  Pallas kernels  134 us (57%)
  waiting for transfers between devices  54.2 us (23%)
  starting transfers between devices  40.7 us (17%)
  other arithmetic  2.58 us (1%)
  local copies, waits for them, and re-layouts  2.47 us (1%)
    ppermute x27, waiting for transfers between devices, send(): return lax.ppermute(value, axis, way)  54.2 us
    ppermute x27, starting transfers between devices, send(): return lax.ppermute(value, axis, way)  40.7 us
    pallas_call x4, Pallas kernels, grad_pieces(): pl.pallas_call(functools.partial(grad_kernel, *cuts, 2 if halves else 1),...  37.7 us
    pallas_call x16, Pallas kernels, make(): pl.pallas_call(functools.partial(make_kernel, plans), grid_spec=pltpu.Pre...  32.8 us
    pallas_call x3, Pallas kernels, grad_blocks(): pl.pallas_call(functools.partial(grad_sum_kernel, total is not None), gri...  31 us
    pallas_call x3, Pallas kernels, tile_part(): pl.pallas_call(functools.partial(tile_kernel, tokens, count), grid_spec=p...  18.8 us
    pallas_call x1, Pallas kernels, act_parts(): pl.pallas_call(functools.partial(act_kernel, spans), grid_spec=pltpu.Pref...  13.6 us
  transfers between devices with their start and end apart: 27, of which 9 were waited for; matrix products, arithmetic and copies ran while one was open for 1% of the time, Pallas kernels for 56%

profile of v3, /device:TPU:0, one launch (start us, length us, event | category | flops | bytes accessed | tf_op | source)
XLA Modules:
  0.0 234.0 jit_solution(5057730206203511699)
XLA Ops:
  0.0 3.0 %collective-permute-start.2 = (bf16[512,1792]{1,0:T(8,128)(2,1)}, bf16[512,1792]{1,0:T(8,128)(2,1)}, u32[]{:S(2)}, u32[]{:S(2)}) collective-permute-start(bf16[512,1792]{1,0:T(8,128)(2,1)} %refs_0_), channel_id=1, source_target_pairs={{0,4},{2,6},{4,0},{6,2},{8,12},{10,14},{12,8},{14,10},{1,5},{3,7},... | collective-permute-start | bytes 5505032 | tf_op jit(solution)/shard_map/near/ppermute | solution.py:55
  3.0 1.9 collective-permute-start.1
  4.9 1.5 collective-permute-start
  6.5 13.6 %act_parts.1 = (f32[512,4096]{1,0:T(8,128)}, bf16[512,1792]{1,0:T(8,128)(2,1)}, bf16[512,1280]{1,0:T(8,128)(2,1)}, bf16[512,1024]{1,0:T(8,128)(2,1)}) custom-call(s32[8]{0:T(128)S(1)} %stack.92.place_ref, bf16[512,1024]{1,0:T(8,128)(2,1)} %acts_ref.1, bf16[1024,4096]{1,0:T(8,128)(2,1)} %basis_ref.5), custom_call_target="tpu_custom_call" | custom-call | flops 1000 | bytes 1000 | tf_op jit(solution)/shard_map/act_parts/pallas_call | solution.py:86
  20.1 7.9 %grad_blocks.3.refs_4_ = f32[512,1792]{1,0:T(8,128)} custom-call(s32[1]{0:T(128)} %bitcast.9.place_ref, bf16[512,1792]{1,0:T(8,128)(2,1)} %refs_0_, bf16[14336,1792]{1,0:T(8,128)(2,1)} %basis_ref.9), custom_call_target="tpu_custom_call" | custom-call | flops 1000 | bytes 1000 | tf_op jit(solution)/shard_map/grad_blocks/pallas_call | solution.py:183
  28.0 15.3 %collective-permute-done.2.refs_0_.refs_1_.refs_2_ = bf16[512,1792]{1,0:T(8,128)(2,1)} collective-permute-done((bf16[512,1792]{1,0:T(8,128)(2,1)}, bf16[512,1792]{1,0:T(8,128)(2,1)}, u32[]{:S(2)}, u32[]{:S(2)}) %collective-permute-start.2) | collective-permute-done | bytes 1835040 | tf_op jit(solution)/shard_map/near/ppermute | solution.py:55
  43.3 1.7 collective-permute-start.4
  45.0 2.8 %make.16 = bf16[512,1792]{1,0:T(8,128)(2,1)} custom-call(s32[1]{0:T(128)} %bitcast.1.place_ref, bf16[512,1792]{1,0:T(8,128)(2,1)} %get-tuple-element.71.refs_0_, bf16[512,1792]{1,0:T(8,128)(2,1)} %collective-permute-done.1.refs_1_), custom_call_target="tpu_custom_call" | custom-call | flops 1000 | bytes 1000 | tf_op jit(solution)/shard_map/make/pallas_call | solution.py:248
  47.8 4.2 %collective-permute-start.3 = (bf16[512,1792]{1,0:T(8,128)(2,1)}, bf16[512,1792]{1,0:T(8,128)(2,1)}, u32[]{:S(2)}, u32[]{:S(2)}) collective-permute-start(bf16[512,1792]{1,0:T(8,128)(2,1)} %make.16), channel_id=1, source_target_pairs={{0,4},{2,6},{4,0},{6,2},{8,12},{10,14},{12,8},{14,10},{1,5},{3,7},... | collective-permute-start | bytes 5505032 | tf_op jit(solution)/shard_map/r1/ppermute | solution.py:55
  51.9 1.9 collective-permute-start.7
  54.0 14.6 %grad_blocks.4.refs_2_ = f32[512,1792]{1,0:T(8,128)} custom-call(s32[2]{0:T(128)S(1)} %pad_add_fusion.place_ref, bf16[512,1792]{1,0:T(8,128)(2,1)} %collective-permute-done.2.refs_0_.refs_1_.refs_2_, bf16[512,1792]{1,0:T(8,128)(2,1)} %collective-permute-done.refs_1_.refs_0_, bf16[14336,1792]{1,0:T(8,128)(2,1)} %basis_ref.9, bf16[14336,1792]{1,0:T(8,128)(2,1)} %basis_ref.9, ...), custom_call_target="tpu_custom_call" | custom-call | flops 1000 | bytes 1000 | tf_op jit(solution)/shard_map/grad_blocks/pallas_call | solution.py:183
  68.6 17.4 %collective-permute-done.4.refs_1_.refs_0_.refs_2_ = bf16[512,1792]{1,0:T(8,128)(2,1)S(1)} collective-permute-done((bf16[512,1792]{1,0:T(8,128)(2,1)}, bf16[512,1792]{1,0:T(8,128)(2,1)S(1)}, u32[]{:S(2)}, u32[]{:S(2)}) %collective-permute-start.4) | collective-permute-done | bytes 1835040 | tf_op jit(solution)/shard_map/near_on/ppermute | solution.py:55
  87.3 2.4 %make.17 = bf16[512,1280]{1,0:T(8,128)(2,1)} custom-call(s32[1]{0:T(128)} %bitcast.1.place_ref, bf16[512,1280]{1,0:T(8,128)(2,1)} %get-tuple-element.76.refs_0_, bf16[512,1792]{1,0:T(8,128)(2,1)} %copy-done), custom_call_target="tpu_custom_call" | custom-call | flops 1000 | bytes 1000 | tf_op jit(solution)/shard_map/make/pallas_call | solution.py:248
  91.1 2.8 %make.18 = bf16[512,1792]{1,0:T(8,128)(2,1)} custom-call(s32[1]{0:T(128)} %bitcast.1.place_ref, bf16[512,1792]{1,0:T(8,128)(2,1)} %collective-permute-done.3.refs_0_.refs_1_, bf16[512,1792]{1,0:T(8,128)(2,1)} %copy-done), custom_call_target="tpu_custom_call" | custom-call | flops 1000 | bytes 1000 | tf_op jit(solution)/shard_map/make/pallas_call | solution.py:248
  93.8 1.5 collective-permute-start.10
  95.3 2.3 make.19
  97.6 1.7 collective-permute-start.5
  99.3 2.5 %make.20 = bf16[512,1024]{1,0:T(8,128)(2,1)} custom-call(s32[1]{0:T(128)} %bitcast.1.place_ref, bf16[512,1024]{1,0:T(8,128)(2,1)} %get-tuple-element.88.refs_0_, bf16[512,1792]{1,0:T(8,128)(2,1)} %copy-done), custom_call_target="tpu_custom_call" | custom-call | flops 1000 | bytes 1000 | tf_op jit(solution)/shard_map/make/pallas_call | solution.py:248
  101.8 3.2 %collective-permute-start.9 = (bf16[512,1024]{1,0:T(8,128)(2,1)}, bf16[512,1024]{1,0:T(8,128)(2,1)S(1)}, u32[]{:S(2)}, u32[]{:S(2)}) collective-permute-start(bf16[512,1024]{1,0:T(8,128)(2,1)} %make.20), channel_id=1, source_target_pairs={{0,4},{2,6},{4,0},{6,2},{8,12},{10,14},{12,8},{14,10},{1,5},{3,7},... | collective-permute-start | bytes 3145736 | tf_op jit(solution)/shard_map/r2_t/ppermute | solution.py:55
  105.1 9.1 %grad_pieces.4.refs_2_ = f32[512,1792]{1,0:T(8,128)} custom-call(s32[2]{0:T(128)S(1)} %pad_add_fusion.2.place_ref, bf16[14336,1792]{1,0:T(8,128)(2,1)} %basis_ref.9, bf16[512,1792]{1,0:T(8,128)(2,1)S(1)} %copy-done.1, bf16[512,1792]{1,0:T(8,128)(2,1)} %collective-permute-done.7.refs_1_, f32[512,1792]{1,0:T(8,128)} %grad_blocks.4.refs_2_), custom_call_target="tpu_custom_call" | custom-call | flops 1000 | bytes 1000 | tf_op jit(solution)/shard_map/grad_pieces/pallas_call | solution.py:143
  114.2 9.6 %grad_pieces.5.refs_2_ = f32[512,1792]{1,0:T(8,128)} custom-call(s32[2]{0:T(128)S(1)} %pad_add_fusion.1.place_ref, bf16[14336,1792]{1,0:T(8,128)(2,1)} %basis_ref.9, bf16[512,1792]{1,0:T(8,128)(2,1)} %collective-permute-done.3.refs_0_.refs_1_, bf16[512,1792]{1,0:T(8,128)(2,1)} %collective-permute-done.1.refs_1_, f32[512,1792]{1,0:T(8,128)} %grad_pieces.4.refs_2_), custom_call_target="tpu_custom_call" | custom-call | flops 1000 | bytes 1000 | tf_op jit(solution)/shard_map/grad_pieces/pallas_call | solution.py:143
  123.9 2.4 %make.21 = bf16[512,1024]{1,0:T(8,128)(2,1)} custom-call(s32[1]{0:T(128)} %bitcast.1.place_ref, f32[512,4096]{1,0:T(8,128)} %get-tuple-element.101.refs_0_.refs_2_.refs_6_, bf16[512,1280]{1,0:T(8,128)(2,1)} %collective-permute-done.6.refs_1_.refs_5_.refs_0_), custom_call_target="tpu_custom_call" | custom-call | flops 1000 | bytes 1000 | tf_op jit(solution)/shard_map/make/pallas_call | solution.py:248
  126.2 1.6 collective-permute-start.13
  127.9 2.4 %collective-permute-start.16 = (bf16[512,1280]{1,0:T(8,128)(2,1)}, bf16[512,1280]{1,0:T(8,128)(2,1)}, u32[]{:S(2)}, u32[]{:S(2)}) collective-permute-start(bf16[512,1280]{1,0:T(8,128)(2,1)} %collective-permute-done.6.refs_1_.refs_5_.refs_0_), channel_id=1, source_target_pairs={{0,2},{2,0},{12,14},{14,12},{1,3},{3,1},{13,15},{15,13},{16,18},{1... | collective-permute-start | bytes 3932168 | tf_op jit(solution)/shard_map/x3_h/ppermute | solution.py:55
  130.3 2.3 make.22
  133.5 3.6 %collective-permute-done.10.refs_0_ = bf16[512,1792]{1,0:T(8,128)(2,1)} collective-permute-done((bf16[512,1792]{1,0:T(8,128)(2,1)}, bf16[512,1792]{1,0:T(8,128)(2,1)}, u32[]{:S(2)}, u32[]{:S(2)}) %collective-permute-start.10) | collective-permute-done | bytes 1835040 | tf_op jit(solution)/shard_map/x2/ppermute | solution.py:55
  137.1 8.5 %grad_blocks.5.refs_3_ = f32[512,1792]{1,0:T(8,128)} custom-call(s32[1]{0:T(128)} %bitcast.14.place_ref, bf16[512,1792]{1,0:T(8,128)(2,1)} %collective-permute-done.10.refs_0_, bf16[14336,1792]{1,0:T(8,128)(2,1)} %basis_ref.9, f32[512,1792]{1,0:T(8,128)} %grad_pieces.5.refs_2_), custom_call_target="tpu_custom_call" | custom-call | flops 1000 | bytes 1000 | tf_op jit(solution)/shard_map/grad_blocks/pallas_call | solution.py:183
  145.6 2.1 make.23.refs_1_
  149.7 1.5 make.24
  152.0 2.0 make.25
  154.0 3.8 %collective-permute-done.12.refs_0_.refs_2_ = bf16[512,512]{1,0:T(8,128)(2,1)S(1)} collective-permute-done((bf16[512,512]{1,0:T(8,128)(2,1)S(1)}, bf16[512,512]{1,0:T(8,128)(2,1)S(1)}, u32[]{:S(2)}, u32[]{:S(2)}) %collective-permute-start.12) | collective-permute-done | bytes 524320 | tf_op jit(solution)/shard_map/all_in_0a/ppermute | solution.py:55
  157.8 2.1 make.26
  159.9 3.1 %collective-permute-done.16.refs_0_ = bf16[512,1280]{1,0:T(8,128)(2,1)} collective-permute-done((bf16[512,1280]{1,0:T(8,128)(2,1)}, bf16[512,1280]{1,0:T(8,128)(2,1)}, u32[]{:S(2)}, u32[]{:S(2)}) %collective-permute-start.16) | collective-permute-done | bytes 1310752 | tf_op jit(solution)/shard_map/x3_h/ppermute | solution.py:55
  163.0 1.5 collective-permute-start.20
  165.3 2.3 make.27.refs_1_
  167.6 1.6 collective-permute-start.18
  172.5 1.5 collective-permute-start.22
  174.0 5.7 %collective-permute-done.14.refs_0_.refs_3_ = bf16[512,512]{1,0:T(8,128)(2,1)} collective-permute-done((bf16[512,512]{1,0:T(8,128)(2,1)}, bf16[512,512]{1,0:T(8,128)(2,1)}, u32[]{:S(2)}, u32[]{:S(2)}) %collective-permute-start.14) | collective-permute-done | bytes 524320 | tf_op jit(solution)/shard_map/all_in_1a/ppermute | solution.py:55
  179.7 1.9 make.29.refs_1_
  182.1 8.8 %grad_pieces.6.refs_4_ = f32[512,1792]{1,0:T(8,128)} custom-call(s32[2]{0:T(128)S(1)} %pad_add_fusion.3.place_ref, bf16[14336,1792]{1,0:T(8,128)(2,1)} %basis_ref.9, bf16[512,1280]{1,0:T(8,128)(2,1)} %collective-permute-done.6.refs_1_.refs_5_.refs_0_, bf16[512,1024]{1,0:T(8,128)(2,1)S(1)} %copy-done.3, bf16[512,1792]{1,0:T(8,128)(2,1)S(1)} %copy-done.1, ...), custom_call_target="tpu_custom_call" | custom-call | flops 1000 | bytes 1000 | tf_op jit(solution)/shard_map/grad_pieces/pallas_call | solution.py:143
  193.5 1.5 collective-permute-done.22.refs_2_
  195.0 10.1 %grad_pieces.7 = (f32[512,896]{1,0:T(8,128)}, f32[512,896]{1,0:T(8,128)}) custom-call(s32[2]{0:T(128)S(1)} %pad_add_fusion.4.place_ref, bf16[14336,1792]{1,0:T(8,128)(2,1)} %basis_ref.9, bf16[512,1280]{1,0:T(8,128)(2,1)} %collective-permute-done.16.refs_0_, bf16[512,768]{1,0:T(8,128)(2,1)} %collective-permute-done.20.refs_1_, ...), custom_call_target="tpu_custom_call" | custom-call | flops 1000 | bytes 1000 | tf_op jit(solution)/shard_map/grad_pieces/pallas_call | solution.py:143
  205.8 1.4 collective-permute-start.26
  209.3 1.8 add_convert_fusion.high_ref
  212.1 9.3 %tile_part.3.refs_3_ = f32[1792,4096]{1,0:T(8,128)} custom-call(s32[4]{0:T(128)S(1)} %pad_add_fusion.6.place_ref, bf16[512,896]{1,0:T(8,128)(2,1)S(1)} %add_convert_fusion.1.low_ref, bf16[512,896]{1,0:T(8,128)(2,1)S(1)} %add_convert_fusion.high_ref, bf16[512,512]{1,0:T(8,128)(2,1)} %make.28.refs_0_, bf16[512,512]{1,0:T(8,128)(2,1)} %make.29.refs_1_, ...), custom_call_target="tpu_custom_call" | custom-call | flops 1000 | bytes 1000 | tf_op jit(solution)/shard_map/tile_part/pallas_call | solution.py:280
  221.4 6.5 %tile_part.4.refs_1_ = f32[1792,4096]{1,0:T(8,128)} custom-call(s32[3]{0:T(128)S(1)} %pad_add_fusion.5.place_ref, bf16[512,896]{1,0:T(8,128)(2,1)S(1)} %add_convert_fusion.1.low_ref, bf16[512,896]{1,0:T(8,128)(2,1)S(1)} %add_convert_fusion.high_ref, bf16[512,512]{1,0:T(8,128)(2,1)S(1)} %make.30.refs_0_, ...), custom_call_target="tpu_custom_call", output_to_operand_aliasing={{}: (6, {})} | custom-call | flops 1000 | bytes 1000 | tf_op jit(solution)/shard_map/tile_part/pallas_call | solution.py:280
  227.9 3.1 %collective-permute-done.25.refs_0_ = bf16[512,512]{1,0:T(8,128)(2,1)S(1)} collective-permute-done((bf16[512,512]{1,0:T(8,128)(2,1)S(1)}, bf16[512,512]{1,0:T(8,128)(2,1)S(1)}, u32[]{:S(2)}, u32[]{:S(2)}) %collective-permute-start.25) | collective-permute-done | bytes 524320 | tf_op jit(solution)/shard_map/all_x_1b/ppermute | solution.py:55
  231.0 3.0 %tile_part.5 = f32[1792,4096]{1,0:T(8,128)} custom-call(s32[1]{0:T(128)} %bitcast.place_ref, bf16[512,896]{1,0:T(8,128)(2,1)S(1)} %add_convert_fusion.1.low_ref, bf16[512,896]{1,0:T(8,128)(2,1)S(1)} %add_convert_fusion.high_ref, bf16[512,512]{1,0:T(8,128)(2,1)S(1)} %collective-permute-done.25.refs_0_, ...), custom_call_target="tpu_custom_call", output_to_operand_aliasing={{}: (4, {})} | custom-call | flops 1000 | bytes 1000 | tf_op jit(solution)/shard_map/tile_part/pallas_call | solution.py:280
  (61 shorter events, 17.6 us)
Async XLA Ops:
  0.0 43.3 %collective-permute-start.2 = (bf16[512,1792]{1,0:T(8,128)(2,1)}, bf16[512,1792]{1,0:T(8,128)(2,1)}, u32[]{:S(2)}, u32[]{:S(2)}) collective-permute-start(bf16[512,1792]{1,0:T(8,128)(2,1)} %refs_0_), channel_id=1, source_target_pairs={{0,4},{2,6},{4,0},{6,2},{8,12},{10,14},{12,8},{14,10},{1,5},{3,7},... | collective-permute-start | bytes 5505032 | tf_op jit(solution)/shard_map/near/ppermute | solution.py:55
  3.0 42.0 %collective-permute-start.1 = (bf16[512,1792]{1,0:T(8,128)(2,1)}, bf16[512,1792]{1,0:T(8,128)(2,1)}, u32[]{:S(2)}, u32[]{:S(2)}) collective-permute-start(bf16[512,1792]{1,0:T(8,128)(2,1)} %refs_0_), channel_id=1, source_target_pairs={{4,8},{6,10},{8,4},{10,6},{5,9},{7,11},{9,5},{11,7},{20,24},{22,26... | collective-permute-start | bytes 5505032 | tf_op jit(solution)/shard_map/mid_own/ppermute | solution.py:55
  4.9 49.0 %collective-permute-start = (bf16[512,1792]{1,0:T(8,128)(2,1)}, bf16[512,1792]{1,0:T(8,128)(2,1)}, u32[]{:S(2)}, u32[]{:S(2)}) collective-permute-start(bf16[512,1792]{1,0:T(8,128)(2,1)} %refs_0_), channel_id=1, source_target_pairs={{0,2},{2,0},{4,6},{6,4},{8,10},{10,8},{12,14},{14,12},{1,3},{3,1},... | collective-permute-start | bytes 5505032 | tf_op jit(solution)/shard_map/own_x/ppermute | solution.py:55
  43.3 42.6 %collective-permute-start.4 = (bf16[512,1792]{1,0:T(8,128)(2,1)}, bf16[512,1792]{1,0:T(8,128)(2,1)S(1)}, u32[]{:S(2)}, u32[]{:S(2)}) collective-permute-start(bf16[512,1792]{1,0:T(8,128)(2,1)} %collective-permute-done.2.refs_0_.refs_1_.refs_2_), channel_id=1, source_target_pairs={{0,2},{2,0},{4,8},{6,10},{8,4},{10,6},{12,14},{14,12},{1,3},{3,1},... | collective-permute-start | bytes 5505032 | tf_op jit(solution)/shard_map/near_on/ppermute | solution.py:55
  47.8 43.3 %collective-permute-start.3 = (bf16[512,1792]{1,0:T(8,128)(2,1)}, bf16[512,1792]{1,0:T(8,128)(2,1)}, u32[]{:S(2)}, u32[]{:S(2)}) collective-permute-start(bf16[512,1792]{1,0:T(8,128)(2,1)} %make.16), channel_id=1, source_target_pairs={{0,4},{2,6},{4,0},{6,2},{8,12},{10,14},{12,8},{14,10},{1,5},{3,7},... | collective-permute-start | bytes 5505032 | tf_op jit(solution)/shard_map/r1/ppermute | solution.py:55
  51.9 53.1 %collective-permute-start.7 = (bf16[512,1792]{1,0:T(8,128)(2,1)}, bf16[512,1792]{1,0:T(8,128)(2,1)}, u32[]{:S(2)}, u32[]{:S(2)}) collective-permute-start(bf16[512,1792]{1,0:T(8,128)(2,1)} %collective-permute-done.1.refs_1_), channel_id=1, source_target_pairs={{4,6},{6,4},{8,10},{10,8},{5,7},{7,5},{9,11},{11,9},{20,22},{22,20... | collective-permute-start | bytes 5505032 | tf_op jit(solution)/shard_map/mid_own_x/ppermute | solution.py:55
  85.9 1.3 copy-start
  89.7 34.2 %collective-permute-start.6 = (bf16[512,1280]{1,0:T(8,128)(2,1)}, bf16[512,1280]{1,0:T(8,128)(2,1)}, u32[]{:S(2)}, u32[]{:S(2)}) collective-permute-start(bf16[512,1280]{1,0:T(8,128)(2,1)} %make.17), channel_id=1, source_target_pairs={{0,4},{2,6},{4,0},{6,2},{8,12},{10,14},{12,8},{14,10},{1,5},{3,7},... | collective-permute-start | bytes 3932168 | tf_op jit(solution)/shard_map/r2_h/ppermute | solution.py:55
  93.8 43.3 %collective-permute-start.10 = (bf16[512,1792]{1,0:T(8,128)(2,1)}, bf16[512,1792]{1,0:T(8,128)(2,1)}, u32[]{:S(2)}, u32[]{:S(2)}) collective-permute-start(bf16[512,1792]{1,0:T(8,128)(2,1)} %make.18), channel_id=1, source_target_pairs={{0,2},{2,0},{4,6},{6,4},{8,10},{10,8},{12,14},{14,12},{1,3},{3,1},... | collective-permute-start | bytes 5505032 | tf_op jit(solution)/shard_map/x2/ppermute | solution.py:55
  97.6 32.7 %collective-permute-start.5 = (bf16[512,1024]{1,0:T(8,128)(2,1)}, bf16[512,1024]{1,0:T(8,128)(2,1)}, u32[]{:S(2)}, u32[]{:S(2)}) collective-permute-start(bf16[512,1024]{1,0:T(8,128)(2,1)} %make.19), channel_id=1, source_target_pairs={{4,8},{6,10},{8,4},{10,6},{5,9},{7,11},{9,5},{11,7},{20,24},{22,26... | collective-permute-start | bytes 3145736 | tf_op jit(solution)/shard_map/mid_a/ppermute | solution.py:55
  99.3 5.8 %copy-start.1 = (bf16[512,1792]{1,0:T(8,128)(2,1)S(1)}, bf16[512,1792]{1,0:T(8,128)(2,1)}, u32[]{:S(2)}) copy-start(bf16[512,1792]{1,0:T(8,128)(2,1)} %copy-done) | copy-start | bytes 5505028
  101.8 43.8 %collective-permute-start.9 = (bf16[512,1024]{1,0:T(8,128)(2,1)}, bf16[512,1024]{1,0:T(8,128)(2,1)S(1)}, u32[]{:S(2)}, u32[]{:S(2)}) collective-permute-start(bf16[512,1024]{1,0:T(8,128)(2,1)} %make.20), channel_id=1, source_target_pairs={{0,4},{2,6},{4,0},{6,2},{8,12},{10,14},{12,8},{14,10},{1,5},{3,7},... | collective-permute-start | bytes 3145736 | tf_op jit(solution)/shard_map/r2_t/ppermute | solution.py:55
  126.2 23.5 %collective-permute-start.13 = (bf16[512,1024]{1,0:T(8,128)(2,1)}, bf16[512,1024]{1,0:T(8,128)(2,1)}, u32[]{:S(2)}, u32[]{:S(2)}) collective-permute-start(bf16[512,1024]{1,0:T(8,128)(2,1)} %make.21), channel_id=1, source_target_pairs={{4,8},{6,10},{8,4},{10,6},{5,9},{7,11},{9,5},{11,7},{20,24},{22,26... | collective-permute-start | bytes 3145736 | tf_op jit(solution)/shard_map/mid_b/ppermute | solution.py:55
  127.9 35.1 %collective-permute-start.16 = (bf16[512,1280]{1,0:T(8,128)(2,1)}, bf16[512,1280]{1,0:T(8,128)(2,1)}, u32[]{:S(2)}, u32[]{:S(2)}) collective-permute-start(bf16[512,1280]{1,0:T(8,128)(2,1)} %collective-permute-done.6.refs_1_.refs_5_.refs_0_), channel_id=1, source_target_pairs={{0,2},{2,0},{12,14},{14,12},{1,3},{3,1},{13,15},{15,13},{16,18},{1... | collective-permute-start | bytes 3932168 | tf_op jit(solution)/shard_map/x3_h/ppermute | solution.py:55
  132.6 13.0 %collective-permute-start.8 = (bf16[512,512]{1,0:T(8,128)(2,1)}, bf16[512,512]{1,0:T(8,128)(2,1)S(1)}, u32[]{:S(2)}, u32[]{:S(2)}) collective-permute-start(bf16[512,512]{1,0:T(8,128)(2,1)} %make.22), channel_id=1, source_target_pairs={{4,6},{6,4},{8,10},{10,8},{5,7},{7,5},{9,11},{11,9},{20,22},{22,20... | collective-permute-start | bytes 1572872 | tf_op jit(solution)/shard_map/sum_x_a/ppermute | solution.py:55
  145.6 2.1 copy-start.2
  147.7 3.6 %copy-start.4 = (bf16[512,512]{1,0:T(8,128)(2,1)}, bf16[512,512]{1,0:T(8,128)(2,1)S(1)}, u32[]{:S(2)}) copy-start(bf16[512,512]{1,0:T(8,128)(2,1)S(1)} %make.23.refs_1_) | copy-start | bytes 1572868
  147.7 10.1 %collective-permute-start.12 = (bf16[512,512]{1,0:T(8,128)(2,1)S(1)}, bf16[512,512]{1,0:T(8,128)(2,1)S(1)}, u32[]{:S(2)}, u32[]{:S(2)}) collective-permute-start(bf16[512,512]{1,0:T(8,128)(2,1)S(1)} %make.23.refs_1_), channel_id=1, source_target_pairs={{0,4},{2,6},{4,0},{6,2},{8,12},{10,14},{12,8},{14,10},{1,5},{3,7},... | collective-permute-start | bytes 1572872 | tf_op jit(solution)/shard_map/all_in_0a/ppermute | solution.py:55
  149.0 8.7 %collective-permute-start.11 = (bf16[512,512]{1,0:T(8,128)(2,1)S(1)}, bf16[512,512]{1,0:T(8,128)(2,1)S(1)}, u32[]{:S(2)}, u32[]{:S(2)}) collective-permute-start(bf16[512,512]{1,0:T(8,128)(2,1)S(1)} %make.23.refs_1_), channel_id=1, source_target_pairs={{4,8},{6,10},{8,4},{10,6},{5,9},{7,11},{9,5},{11,7},{20,24},{22,26... | collective-permute-start | bytes 1572872 | tf_op jit(solution)/shard_map/all_mid_a/ppermute | solution.py:55
  151.3 14.0 %collective-permute-start.15 = (bf16[512,512]{1,0:T(8,128)(2,1)S(1)}, bf16[512,512]{1,0:T(8,128)(2,1)S(1)}, u32[]{:S(2)}, u32[]{:S(2)}) collective-permute-start(bf16[512,512]{1,0:T(8,128)(2,1)S(1)} %make.24), channel_id=1, source_target_pairs={{4,6},{6,4},{8,10},{10,8},{5,7},{7,5},{9,11},{11,9},{20,22},{22,20... | collective-permute-start | bytes 1572872 | tf_op jit(solution)/shard_map/sum_x_b/ppermute | solution.py:55
  157.8 7.5 %copy-start.6 = (bf16[512,512]{1,0:T(8,128)(2,1)}, bf16[512,512]{1,0:T(8,128)(2,1)S(1)}, u32[]{:S(2)}) copy-start(bf16[512,512]{1,0:T(8,128)(2,1)S(1)} %collective-permute-done.11.refs_1_) | copy-start | bytes 1572868
  163.0 27.9 %collective-permute-start.20 = (bf16[512,768]{1,0:T(8,128)(2,1)}, bf16[512,768]{1,0:T(8,128)(2,1)}, u32[]{:S(2)}, u32[]{:S(2)}) collective-permute-start(bf16[512,768]{1,0:T(8,128)(2,1)} %make.25), channel_id=1, source_target_pairs={{0,2},{2,0},{4,6},{6,4},{8,10},{10,8},{12,14},{14,12},{1,3},{3,1},... | collective-permute-start | bytes 2359304 | tf_op jit(solution)/shard_map/x3_t/ppermute | solution.py:55
  164.5 15.2 %collective-permute-start.14 = (bf16[512,512]{1,0:T(8,128)(2,1)}, bf16[512,512]{1,0:T(8,128)(2,1)}, u32[]{:S(2)}, u32[]{:S(2)}) collective-permute-start(bf16[512,512]{1,0:T(8,128)(2,1)} %make.26), channel_id=1, source_target_pairs={{0,4},{2,6},{4,0},{6,2},{8,12},{10,14},{12,8},{14,10},{1,5},{3,7},... | collective-permute-start | bytes 1572872 | tf_op jit(solution)/shard_map/all_in_1a/ppermute | solution.py:55
  167.6 14.5 %copy-start.3 = (bf16[512,1024]{1,0:T(8,128)(2,1)S(1)}, bf16[512,1024]{1,0:T(8,128)(2,1)}, u32[]{:S(2)}) copy-start(bf16[512,1024]{1,0:T(8,128)(2,1)} %copy-done.2) | copy-start | bytes 3145732
  167.6 23.3 %collective-permute-start.18 = (bf16[512,512]{1,0:T(8,128)(2,1)}, bf16[512,512]{1,0:T(8,128)(2,1)}, u32[]{:S(2)}, u32[]{:S(2)}) collective-permute-start(bf16[512,512]{1,0:T(8,128)(2,1)} %make.27.refs_1_), channel_id=1, source_target_pairs={{4,8},{6,10},{8,4},{10,6},{5,9},{7,11},{9,5},{11,7},{20,24},{22,26... | collective-permute-start | bytes 1572872 | tf_op jit(solution)/shard_map/all_mid_b/ppermute | solution.py:55
  169.2 21.7 %collective-permute-start.19 = (bf16[512,512]{1,0:T(8,128)(2,1)}, bf16[512,512]{1,0:T(8,128)(2,1)}, u32[]{:S(2)}, u32[]{:S(2)}) collective-permute-start(bf16[512,512]{1,0:T(8,128)(2,1)} %make.27.refs_1_), channel_id=1, source_target_pairs={{4,0},{6,2},{8,12},{10,14},{5,1},{7,3},{9,13},{11,15},{20,16},{22,... | collective-permute-start | bytes 1572872 | tf_op jit(solution)/shard_map/all_in_0b/ppermute | solution.py:55
  170.6 1.0 copy-start.5
  171.6 8.0 %copy-start.7 = (bf16[512,512]{1,0:T(8,128)(2,1)S(1)}, bf16[512,512]{1,0:T(8,128)(2,1)}, u32[]{:S(2)}) copy-start(bf16[512,512]{1,0:T(8,128)(2,1)} %copy-done.6) | copy-start | bytes 1572868
  172.5 22.5 %collective-permute-start.22 = (bf16[512,512]{1,0:T(8,128)(2,1)}, bf16[512,512]{1,0:T(8,128)(2,1)}, u32[]{:S(2)}, u32[]{:S(2)}) collective-permute-start(bf16[512,512]{1,0:T(8,128)(2,1)} %make.28.refs_0_), channel_id=1, source_target_pairs={{0,2},{2,0},{4,6},{6,4},{8,10},{10,8},{12,14},{14,12},{1,3},{3,1},... | collective-permute-start | bytes 1572872 | tf_op jit(solution)/shard_map/all_x_0a/ppermute | solution.py:55
  181.6 23.6 %collective-permute-start.17 = (bf16[512,512]{1,0:T(8,128)(2,1)}, bf16[512,512]{1,0:T(8,128)(2,1)}, u32[]{:S(2)}, u32[]{:S(2)}) collective-permute-start(bf16[512,512]{1,0:T(8,128)(2,1)} %make.29.refs_1_), channel_id=1, source_target_pairs={{0,2},{2,0},{4,6},{6,4},{8,10},{10,8},{12,14},{14,12},{1,3},{3,1},... | collective-permute-start | bytes 1572872 | tf_op jit(solution)/shard_map/all_x_1a/ppermute | solution.py:55
  190.9 14.2 %collective-permute-start.21 = (bf16[512,512]{1,0:T(8,128)(2,1)}, bf16[512,512]{1,0:T(8,128)(2,1)S(1)}, u32[]{:S(2)}, u32[]{:S(2)}) collective-permute-start(bf16[512,512]{1,0:T(8,128)(2,1)} %collective-permute-done.18.refs_1_), channel_id=1, source_target_pairs={{4,0},{6,2},{8,12},{10,14},{5,1},{7,3},{9,13},{11,15},{20,16},{22,... | collective-permute-start | bytes 1572872 | tf_op jit(solution)/shard_map/all_in_1b/ppermute | solution.py:55
  205.1 4.1 %collective-permute-start.24 = (f32[512,896]{1,0:T(8,128)}, f32[512,896]{1,0:T(8,128)S(1)}, u32[]{:S(2)}, u32[]{:S(2)}) collective-permute-start(f32[512,896]{1,0:T(8,128)} %get-tuple-element.132), channel_id=1, source_target_pairs={{0,1},{1,0},{2,3},{3,2},{4,5},{5,4},{6,7},{7,6},{8,9},{9,8},{10,11... | collective-permute-start | bytes 5505032 | tf_op jit(solution)/shard_map/core_high/ppermute | solution.py:55
  205.2 6.6 %collective-permute-start.23 = (f32[512,896]{1,0:T(8,128)}, f32[512,896]{1,0:T(8,128)S(1)}, u32[]{:S(2)}, u32[]{:S(2)}) collective-permute-start(f32[512,896]{1,0:T(8,128)} %get-tuple-element.130), channel_id=1, source_target_pairs={{0,1},{1,0},{2,3},{3,2},{4,5},{5,4},{6,7},{7,6},{8,9},{9,8},{10,11... | collective-permute-start | bytes 5505032 | tf_op jit(solution)/shard_map/core_low/ppermute | solution.py:55
  205.8 15.5 %collective-permute-start.26 = (bf16[512,512]{1,0:T(8,128)(2,1)S(1)}, bf16[512,512]{1,0:T(8,128)(2,1)S(1)}, u32[]{:S(2)}, u32[]{:S(2)}) collective-permute-start(bf16[512,512]{1,0:T(8,128)(2,1)S(1)} %make.30.refs_0_), channel_id=1, source_target_pairs={{0,2},{2,0},{4,6},{6,4},{8,10},{10,8},{12,14},{14,12},{1,3},{3,1},... | collective-permute-start | bytes 1572872 | tf_op jit(solution)/shard_map/all_x_0b/ppermute | solution.py:55
  208.6 3.2 %copy-start.8 = (f32[512,896]{1,0:T(8,128)S(1)}, f32[512,896]{1,0:T(8,128)}, u32[]{:S(2)}) copy-start(f32[512,896]{1,0:T(8,128)} %get-tuple-element.130) | copy-start | bytes 5505028
  208.6 22.4 %collective-permute-start.25 = (bf16[512,512]{1,0:T(8,128)(2,1)S(1)}, bf16[512,512]{1,0:T(8,128)(2,1)S(1)}, u32[]{:S(2)}, u32[]{:S(2)}) collective-permute-start(bf16[512,512]{1,0:T(8,128)(2,1)S(1)} %make.31.refs_1_), channel_id=1, source_target_pairs={{0,2},{2,0},{4,6},{6,4},{8,10},{10,8},{12,14},{14,12},{1,3},{3,1},... | collective-permute-start | bytes 1572872 | tf_op jit(solution)/shard_map/all_x_1b/ppermute | solution.py:55

commit v4 on v3

--- a/solution.py
+++ b/solution.py
@@ -385,7 +385,7 @@
     m_b, t00_a = barrier(m_b, t00_a)
     y9 = put(None, [[(after(wide, t00_a), 12, 2), (r2_t, 0, 2), (m_b, 0, 2)]], 2)
     xm_b = send("sum_x_b", y9, X_MID)
-    y8 = put(one(after(r2_t, y9), 0, 2), [[(a, 0, 2)], [(a, 6, 1)]], 3)
+    y8 = put(one(after(r2_t, y9), 0, 2), one(a, 0, 2), 2)
 
     e00_a, y8 = barrier(e00_a, y8)
     t10_a, y8 = barrier(t10_a, y8)
@@ -395,9 +395,9 @@
     x3_t = send("x3_t", after(y8, y10), X_ALL)
     xm_b, y10 = barrier(xm_b, y10)
     sums = [[(after(wide, y10), 14, 2), (r2_t, 2, 2), (m_b, 2, 2), (xm_b, 0, 2)]]
-    t00_b = put(None, sums, 2)
+    t00_b = put(one(x0, 6, 1), sums, 2)
+    e00_b = send("all_in_0b", t00_b, Z_NEAR)
     t10_b = send("all_mid_b", t00_b, Z_MID)
-    e00_b = send("all_in_0b", t00_b, Z_IN)
     u00_a = put(one(after(e00_a, t00_b), 0, 2), one(t00_a, 0, 2), 2)
     s01_a = send("all_x_0a", u00_a, X_ALL)
 
@@ -407,13 +407,14 @@
     total = block_of([(r2_h, 0, 5), (r2_t, 0, 2)], [(b2, 0, 7)], z_block(farthest, x), after(total, u10_a))
     x3_t, total = barrier(x3_t, total)
 
-    t10_b, e00_b, total = barrier(t10_b, e00_b, total)
+    e00_b, total = barrier(e00_b, total)
+    t10_b, total = barrier(t10_b, total)
     e10_b = send("all_in_1b", t10_b, Z_IN)
     u00_b = put(one(e00_b, 0, 2), one(t00_b, 0, 2), 2)
     s01_b = send("all_x_0b", u00_b, X_ALL)
     s01_a, total = barrier(s01_a, after(total, u00_b))
     at_end = [(x3_h, 0, 5), (x3_t, 0, 2)]
-    at_mid = [(x3_t, 0, 2), (e00_a, 0, 2), (e10_a, 0, 2), (x3_t, 2, 1)]
+    at_mid = [(x3_t, 0, 2), (e00_a, 0, 2), (e10_a, 0, 2), (e00_b, 0, 1)]
     low, high = block_of(at_end, at_mid, z_block(either(farthest, near), 1 - x), total, halves=True)
 
     s11_a, e10_b, low, high = barrier(s11_a, e10_b, low, high)

time: 235 us -> 232 us (0.987)
  waiting for transfers between devices: 54.2 us -> 44.8 us
  starting transfers between devices: 40.7 us -> 46.2 us
    ppermute x27, waiting for transfers between devices: 54.2 us -> 44.8 us  [send(): return lax.ppermute(value, axis, way)]
    ppermute x27, starting transfers between devices: 40.7 us -> 46.2 us  [send(): return lax.ppermute(value, axis, way)]
  transfers between devices with their start and end apart: 27 -> 27, of which waited for: 9 -> 7; matrix products, arithmetic and copies ran while one was open for 1% -> 1% of each run, Pallas kernels for 56% -> 57%
where the time goes in v4:
time: 232 us; the launch traced here: 231 us
  Pallas kernels  134 us (58%)
  starting transfers between devices  46.2 us (20%)
  waiting for transfers between devices  44.8 us (19%)
  other arithmetic  2.73 us (1%)
  local copies, waits for them, and re-layouts  2.47 us (1%)
    ppermute x27, starting transfers between devices, send(): return lax.ppermute(value, axis, way)  46.2 us
    ppermute x27, waiting for transfers between devices, send(): return lax.ppermute(value, axis, way)  44.8 us
    pallas_call x4, Pallas kernels, grad_pieces(): pl.pallas_call(functools.partial(grad_kernel, *cuts, 2 if halves else 1),...  37.8 us
    pallas_call x16, Pallas kernels, make(): pl.pallas_call(functools.partial(make_kernel, plans), grid_spec=pltpu.Pre...  32.9 us
    pallas_call x3, Pallas kernels, grad_blocks(): pl.pallas_call(functools.partial(grad_sum_kernel, total is not None), gri...  31 us
    pallas_call x3, Pallas kernels, tile_part(): pl.pallas_call(functools.partial(tile_kernel, tokens, count), grid_spec=p...  18.8 us
    pallas_call x1, Pallas kernels, act_parts(): pl.pallas_call(functools.partial(act_kernel, spans), grid_spec=pltpu.Pref...  13.6 us
  transfers between devices with their start and end apart: 27, of which 7 were waited for; matrix products, arithmetic and copies ran while one was open for 1% of the time, Pallas kernels for 57%

profile of v4, /device:TPU:0, one launch (start us, length us, event | category | flops | bytes accessed | tf_op | source)
XLA Modules:
  0.0 230.6 jit_solution(7842137240627646283)
XLA Ops:
  0.0 3.0 %collective-permute-start.2 = (bf16[512,1792]{1,0:T(8,128)(2,1)}, bf16[512,1792]{1,0:T(8,128)(2,1)}, u32[]{:S(2)}, u32[]{:S(2)}) collective-permute-start(bf16[512,1792]{1,0:T(8,128)(2,1)} %refs_0_), channel_id=1, source_target_pairs={{0,4},{2,6},{4,0},{6,2},{8,12},{10,14},{12,8},{14,10},{1,5},{3,7},... | collective-permute-start | bytes 5505032 | tf_op jit(solution)/shard_map/near/ppermute | solution.py:55
  3.0 1.9 collective-permute-start.1
  4.9 1.5 collective-permute-start
  6.5 13.6 %act_parts.1 = (f32[512,4096]{1,0:T(8,128)}, bf16[512,1792]{1,0:T(8,128)(2,1)}, bf16[512,1280]{1,0:T(8,128)(2,1)}, bf16[512,1024]{1,0:T(8,128)(2,1)}) custom-call(s32[8]{0:T(128)S(1)} %stack.92.place_ref, bf16[512,1024]{1,0:T(8,128)(2,1)} %acts_ref.1, bf16[1024,4096]{1,0:T(8,128)(2,1)} %basis_ref.5), custom_call_target="tpu_custom_call" | custom-call | flops 1000 | bytes 1000 | tf_op jit(solution)/shard_map/act_parts/pallas_call | solution.py:86
  20.1 7.9 %grad_blocks.3.refs_4_ = f32[512,1792]{1,0:T(8,128)} custom-call(s32[1]{0:T(128)} %bitcast.9.place_ref, bf16[512,1792]{1,0:T(8,128)(2,1)} %refs_0_, bf16[14336,1792]{1,0:T(8,128)(2,1)} %basis_ref.9), custom_call_target="tpu_custom_call" | custom-call | flops 1000 | bytes 1000 | tf_op jit(solution)/shard_map/grad_blocks/pallas_call | solution.py:183
  28.0 15.3 %collective-permute-done.2.refs_0_.refs_1_ = bf16[512,1792]{1,0:T(8,128)(2,1)} collective-permute-done((bf16[512,1792]{1,0:T(8,128)(2,1)}, bf16[512,1792]{1,0:T(8,128)(2,1)}, u32[]{:S(2)}, u32[]{:S(2)}) %collective-permute-start.2) | collective-permute-done | bytes 1835040 | tf_op jit(solution)/shard_map/near/ppermute | solution.py:55
  43.3 1.7 collective-permute-start.4
  45.0 2.8 %make.16 = bf16[512,1792]{1,0:T(8,128)(2,1)} custom-call(s32[1]{0:T(128)} %bitcast.1.place_ref, bf16[512,1792]{1,0:T(8,128)(2,1)} %get-tuple-element.72.refs_0_, bf16[512,1792]{1,0:T(8,128)(2,1)} %collective-permute-done.1.refs_1_), custom_call_target="tpu_custom_call" | custom-call | flops 1000 | bytes 1000 | tf_op jit(solution)/shard_map/make/pallas_call | solution.py:248
  47.8 4.2 %collective-permute-start.3 = (bf16[512,1792]{1,0:T(8,128)(2,1)}, bf16[512,1792]{1,0:T(8,128)(2,1)}, u32[]{:S(2)}, u32[]{:S(2)}) collective-permute-start(bf16[512,1792]{1,0:T(8,128)(2,1)} %make.16), channel_id=1, source_target_pairs={{0,4},{2,6},{4,0},{6,2},{8,12},{10,14},{12,8},{14,10},{1,5},{3,7},... | collective-permute-start | bytes 5505032 | tf_op jit(solution)/shard_map/r1/ppermute | solution.py:55
  51.9 1.9 collective-permute-start.7
  53.9 14.6 %grad_blocks.4.refs_2_ = f32[512,1792]{1,0:T(8,128)} custom-call(s32[2]{0:T(128)S(1)} %pad_add_fusion.place_ref, bf16[512,1792]{1,0:T(8,128)(2,1)} %collective-permute-done.2.refs_0_.refs_1_, bf16[512,1792]{1,0:T(8,128)(2,1)} %collective-permute-done.refs_1_.refs_0_, bf16[14336,1792]{1,0:T(8,128)(2,1)} %basis_ref.9, bf16[14336,1792]{1,0:T(8,128)(2,1)} %basis_ref.9, ...), custom_call_target="tpu_custom_call" | custom-call | flops 1000 | bytes 1000 | tf_op jit(solution)/shard_map/grad_blocks/pallas_call | solution.py:183
  68.5 17.4 %collective-permute-done.4.refs_1_.refs_0_.refs_2_ = bf16[512,1792]{1,0:T(8,128)(2,1)S(1)} collective-permute-done((bf16[512,1792]{1,0:T(8,128)(2,1)}, bf16[512,1792]{1,0:T(8,128)(2,1)S(1)}, u32[]{:S(2)}, u32[]{:S(2)}) %collective-permute-start.4) | collective-permute-done | bytes 1835040 | tf_op jit(solution)/shard_map/near_on/ppermute | solution.py:55
  87.3 2.4 %make.17 = bf16[512,1280]{1,0:T(8,128)(2,1)} custom-call(s32[1]{0:T(128)} %bitcast.1.place_ref, bf16[512,1280]{1,0:T(8,128)(2,1)} %get-tuple-element.77.refs_0_, bf16[512,1792]{1,0:T(8,128)(2,1)} %copy-done), custom_call_target="tpu_custom_call" | custom-call | flops 1000 | bytes 1000 | tf_op jit(solution)/shard_map/make/pallas_call | solution.py:248
  89.7 1.4 collective-permute-start.6
  91.1 2.8 %make.18 = bf16[512,1792]{1,0:T(8,128)(2,1)} custom-call(s32[1]{0:T(128)} %bitcast.1.place_ref, bf16[512,1792]{1,0:T(8,128)(2,1)} %collective-permute-done.3.refs_0_.refs_1_, bf16[512,1792]{1,0:T(8,128)(2,1)} %copy-done), custom_call_target="tpu_custom_call" | custom-call | flops 1000 | bytes 1000 | tf_op jit(solution)/shard_map/make/pallas_call | solution.py:248
  93.8 1.5 collective-permute-start.10
  95.3 2.3 %make.19 = bf16[512,1024]{1,0:T(8,128)(2,1)} custom-call(s32[1]{0:T(128)} %bitcast.1.place_ref, f32[512,4096]{1,0:T(8,128)} %get-tuple-element.102.refs_0_.refs_2_.refs_6_.refs_1_, bf16[512,1792]{1,0:T(8,128)(2,1)} %collective-permute-done.3.refs_0_.refs_1_), custom_call_target="tpu_custom_call" | custom-call | flops 1000 | bytes 1000 | tf_op jit(solution)/shard_map/make/pallas_call | solution.py:248
  97.6 1.7 collective-permute-start.5
  99.4 2.6 %make.20 = bf16[512,1024]{1,0:T(8,128)(2,1)} custom-call(s32[1]{0:T(128)} %bitcast.1.place_ref, bf16[512,1024]{1,0:T(8,128)(2,1)} %get-tuple-element.89.refs_0_, bf16[512,1792]{1,0:T(8,128)(2,1)} %copy-done), custom_call_target="tpu_custom_call" | custom-call | flops 1000 | bytes 1000 | tf_op jit(solution)/shard_map/make/pallas_call | solution.py:248
  101.9 3.1 %collective-permute-start.9 = (bf16[512,1024]{1,0:T(8,128)(2,1)}, bf16[512,1024]{1,0:T(8,128)(2,1)S(1)}, u32[]{:S(2)}, u32[]{:S(2)}) collective-permute-start(bf16[512,1024]{1,0:T(8,128)(2,1)} %make.20), channel_id=1, source_target_pairs={{0,4},{2,6},{4,0},{6,2},{8,12},{10,14},{12,8},{14,10},{1,5},{3,7},... | collective-permute-start | bytes 3145736 | tf_op jit(solution)/shard_map/r2_t/ppermute | solution.py:55
  105.1 9.1 %grad_pieces.4.refs_2_ = f32[512,1792]{1,0:T(8,128)} custom-call(s32[2]{0:T(128)S(1)} %pad_add_fusion.2.place_ref, bf16[14336,1792]{1,0:T(8,128)(2,1)} %basis_ref.9, bf16[512,1792]{1,0:T(8,128)(2,1)S(1)} %copy-done.1, bf16[512,1792]{1,0:T(8,128)(2,1)} %collective-permute-done.7.refs_1_, f32[512,1792]{1,0:T(8,128)} %grad_blocks.4.refs_2_), custom_call_target="tpu_custom_call" | custom-call | flops 1000 | bytes 1000 | tf_op jit(solution)/shard_map/grad_pieces/pallas_call | solution.py:143
  114.3 9.6 %grad_pieces.5.refs_2_ = f32[512,1792]{1,0:T(8,128)} custom-call(s32[2]{0:T(128)S(1)} %pad_add_fusion.1.place_ref, bf16[14336,1792]{1,0:T(8,128)(2,1)} %basis_ref.9, bf16[512,1792]{1,0:T(8,128)(2,1)} %collective-permute-done.3.refs_0_.refs_1_, bf16[512,1792]{1,0:T(8,128)(2,1)} %collective-permute-done.1.refs_1_, f32[512,1792]{1,0:T(8,128)} %grad_pieces.4.refs_2_), custom_call_target="tpu_custom_call" | custom-call | flops 1000 | bytes 1000 | tf_op jit(solution)/shard_map/grad_pieces/pallas_call | solution.py:143
  123.9 2.4 %make.21 = bf16[512,1024]{1,0:T(8,128)(2,1)} custom-call(s32[1]{0:T(128)} %bitcast.1.place_ref, f32[512,4096]{1,0:T(8,128)} %get-tuple-element.102.refs_0_.refs_2_.refs_6_.refs_1_, bf16[512,1280]{1,0:T(8,128)(2,1)} %collective-permute-done.6.refs_1_.refs_5_.refs_0_), custom_call_target="tpu_custom_call" | custom-call | flops 1000 | bytes 1000 | tf_op jit(solution)/shard_map/make/pallas_call | solution.py:248
  126.2 1.6 collective-permute-start.13
  127.9 2.4 %collective-permute-start.16 = (bf16[512,1280]{1,0:T(8,128)(2,1)}, bf16[512,1280]{1,0:T(8,128)(2,1)}, u32[]{:S(2)}, u32[]{:S(2)}) collective-permute-start(bf16[512,1280]{1,0:T(8,128)(2,1)} %collective-permute-done.6.refs_1_.refs_5_.refs_0_), channel_id=1, source_target_pairs={{0,2},{2,0},{12,14},{14,12},{1,3},{3,1},{13,15},{15,13},{16,18},{1... | collective-permute-start | bytes 3932168 | tf_op jit(solution)/shard_map/x3_h/ppermute | solution.py:55
  130.3 2.3 %make.22 = bf16[512,512]{1,0:T(8,128)(2,1)} custom-call(s32[1]{0:T(128)} %bitcast.1.place_ref, f32[512,4096]{1,0:T(8,128)} %get-tuple-element.102.refs_0_.refs_2_.refs_6_.refs_1_, bf16[512,1792]{1,0:T(8,128)(2,1)} %collective-permute-done.3.refs_0_.refs_1_, bf16[512,1024]{1,0:T(8,128)(2,1)} %collective-permute-done.5.refs_2_.refs_3_.refs_7_), custom_call_target="tpu_custom_call" | custom-call | flops 1000 | bytes 1000 | tf_op jit(solution)/shard_map/make/pallas_call | solution.py:248
  133.5 3.6 %collective-permute-done.10.refs_0_ = bf16[512,1792]{1,0:T(8,128)(2,1)} collective-permute-done((bf16[512,1792]{1,0:T(8,128)(2,1)}, bf16[512,1792]{1,0:T(8,128)(2,1)}, u32[]{:S(2)}, u32[]{:S(2)}) %collective-permute-start.10) | collective-permute-done | bytes 1835040 | tf_op jit(solution)/shard_map/x2/ppermute | solution.py:55
  137.1 8.5 %grad_blocks.5.refs_3_ = f32[512,1792]{1,0:T(8,128)} custom-call(s32[1]{0:T(128)} %bitcast.14.place_ref, bf16[512,1792]{1,0:T(8,128)(2,1)} %collective-permute-done.10.refs_0_, bf16[14336,1792]{1,0:T(8,128)(2,1)} %basis_ref.9, f32[512,1792]{1,0:T(8,128)} %grad_pieces.5.refs_2_), custom_call_target="tpu_custom_call" | custom-call | flops 1000 | bytes 1000 | tf_op jit(solution)/shard_map/grad_blocks/pallas_call | solution.py:183
  145.6 2.1 make.23.refs_1_
  147.7 1.4 collective-permute-start.12
  149.8 1.5 make.24
  152.1 2.0 make.25
  154.1 3.8 %collective-permute-done.12.refs_0_.refs_2_ = bf16[512,512]{1,0:T(8,128)(2,1)S(1)} collective-permute-done((bf16[512,512]{1,0:T(8,128)(2,1)S(1)}, bf16[512,512]{1,0:T(8,128)(2,1)S(1)}, u32[]{:S(2)}, u32[]{:S(2)}) %collective-permute-start.12) | collective-permute-done | bytes 524320 | tf_op jit(solution)/shard_map/all_in_0a/ppermute | solution.py:55
  157.9 2.1 make.26
  160.0 4.8 %collective-permute-start.14 = (bf16[512,512]{1,0:T(8,128)(2,1)}, bf16[512,512]{1,0:T(8,128)(2,1)}, u32[]{:S(2)}, u32[]{:S(2)}) collective-permute-start(bf16[512,512]{1,0:T(8,128)(2,1)} %make.26), channel_id=1, source_target_pairs={{0,4},{2,6},{4,0},{6,2},{8,12},{10,14},{12,8},{14,10},{1,5},{3,7},... | collective-permute-start | bytes 1572872 | tf_op jit(solution)/shard_map/all_in_1a/ppermute | solution.py:55
  165.4 2.4 %make.27.refs_1_ = bf16[512,512]{1,0:T(8,128)(2,1)} custom-call(s32[1]{0:T(128)} %bitcast.1.place_ref, bf16[512,1792]{1,0:T(8,128)(2,1)} %collective-permute-done.refs_1_.refs_0_, f32[512,4096]{1,0:T(8,128)} %get-tuple-element.102.refs_0_.refs_2_.refs_6_.refs_1_, bf16[512,1024]{1,0:T(8,128)(2,1)} %copy-done.2, ...), custom_call_target="tpu_custom_call" | custom-call | flops 1000 | bytes 1000 | tf_op jit(solution)/shard_map/make/pallas_call | solution.py:248
  167.8 3.5 %collective-permute-start.19 = (bf16[512,512]{1,0:T(8,128)(2,1)}, bf16[512,512]{1,0:T(8,128)(2,1)}, u32[]{:S(2)}, u32[]{:S(2)}) collective-permute-start(bf16[512,512]{1,0:T(8,128)(2,1)} %make.27.refs_1_), channel_id=1, source_target_pairs={{0,4},{2,6},{4,0},{6,2},{8,12},{10,14},{12,8},{14,10},{1,5},{3,7},... | collective-permute-start | bytes 1572872 | tf_op jit(solution)/shard_map/all_in_0b/ppermute | solution.py:55
  171.3 1.5 collective-permute-start.18
  174.7 2.5 %collective-permute-start.22 = (bf16[512,512]{1,0:T(8,128)(2,1)}, bf16[512,512]{1,0:T(8,128)(2,1)}, u32[]{:S(2)}, u32[]{:S(2)}) collective-permute-start(bf16[512,512]{1,0:T(8,128)(2,1)} %make.28.refs_0_), channel_id=1, source_target_pairs={{0,2},{2,0},{4,6},{6,4},{8,10},{10,8},{12,14},{14,12},{1,3},{3,1},... | collective-permute-start | bytes 1572872 | tf_op jit(solution)/shard_map/all_x_0a/ppermute | solution.py:55
  178.0 1.9 make.29.refs_1_
  180.0 8.8 %grad_pieces.6.refs_5_ = f32[512,1792]{1,0:T(8,128)} custom-call(s32[2]{0:T(128)S(1)} %pad_add_fusion.3.place_ref, bf16[14336,1792]{1,0:T(8,128)(2,1)} %basis_ref.9, bf16[512,1280]{1,0:T(8,128)(2,1)} %collective-permute-done.6.refs_1_.refs_5_.refs_0_, bf16[512,1024]{1,0:T(8,128)(2,1)S(1)} %copy-done.3, bf16[512,1792]{1,0:T(8,128)(2,1)S(1)} %copy-done.1, ...), custom_call_target="tpu_custom_call" | custom-call | flops 1000 | bytes 1000 | tf_op jit(solution)/shard_map/grad_pieces/pallas_call | solution.py:143
  191.4 10.2 %grad_pieces.7 = (f32[512,896]{1,0:T(8,128)}, f32[512,896]{1,0:T(8,128)}) custom-call(s32[2]{0:T(128)S(1)} %pad_add_fusion.4.place_ref, bf16[14336,1792]{1,0:T(8,128)(2,1)} %basis_ref.9, bf16[512,1280]{1,0:T(8,128)(2,1)} %collective-permute-done.16.refs_0_, bf16[512,512]{1,0:T(8,128)(2,1)} %collective-permute-done.20.refs_1_, ...), custom_call_target="tpu_custom_call" | custom-call | flops 1000 | bytes 1000 | tf_op jit(solution)/shard_map/grad_pieces/pallas_call | solution.py:143
  202.4 1.8 collective-permute-start.26
  205.8 1.9 add_convert_fusion.high_ref
  208.6 9.3 %tile_part.3.refs_3_ = f32[1792,4096]{1,0:T(8,128)} custom-call(s32[4]{0:T(128)S(1)} %pad_add_fusion.6.place_ref, bf16[512,896]{1,0:T(8,128)(2,1)S(1)} %add_convert_fusion.1.low_ref, bf16[512,896]{1,0:T(8,128)(2,1)S(1)} %add_convert_fusion.high_ref, bf16[512,512]{1,0:T(8,128)(2,1)} %make.28.refs_0_, bf16[512,512]{1,0:T(8,128)(2,1)} %make.29.refs_1_, ...), custom_call_target="tpu_custom_call" | custom-call | flops 1000 | bytes 1000 | tf_op jit(solution)/shard_map/tile_part/pallas_call | solution.py:280
  217.9 6.5 %tile_part.4.refs_1_ = f32[1792,4096]{1,0:T(8,128)} custom-call(s32[3]{0:T(128)S(1)} %pad_add_fusion.5.place_ref, bf16[512,896]{1,0:T(8,128)(2,1)S(1)} %add_convert_fusion.1.low_ref, bf16[512,896]{1,0:T(8,128)(2,1)S(1)} %add_convert_fusion.high_ref, bf16[512,512]{1,0:T(8,128)(2,1)S(1)} %make.30.refs_0_, ...), custom_call_target="tpu_custom_call", output_to_operand_aliasing={{}: (6, {})} | custom-call | flops 1000 | bytes 1000 | tf_op jit(solution)/shard_map/tile_part/pallas_call | solution.py:280
  224.4 3.1 %collective-permute-done.25.refs_0_ = bf16[512,512]{1,0:T(8,128)(2,1)S(1)} collective-permute-done((bf16[512,512]{1,0:T(8,128)(2,1)S(1)}, bf16[512,512]{1,0:T(8,128)(2,1)S(1)}, u32[]{:S(2)}, u32[]{:S(2)}) %collective-permute-start.25) | collective-permute-done | bytes 524320 | tf_op jit(solution)/shard_map/all_x_1b/ppermute | solution.py:55
  227.6 3.0 %tile_part.5 = f32[1792,4096]{1,0:T(8,128)} custom-call(s32[1]{0:T(128)} %bitcast.place_ref, bf16[512,896]{1,0:T(8,128)(2,1)S(1)} %add_convert_fusion.1.low_ref, bf16[512,896]{1,0:T(8,128)(2,1)S(1)} %add_convert_fusion.high_ref, bf16[512,512]{1,0:T(8,128)(2,1)S(1)} %collective-permute-done.25.refs_0_, ...), custom_call_target="tpu_custom_call", output_to_operand_aliasing={{}: (4, {})} | custom-call | flops 1000 | bytes 1000 | tf_op jit(solution)/shard_map/tile_part/pallas_call | solution.py:280
  (61 shorter events, 13.0 us)
Async XLA Ops:
  0.0 43.3 %collective-permute-start.2 = (bf16[512,1792]{1,0:T(8,128)(2,1)}, bf16[512,1792]{1,0:T(8,128)(2,1)}, u32[]{:S(2)}, u32[]{:S(2)}) collective-permute-start(bf16[512,1792]{1,0:T(8,128)(2,1)} %refs_0_), channel_id=1, source_target_pairs={{0,4},{2,6},{4,0},{6,2},{8,12},{10,14},{12,8},{14,10},{1,5},{3,7},... | collective-permute-start | bytes 5505032 | tf_op jit(solution)/shard_map/near/ppermute | solution.py:55
  3.0 42.0 %collective-permute-start.1 = (bf16[512,1792]{1,0:T(8,128)(2,1)}, bf16[512,1792]{1,0:T(8,128)(2,1)}, u32[]{:S(2)}, u32[]{:S(2)}) collective-permute-start(bf16[512,1792]{1,0:T(8,128)(2,1)} %refs_0_), channel_id=1, source_target_pairs={{4,8},{6,10},{8,4},{10,6},{5,9},{7,11},{9,5},{11,7},{20,24},{22,26... | collective-permute-start | bytes 5505032 | tf_op jit(solution)/shard_map/mid_own/ppermute | solution.py:55
  4.9 49.0 %collective-permute-start = (bf16[512,1792]{1,0:T(8,128)(2,1)}, bf16[512,1792]{1,0:T(8,128)(2,1)}, u32[]{:S(2)}, u32[]{:S(2)}) collective-permute-start(bf16[512,1792]{1,0:T(8,128)(2,1)} %refs_0_), channel_id=1, source_target_pairs={{0,2},{2,0},{4,6},{6,4},{8,10},{10,8},{12,14},{14,12},{1,3},{3,1},... | collective-permute-start | bytes 5505032 | tf_op jit(solution)/shard_map/own_x/ppermute | solution.py:55
  43.3 42.6 %collective-permute-start.4 = (bf16[512,1792]{1,0:T(8,128)(2,1)}, bf16[512,1792]{1,0:T(8,128)(2,1)S(1)}, u32[]{:S(2)}, u32[]{:S(2)}) collective-permute-start(bf16[512,1792]{1,0:T(8,128)(2,1)} %collective-permute-done.2.refs_0_.refs_1_), channel_id=1, source_target_pairs={{0,2},{2,0},{4,8},{6,10},{8,4},{10,6},{12,14},{14,12},{1,3},{3,1},... | collective-permute-start | bytes 5505032 | tf_op jit(solution)/shard_map/near_on/ppermute | solution.py:55
  47.8 43.3 %collective-permute-start.3 = (bf16[512,1792]{1,0:T(8,128)(2,1)}, bf16[512,1792]{1,0:T(8,128)(2,1)}, u32[]{:S(2)}, u32[]{:S(2)}) collective-permute-start(bf16[512,1792]{1,0:T(8,128)(2,1)} %make.16), channel_id=1, source_target_pairs={{0,4},{2,6},{4,0},{6,2},{8,12},{10,14},{12,8},{14,10},{1,5},{3,7},... | collective-permute-start | bytes 5505032 | tf_op jit(solution)/shard_map/r1/ppermute | solution.py:55
  51.9 53.2 %collective-permute-start.7 = (bf16[512,1792]{1,0:T(8,128)(2,1)}, bf16[512,1792]{1,0:T(8,128)(2,1)}, u32[]{:S(2)}, u32[]{:S(2)}) collective-permute-start(bf16[512,1792]{1,0:T(8,128)(2,1)} %collective-permute-done.1.refs_1_), channel_id=1, source_target_pairs={{4,6},{6,4},{8,10},{10,8},{5,7},{7,5},{9,11},{11,9},{20,22},{22,20... | collective-permute-start | bytes 5505032 | tf_op jit(solution)/shard_map/mid_own_x/ppermute | solution.py:55
  85.9 1.3 copy-start
  89.7 34.2 %collective-permute-start.6 = (bf16[512,1280]{1,0:T(8,128)(2,1)}, bf16[512,1280]{1,0:T(8,128)(2,1)}, u32[]{:S(2)}, u32[]{:S(2)}) collective-permute-start(bf16[512,1280]{1,0:T(8,128)(2,1)} %make.17), channel_id=1, source_target_pairs={{0,4},{2,6},{4,0},{6,2},{8,12},{10,14},{12,8},{14,10},{1,5},{3,7},... | collective-permute-start | bytes 3932168 | tf_op jit(solution)/shard_map/r2_h/ppermute | solution.py:55
  93.8 43.3 %collective-permute-start.10 = (bf16[512,1792]{1,0:T(8,128)(2,1)}, bf16[512,1792]{1,0:T(8,128)(2,1)}, u32[]{:S(2)}, u32[]{:S(2)}) collective-permute-start(bf16[512,1792]{1,0:T(8,128)(2,1)} %make.18), channel_id=1, source_target_pairs={{0,2},{2,0},{4,6},{6,4},{8,10},{10,8},{12,14},{14,12},{1,3},{3,1},... | collective-permute-start | bytes 5505032 | tf_op jit(solution)/shard_map/x2/ppermute | solution.py:55
  97.6 32.7 %collective-permute-start.5 = (bf16[512,1024]{1,0:T(8,128)(2,1)}, bf16[512,1024]{1,0:T(8,128)(2,1)}, u32[]{:S(2)}, u32[]{:S(2)}) collective-permute-start(bf16[512,1024]{1,0:T(8,128)(2,1)} %make.19), channel_id=1, source_target_pairs={{4,8},{6,10},{8,4},{10,6},{5,9},{7,11},{9,5},{11,7},{20,24},{22,26... | collective-permute-start | bytes 3145736 | tf_op jit(solution)/shard_map/mid_a/ppermute | solution.py:55
  99.4 5.7 %copy-start.1 = (bf16[512,1792]{1,0:T(8,128)(2,1)S(1)}, bf16[512,1792]{1,0:T(8,128)(2,1)}, u32[]{:S(2)}) copy-start(bf16[512,1792]{1,0:T(8,128)(2,1)} %copy-done) | copy-start | bytes 5505028
  101.9 43.6 %collective-permute-start.9 = (bf16[512,1024]{1,0:T(8,128)(2,1)}, bf16[512,1024]{1,0:T(8,128)(2,1)S(1)}, u32[]{:S(2)}, u32[]{:S(2)}) collective-permute-start(bf16[512,1024]{1,0:T(8,128)(2,1)} %make.20), channel_id=1, source_target_pairs={{0,4},{2,6},{4,0},{6,2},{8,12},{10,14},{12,8},{14,10},{1,5},{3,7},... | collective-permute-start | bytes 3145736 | tf_op jit(solution)/shard_map/r2_t/ppermute | solution.py:55
  126.2 23.6 %collective-permute-start.13 = (bf16[512,1024]{1,0:T(8,128)(2,1)}, bf16[512,1024]{1,0:T(8,128)(2,1)}, u32[]{:S(2)}, u32[]{:S(2)}) collective-permute-start(bf16[512,1024]{1,0:T(8,128)(2,1)} %make.21), channel_id=1, source_target_pairs={{4,8},{6,10},{8,4},{10,6},{5,9},{7,11},{9,5},{11,7},{20,24},{22,26... | collective-permute-start | bytes 3145736 | tf_op jit(solution)/shard_map/mid_b/ppermute | solution.py:55
  127.9 37.0 %collective-permute-start.16 = (bf16[512,1280]{1,0:T(8,128)(2,1)}, bf16[512,1280]{1,0:T(8,128)(2,1)}, u32[]{:S(2)}, u32[]{:S(2)}) collective-permute-start(bf16[512,1280]{1,0:T(8,128)(2,1)} %collective-permute-done.6.refs_1_.refs_5_.refs_0_), channel_id=1, source_target_pairs={{0,2},{2,0},{12,14},{14,12},{1,3},{3,1},{13,15},{15,13},{16,18},{1... | collective-permute-start | bytes 3932168 | tf_op jit(solution)/shard_map/x3_h/ppermute | solution.py:55
  132.6 13.0 %collective-permute-start.8 = (bf16[512,512]{1,0:T(8,128)(2,1)}, bf16[512,512]{1,0:T(8,128)(2,1)S(1)}, u32[]{:S(2)}, u32[]{:S(2)}) collective-permute-start(bf16[512,512]{1,0:T(8,128)(2,1)} %make.22), channel_id=1, source_target_pairs={{4,6},{6,4},{8,10},{10,8},{5,7},{7,5},{9,11},{11,9},{20,22},{22,20... | collective-permute-start | bytes 1572872 | tf_op jit(solution)/shard_map/sum_x_a/ppermute | solution.py:55
  145.6 2.1 copy-start.2
  147.7 3.7 %copy-start.4 = (bf16[512,512]{1,0:T(8,128)(2,1)}, bf16[512,512]{1,0:T(8,128)(2,1)S(1)}, u32[]{:S(2)}) copy-start(bf16[512,512]{1,0:T(8,128)(2,1)S(1)} %make.23.refs_1_) | copy-start | bytes 1572868
  147.7 10.2 %collective-permute-start.12 = (bf16[512,512]{1,0:T(8,128)(2,1)S(1)}, bf16[512,512]{1,0:T(8,128)(2,1)S(1)}, u32[]{:S(2)}, u32[]{:S(2)}) collective-permute-start(bf16[512,512]{1,0:T(8,128)(2,1)S(1)} %make.23.refs_1_), channel_id=1, source_target_pairs={{0,4},{2,6},{4,0},{6,2},{8,12},{10,14},{12,8},{14,10},{1,5},{3,7},... | collective-permute-start | bytes 1572872 | tf_op jit(solution)/shard_map/all_in_0a/ppermute | solution.py:55
  149.1 8.8 %collective-permute-start.11 = (bf16[512,512]{1,0:T(8,128)(2,1)S(1)}, bf16[512,512]{1,0:T(8,128)(2,1)S(1)}, u32[]{:S(2)}, u32[]{:S(2)}) collective-permute-start(bf16[512,512]{1,0:T(8,128)(2,1)S(1)} %make.23.refs_1_), channel_id=1, source_target_pairs={{4,8},{6,10},{8,4},{10,6},{5,9},{7,11},{9,5},{11,7},{20,24},{22,26... | collective-permute-start | bytes 1572872 | tf_op jit(solution)/shard_map/all_mid_a/ppermute | solution.py:55
  151.4 14.0 %collective-permute-start.15 = (bf16[512,512]{1,0:T(8,128)(2,1)S(1)}, bf16[512,512]{1,0:T(8,128)(2,1)S(1)}, u32[]{:S(2)}, u32[]{:S(2)}) collective-permute-start(bf16[512,512]{1,0:T(8,128)(2,1)S(1)} %make.24), channel_id=1, source_target_pairs={{4,6},{6,4},{8,10},{10,8},{5,7},{7,5},{9,11},{11,9},{20,22},{22,20... | collective-permute-start | bytes 1572872 | tf_op jit(solution)/shard_map/sum_x_b/ppermute | solution.py:55
  157.9 7.4 %copy-start.6 = (bf16[512,512]{1,0:T(8,128)(2,1)}, bf16[512,512]{1,0:T(8,128)(2,1)S(1)}, u32[]{:S(2)}) copy-start(bf16[512,512]{1,0:T(8,128)(2,1)S(1)} %collective-permute-done.11.refs_1_) | copy-start | bytes 1572868
  160.0 18.0 %collective-permute-start.14 = (bf16[512,512]{1,0:T(8,128)(2,1)}, bf16[512,512]{1,0:T(8,128)(2,1)}, u32[]{:S(2)}, u32[]{:S(2)}) collective-permute-start(bf16[512,512]{1,0:T(8,128)(2,1)} %make.26), channel_id=1, source_target_pairs={{0,4},{2,6},{4,0},{6,2},{8,12},{10,14},{12,8},{14,10},{1,5},{3,7},... | collective-permute-start | bytes 1572872 | tf_op jit(solution)/shard_map/all_in_1a/ppermute | solution.py:55
  164.9 23.9 %collective-permute-start.20 = (bf16[512,512]{1,0:T(8,128)(2,1)}, bf16[512,512]{1,0:T(8,128)(2,1)}, u32[]{:S(2)}, u32[]{:S(2)}) collective-permute-start(bf16[512,512]{1,0:T(8,128)(2,1)} %make.25), channel_id=1, source_target_pairs={{0,2},{2,0},{4,6},{6,4},{8,10},{10,8},{12,14},{14,12},{1,3},{3,1},... | collective-permute-start | bytes 1572872 | tf_op jit(solution)/shard_map/x3_t/ppermute | solution.py:55
  167.8 12.2 %copy-start.3 = (bf16[512,1024]{1,0:T(8,128)(2,1)S(1)}, bf16[512,1024]{1,0:T(8,128)(2,1)}, u32[]{:S(2)}) copy-start(bf16[512,1024]{1,0:T(8,128)(2,1)} %copy-done.2) | copy-start | bytes 3145732
  167.8 21.0 %collective-permute-start.19 = (bf16[512,512]{1,0:T(8,128)(2,1)}, bf16[512,512]{1,0:T(8,128)(2,1)}, u32[]{:S(2)}, u32[]{:S(2)}) collective-permute-start(bf16[512,512]{1,0:T(8,128)(2,1)} %make.27.refs_1_), channel_id=1, source_target_pairs={{0,4},{2,6},{4,0},{6,2},{8,12},{10,14},{12,8},{14,10},{1,5},{3,7},... | collective-permute-start | bytes 1572872 | tf_op jit(solution)/shard_map/all_in_0b/ppermute | solution.py:55
  171.3 17.5 %collective-permute-start.18 = (bf16[512,512]{1,0:T(8,128)(2,1)}, bf16[512,512]{1,0:T(8,128)(2,1)}, u32[]{:S(2)}, u32[]{:S(2)}) collective-permute-start(bf16[512,512]{1,0:T(8,128)(2,1)} %make.27.refs_1_), channel_id=1, source_target_pairs={{4,8},{6,10},{8,4},{10,6},{5,9},{7,11},{9,5},{11,7},{20,24},{22,26... | collective-permute-start | bytes 1572872 | tf_op jit(solution)/shard_map/all_mid_b/ppermute | solution.py:55
  172.8 1.0 copy-start.5
  173.9 4.1 %copy-start.7 = (bf16[512,512]{1,0:T(8,128)(2,1)S(1)}, bf16[512,512]{1,0:T(8,128)(2,1)}, u32[]{:S(2)}) copy-start(bf16[512,512]{1,0:T(8,128)(2,1)} %copy-done.6) | copy-start | bytes 1572868
  174.7 16.7 %collective-permute-start.22 = (bf16[512,512]{1,0:T(8,128)(2,1)}, bf16[512,512]{1,0:T(8,128)(2,1)}, u32[]{:S(2)}, u32[]{:S(2)}) collective-permute-start(bf16[512,512]{1,0:T(8,128)(2,1)} %make.28.refs_0_), channel_id=1, source_target_pairs={{0,2},{2,0},{4,6},{6,4},{8,10},{10,8},{12,14},{14,12},{1,3},{3,1},... | collective-permute-start | bytes 1572872 | tf_op jit(solution)/shard_map/all_x_0a/ppermute | solution.py:55
  179.9 21.7 %collective-permute-start.17 = (bf16[512,512]{1,0:T(8,128)(2,1)}, bf16[512,512]{1,0:T(8,128)(2,1)}, u32[]{:S(2)}, u32[]{:S(2)}) collective-permute-start(bf16[512,512]{1,0:T(8,128)(2,1)} %make.29.refs_1_), channel_id=1, source_target_pairs={{0,2},{2,0},{4,6},{6,4},{8,10},{10,8},{12,14},{14,12},{1,3},{3,1},... | collective-permute-start | bytes 1572872 | tf_op jit(solution)/shard_map/all_x_1a/ppermute | solution.py:55
  188.8 12.9 %collective-permute-start.21 = (bf16[512,512]{1,0:T(8,128)(2,1)}, bf16[512,512]{1,0:T(8,128)(2,1)S(1)}, u32[]{:S(2)}, u32[]{:S(2)}) collective-permute-start(bf16[512,512]{1,0:T(8,128)(2,1)} %collective-permute-done.18.refs_1_), channel_id=1, source_target_pairs={{4,0},{6,2},{8,12},{10,14},{5,1},{7,3},{9,13},{11,15},{20,16},{22,... | collective-permute-start | bytes 1572872 | tf_op jit(solution)/shard_map/all_in_1b/ppermute | solution.py:55
  201.7 4.1 %collective-permute-start.24 = (f32[512,896]{1,0:T(8,128)}, f32[512,896]{1,0:T(8,128)S(1)}, u32[]{:S(2)}, u32[]{:S(2)}) collective-permute-start(f32[512,896]{1,0:T(8,128)} %get-tuple-element.134), channel_id=1, source_target_pairs={{0,1},{1,0},{2,3},{3,2},{4,5},{5,4},{6,7},{7,6},{8,9},{9,8},{10,11... | collective-permute-start | bytes 5505032 | tf_op jit(solution)/shard_map/core_high/ppermute | solution.py:55
  201.7 6.6 %collective-permute-start.23 = (f32[512,896]{1,0:T(8,128)}, f32[512,896]{1,0:T(8,128)S(1)}, u32[]{:S(2)}, u32[]{:S(2)}) collective-permute-start(f32[512,896]{1,0:T(8,128)} %get-tuple-element.132), channel_id=1, source_target_pairs={{0,1},{1,0},{2,3},{3,2},{4,5},{5,4},{6,7},{7,6},{8,9},{9,8},{10,11... | collective-permute-start | bytes 5505032 | tf_op jit(solution)/shard_map/core_low/ppermute | solution.py:55
  202.4 15.5 %collective-permute-start.26 = (bf16[512,512]{1,0:T(8,128)(2,1)S(1)}, bf16[512,512]{1,0:T(8,128)(2,1)S(1)}, u32[]{:S(2)}, u32[]{:S(2)}) collective-permute-start(bf16[512,512]{1,0:T(8,128)(2,1)S(1)} %make.30.refs_0_), channel_id=1, source_target_pairs={{0,2},{2,0},{4,6},{6,4},{8,10},{10,8},{12,14},{14,12},{1,3},{3,1},... | collective-permute-start | bytes 1572872 | tf_op jit(solution)/shard_map/all_x_0b/ppermute | solution.py:55
  205.5 2.8 %copy-start.8 = (f32[512,896]{1,0:T(8,128)S(1)}, f32[512,896]{1,0:T(8,128)}, u32[]{:S(2)}) copy-start(f32[512,896]{1,0:T(8,128)} %get-tuple-element.132) | copy-start | bytes 5505028
  205.5 22.1 %collective-permute-start.25 = (bf16[512,512]{1,0:T(8,128)(2,1)S(1)}, bf16[512,512]{1,0:T(8,128)(2,1)S(1)}, u32[]{:S(2)}, u32[]{:S(2)}) collective-permute-start(bf16[512,512]{1,0:T(8,128)(2,1)S(1)} %make.31.refs_1_), channel_id=1, source_target_pairs={{0,2},{2,0},{4,6},{6,4},{8,10},{10,8},{12,14},{14,12},{1,3},{3,1},... | collective-permute-start | bytes 1572872 | tf_op jit(solution)/shard_map/all_x_1b/ppermute | solution.py:55

commit v5 on v4

--- a/solution.py
+++ b/solution.py
@@ -50,7 +50,12 @@
 Z_IN = pairs(lambda z, x: None if is_end(z) else (z ^ 1, x))
 
 
-def send(name, value, way, axis="out"):
+def send(name, value, way, axis="out", full=False):
+    if full:
+        axis = ("groups", "out")
+        idle = [n for n in range(8) if n not in [source for source, _ in way]]
+        way = [(g * 8 + a, g * 8 + b) for g in range(2) for a, b in way]
+        way += [(g * 8 + n, (1 - g) * 8 + n) for g in range(2) for n in idle]
     with jax.named_scope(name):
         return lax.ppermute(value, axis, way)
 
@@ -335,7 +340,7 @@
 
     a = send("near", grads, Z_NEAR)
     x0 = send("own_x", grads, X_ALL)
-    b1 = send("mid_own", grads, Z_MID)
+    b1 = send("mid_own", grads, Z_MID, full=True)
     order = [(1, 1, 0), (1, 0, 0), (0, 1, 0), (0, 0, 0), (1, 1, 1), (1, 0, 1), (0, 1, 1), (0, 0, 1)]
     sent = [0, 1, 2, 3, 4, 5, 6], [8, 9, 10, 11, 7], [12, 13, 14, 15]
     wide, n1, n2, n3 = act_parts([column(*e) for e in order], sent, unit, acts, basis_in)
@@ -346,7 +351,7 @@
     b1, total = barrier(b1, total)
     y1 = put(one(n1, 0, 7), one(b1, 0, 7), 7)
     r1 = send("r1", y1, Z_NEAR)
-    xb1 = send("mid_own_x", after(b1, y1), X_MID)
+    xb1 = send("mid_own_x", after(b1, y1), X_MID, full=True)
     total = blocks([a, x0], [z_block(near, x), z_block(z, 1 - x)], total)
 
     b2, total = barrier(c1, total)
@@ -356,7 +361,7 @@
     y3 = put(one(r1, 0, 7), one(b2, 0, 7), 7)
     x2 = send("x2", y3, X_ALL)
     y4 = put(None, [[(after(wide, y3), 0, 4), (r1, 0, 4)]], 4)
-    m_a = send("mid_a", y4, Z_MID)
+    m_a = send("mid_a", y4, Z_MID, full=True)
     y5 = put(one(after(n3, y4), 0, 4), one(b2, 5, 2), 4)
     r2_t = send("r2_t", y5, Z_NEAR)
     xb1, total = barrier(xb1, total)
@@ -365,8 +370,8 @@
 
     r2_h, total = barrier(r2_h, total)
     y6 = put(None, [[(wide, 8, 4), (r2_h, 0, 4)]], 4)
-    m_b = send("mid_b", y6, Z_MID)
-    x3_h = send("x3_h", after(r2_h, y6), X_END)
+    m_b = send("mid_b", y6, Z_MID, full=True)
+    x3_h = send("x3_h", after(r2_h, y6), X_END, full=True)
     m_a, y6, total = barrier(m_a, y6, total)
     y7 = put(None, [[(wide, 4, 2), (r1, 4, 2), (m_a, 0, 2)]], 2)
     xm_a = send("sum_x_a", y7, X_MID)
@@ -435,7 +440,7 @@
 
 def solution(mesh):
     return jax.shard_map(
-        grid_of_eight if mesh.shape["out"] == 8 and mesh.shape["inp"] == 2 else plain,
+        grid_of_eight if tuple(mesh.shape[n] for n in ("groups", "out", "inp")) == (2, 8, 2) else plain,
         mesh=mesh,
         in_specs=(
             P("groups", ("inp", "out")),

time: 232 us -> 232 us (level)
  starting transfers between devices: 46.2 us -> 39.3 us
  waiting for transfers between devices: 44.8 us -> 51.7 us
    ppermute x27, starting transfers between devices: 46.2 us -> 39.3 us  [send(): return lax.ppermute(value, axis, way)]
    ppermute x27, waiting for transfers between devices: 44.8 us -> 51.7 us  [send(): return lax.ppermute(value, axis, way)]
where the time goes in v5:
time: 232 us; the launch traced here: 230 us
  Pallas kernels  134 us (58%)
  waiting for transfers between devices  51.7 us (22%)
  starting transfers between devices  39.3 us (17%)
  other arithmetic  2.58 us (1%)
  local copies, waits for them, and re-layouts  2.47 us (1%)
    ppermute x27, waiting for transfers between devices, send(): return lax.ppermute(value, axis, way)  51.7 us
    ppermute x27, starting transfers between devices, send(): return lax.ppermute(value, axis, way)  39.3 us
    pallas_call x4, Pallas kernels, grad_pieces(): pl.pallas_call(functools.partial(grad_kernel, *cuts, 2 if halves else 1),...  37.8 us
    pallas_call x16, Pallas kernels, make(): pl.pallas_call(functools.partial(make_kernel, plans), grid_spec=pltpu.Pre...  32.9 us
    pallas_call x3, Pallas kernels, grad_blocks(): pl.pallas_call(functools.partial(grad_sum_kernel, total is not None), gri...  31 us
    pallas_call x3, Pallas kernels, tile_part(): pl.pallas_call(functools.partial(tile_kernel, tokens, count), grid_spec=p...  18.8 us
    pallas_call x1, Pallas kernels, act_parts(): pl.pallas_call(functools.partial(act_kernel, spans), grid_spec=pltpu.Pref...  13.6 us
  transfers between devices with their start and end apart: 27, of which 7 were waited for; matrix products, arithmetic and copies ran while one was open for 1% of the time, Pallas kernels for 57%

profile of v5, /device:TPU:0, one launch (start us, length us, event | category | flops | bytes accessed | tf_op | source)
XLA Modules:
  0.0 230.3 jit_solution(5126449957757912813)
XLA Ops:
  0.0 3.0 %collective-permute-start.2 = (bf16[512,1792]{1,0:T(8,128)(2,1)}, bf16[512,1792]{1,0:T(8,128)(2,1)}, u32[]{:S(2)}, u32[]{:S(2)}) collective-permute-start(bf16[512,1792]{1,0:T(8,128)(2,1)} %refs_0_), channel_id=1, source_target_pairs={{0,4},{2,6},{4,0},{6,2},{8,12},{10,14},{12,8},{14,10},{1,5},{3,7},... | collective-permute-start | bytes 5505032 | tf_op jit(solution)/shard_map/near/ppermute | solution.py:60
  3.0 1.5 collective-permute-start.1
  4.5 1.5 collective-permute-start
  6.1 13.6 %act_parts.1 = (f32[512,4096]{1,0:T(8,128)}, bf16[512,1792]{1,0:T(8,128)(2,1)}, bf16[512,1280]{1,0:T(8,128)(2,1)}, bf16[512,1024]{1,0:T(8,128)(2,1)}) custom-call(s32[8]{0:T(128)S(1)} %stack.92.place_ref, bf16[512,1024]{1,0:T(8,128)(2,1)} %acts_ref.1, bf16[1024,4096]{1,0:T(8,128)(2,1)} %basis_ref.5), custom_call_target="tpu_custom_call" | custom-call | flops 1000 | bytes 1000 | tf_op jit(solution)/shard_map/act_parts/pallas_call | solution.py:91
  19.7 7.9 %grad_blocks.3.refs_4_ = f32[512,1792]{1,0:T(8,128)} custom-call(s32[1]{0:T(128)} %bitcast.9.place_ref, bf16[512,1792]{1,0:T(8,128)(2,1)} %refs_0_, bf16[14336,1792]{1,0:T(8,128)(2,1)} %basis_ref.9), custom_call_target="tpu_custom_call" | custom-call | flops 1000 | bytes 1000 | tf_op jit(solution)/shard_map/grad_blocks/pallas_call | solution.py:188
  27.6 15.7 %collective-permute-done.2.refs_0_.refs_1_ = bf16[512,1792]{1,0:T(8,128)(2,1)} collective-permute-done((bf16[512,1792]{1,0:T(8,128)(2,1)}, bf16[512,1792]{1,0:T(8,128)(2,1)}, u32[]{:S(2)}, u32[]{:S(2)}) %collective-permute-start.2) | collective-permute-done | bytes 1835040 | tf_op jit(solution)/shard_map/near/ppermute | solution.py:60
  43.3 1.7 collective-permute-start.4
  45.0 2.8 %make.16 = bf16[512,1792]{1,0:T(8,128)(2,1)} custom-call(s32[1]{0:T(128)} %bitcast.1.place_ref, bf16[512,1792]{1,0:T(8,128)(2,1)} %get-tuple-element.72.refs_0_, bf16[512,1792]{1,0:T(8,128)(2,1)} %collective-permute-done.1.refs_1_), custom_call_target="tpu_custom_call" | custom-call | flops 1000 | bytes 1000 | tf_op jit(solution)/shard_map/make/pallas_call | solution.py:253
  47.8 1.7 collective-permute-start.3
  49.4 1.5 collective-permute-start.7
  51.0 14.6 %grad_blocks.4.refs_2_ = f32[512,1792]{1,0:T(8,128)} custom-call(s32[2]{0:T(128)S(1)} %pad_add_fusion.place_ref, bf16[512,1792]{1,0:T(8,128)(2,1)} %collective-permute-done.2.refs_0_.refs_1_, bf16[512,1792]{1,0:T(8,128)(2,1)} %collective-permute-done.refs_1_.refs_0_, bf16[14336,1792]{1,0:T(8,128)(2,1)} %basis_ref.9, bf16[14336,1792]{1,0:T(8,128)(2,1)} %basis_ref.9, ...), custom_call_target="tpu_custom_call" | custom-call | flops 1000 | bytes 1000 | tf_op jit(solution)/shard_map/grad_blocks/pallas_call | solution.py:188
  65.6 19.7 %collective-permute-done.4.refs_1_.refs_0_.refs_2_ = bf16[512,1792]{1,0:T(8,128)(2,1)S(1)} collective-permute-done((bf16[512,1792]{1,0:T(8,128)(2,1)}, bf16[512,1792]{1,0:T(8,128)(2,1)S(1)}, u32[]{:S(2)}, u32[]{:S(2)}) %collective-permute-start.4) | collective-permute-done | bytes 1835040 | tf_op jit(solution)/shard_map/near_on/ppermute | solution.py:60
  85.3 1.3 copy-done
  86.6 2.4 %make.17 = bf16[512,1280]{1,0:T(8,128)(2,1)} custom-call(s32[1]{0:T(128)} %bitcast.1.place_ref, bf16[512,1280]{1,0:T(8,128)(2,1)} %get-tuple-element.77.refs_0_, bf16[512,1792]{1,0:T(8,128)(2,1)} %copy-done), custom_call_target="tpu_custom_call" | custom-call | flops 1000 | bytes 1000 | tf_op jit(solution)/shard_map/make/pallas_call | solution.py:253
  89.9 2.8 %make.18 = bf16[512,1792]{1,0:T(8,128)(2,1)} custom-call(s32[1]{0:T(128)} %bitcast.1.place_ref, bf16[512,1792]{1,0:T(8,128)(2,1)} %collective-permute-done.3.refs_0_.refs_1_, bf16[512,1792]{1,0:T(8,128)(2,1)} %copy-done), custom_call_target="tpu_custom_call" | custom-call | flops 1000 | bytes 1000 | tf_op jit(solution)/shard_map/make/pallas_call | solution.py:253
  92.7 1.5 collective-permute-start.10
  94.1 2.3 %make.19 = bf16[512,1024]{1,0:T(8,128)(2,1)} custom-call(s32[1]{0:T(128)} %bitcast.1.place_ref, f32[512,4096]{1,0:T(8,128)} %get-tuple-element.102.refs_0_.refs_2_.refs_6_.refs_1_, bf16[512,1792]{1,0:T(8,128)(2,1)} %collective-permute-done.3.refs_0_.refs_1_), custom_call_target="tpu_custom_call" | custom-call | flops 1000 | bytes 1000 | tf_op jit(solution)/shard_map/make/pallas_call | solution.py:253
  96.5 1.5 collective-permute-start.5
  98.1 2.6 %make.20 = bf16[512,1024]{1,0:T(8,128)(2,1)} custom-call(s32[1]{0:T(128)} %bitcast.1.place_ref, bf16[512,1024]{1,0:T(8,128)(2,1)} %get-tuple-element.89.refs_0_, bf16[512,1792]{1,0:T(8,128)(2,1)} %copy-done), custom_call_target="tpu_custom_call" | custom-call | flops 1000 | bytes 1000 | tf_op jit(solution)/shard_map/make/pallas_call | solution.py:253
  100.6 2.1 collective-permute-start.9
  102.8 9.1 %grad_pieces.4.refs_2_ = f32[512,1792]{1,0:T(8,128)} custom-call(s32[2]{0:T(128)S(1)} %pad_add_fusion.2.place_ref, bf16[14336,1792]{1,0:T(8,128)(2,1)} %basis_ref.9, bf16[512,1792]{1,0:T(8,128)(2,1)S(1)} %copy-done.1, bf16[512,1792]{1,0:T(8,128)(2,1)} %collective-permute-done.7.refs_1_, f32[512,1792]{1,0:T(8,128)} %grad_blocks.4.refs_2_), custom_call_target="tpu_custom_call" | custom-call | flops 1000 | bytes 1000 | tf_op jit(solution)/shard_map/grad_pieces/pallas_call | solution.py:148
  111.9 9.6 %grad_pieces.5.refs_2_ = f32[512,1792]{1,0:T(8,128)} custom-call(s32[2]{0:T(128)S(1)} %pad_add_fusion.1.place_ref, bf16[14336,1792]{1,0:T(8,128)(2,1)} %basis_ref.9, bf16[512,1792]{1,0:T(8,128)(2,1)} %collective-permute-done.3.refs_0_.refs_1_, bf16[512,1792]{1,0:T(8,128)(2,1)} %collective-permute-done.1.refs_1_, f32[512,1792]{1,0:T(8,128)} %grad_pieces.4.refs_2_), custom_call_target="tpu_custom_call" | custom-call | flops 1000 | bytes 1000 | tf_op jit(solution)/shard_map/grad_pieces/pallas_call | solution.py:148
  121.5 2.4 %make.21 = bf16[512,1024]{1,0:T(8,128)(2,1)} custom-call(s32[1]{0:T(128)} %bitcast.1.place_ref, f32[512,4096]{1,0:T(8,128)} %get-tuple-element.102.refs_0_.refs_2_.refs_6_.refs_1_, bf16[512,1280]{1,0:T(8,128)(2,1)} %collective-permute-done.6.refs_1_.refs_5_.refs_0_), custom_call_target="tpu_custom_call" | custom-call | flops 1000 | bytes 1000 | tf_op jit(solution)/shard_map/make/pallas_call | solution.py:253
  123.9 1.5 collective-permute-start.13
  125.9 2.3 %make.22 = bf16[512,512]{1,0:T(8,128)(2,1)} custom-call(s32[1]{0:T(128)} %bitcast.1.place_ref, f32[512,4096]{1,0:T(8,128)} %get-tuple-element.102.refs_0_.refs_2_.refs_6_.refs_1_, bf16[512,1792]{1,0:T(8,128)(2,1)} %collective-permute-done.3.refs_0_.refs_1_, bf16[512,1024]{1,0:T(8,128)(2,1)} %collective-permute-done.5.refs_2_.refs_3_.refs_7_), custom_call_target="tpu_custom_call" | custom-call | flops 1000 | bytes 1000 | tf_op jit(solution)/shard_map/make/pallas_call | solution.py:253
  129.1 6.8 %collective-permute-done.10.refs_0_ = bf16[512,1792]{1,0:T(8,128)(2,1)} collective-permute-done((bf16[512,1792]{1,0:T(8,128)(2,1)}, bf16[512,1792]{1,0:T(8,128)(2,1)}, u32[]{:S(2)}, u32[]{:S(2)}) %collective-permute-start.10) | collective-permute-done | bytes 1835040 | tf_op jit(solution)/shard_map/x2/ppermute | solution.py:60
  135.9 8.5 %grad_blocks.5.refs_3_ = f32[512,1792]{1,0:T(8,128)} custom-call(s32[1]{0:T(128)} %bitcast.14.place_ref, bf16[512,1792]{1,0:T(8,128)(2,1)} %collective-permute-done.10.refs_0_, bf16[14336,1792]{1,0:T(8,128)(2,1)} %basis_ref.9, f32[512,1792]{1,0:T(8,128)} %grad_pieces.5.refs_2_), custom_call_target="tpu_custom_call" | custom-call | flops 1000 | bytes 1000 | tf_op jit(solution)/shard_map/grad_blocks/pallas_call | solution.py:188
  144.4 2.1 make.23.refs_1_
  146.6 1.3 collective-permute-start.12
  148.6 1.5 make.24
  150.8 2.0 make.25
  152.8 4.9 %collective-permute-done.12.refs_0_.refs_2_ = bf16[512,512]{1,0:T(8,128)(2,1)S(1)} collective-permute-done((bf16[512,512]{1,0:T(8,128)(2,1)S(1)}, bf16[512,512]{1,0:T(8,128)(2,1)S(1)}, u32[]{:S(2)}, u32[]{:S(2)}) %collective-permute-start.12) | collective-permute-done | bytes 524320 | tf_op jit(solution)/shard_map/all_in_0a/ppermute | solution.py:60
  157.8 2.1 make.26
  159.9 3.6 %collective-permute-start.14 = (bf16[512,512]{1,0:T(8,128)(2,1)}, bf16[512,512]{1,0:T(8,128)(2,1)}, u32[]{:S(2)}, u32[]{:S(2)}) collective-permute-start(bf16[512,512]{1,0:T(8,128)(2,1)} %make.26), channel_id=1, source_target_pairs={{0,4},{2,6},{4,0},{6,2},{8,12},{10,14},{12,8},{14,10},{1,5},{3,7},... | collective-permute-start | bytes 1572872 | tf_op jit(solution)/shard_map/all_in_1a/ppermute | solution.py:60
  164.7 2.4 %make.27.refs_1_ = bf16[512,512]{1,0:T(8,128)(2,1)} custom-call(s32[1]{0:T(128)} %bitcast.1.place_ref, bf16[512,1792]{1,0:T(8,128)(2,1)} %collective-permute-done.refs_1_.refs_0_, f32[512,4096]{1,0:T(8,128)} %get-tuple-element.102.refs_0_.refs_2_.refs_6_.refs_1_, bf16[512,1024]{1,0:T(8,128)(2,1)} %copy-done.2, ...), custom_call_target="tpu_custom_call" | custom-call | flops 1000 | bytes 1000 | tf_op jit(solution)/shard_map/make/pallas_call | solution.py:253
  167.1 3.3 %collective-permute-start.19 = (bf16[512,512]{1,0:T(8,128)(2,1)}, bf16[512,512]{1,0:T(8,128)(2,1)}, u32[]{:S(2)}, u32[]{:S(2)}) collective-permute-start(bf16[512,512]{1,0:T(8,128)(2,1)} %make.27.refs_1_), channel_id=1, source_target_pairs={{0,4},{2,6},{4,0},{6,2},{8,12},{10,14},{12,8},{14,10},{1,5},{3,7},... | collective-permute-start | bytes 1572872 | tf_op jit(solution)/shard_map/all_in_0b/ppermute | solution.py:60
  170.4 1.5 collective-permute-start.18
  173.9 2.2 collective-permute-start.22
  176.7 1.9 make.29.refs_1_
  179.8 8.8 %grad_pieces.6.refs_5_ = f32[512,1792]{1,0:T(8,128)} custom-call(s32[2]{0:T(128)S(1)} %pad_add_fusion.3.place_ref, bf16[14336,1792]{1,0:T(8,128)(2,1)} %basis_ref.9, bf16[512,1280]{1,0:T(8,128)(2,1)} %collective-permute-done.6.refs_1_.refs_5_.refs_0_, bf16[512,1024]{1,0:T(8,128)(2,1)S(1)} %copy-done.3, bf16[512,1792]{1,0:T(8,128)(2,1)S(1)} %copy-done.1, ...), custom_call_target="tpu_custom_call" | custom-call | flops 1000 | bytes 1000 | tf_op jit(solution)/shard_map/grad_pieces/pallas_call | solution.py:148
  191.2 10.2 %grad_pieces.7 = (f32[512,896]{1,0:T(8,128)}, f32[512,896]{1,0:T(8,128)}) custom-call(s32[2]{0:T(128)S(1)} %pad_add_fusion.4.place_ref, bf16[14336,1792]{1,0:T(8,128)(2,1)} %basis_ref.9, bf16[512,1280]{1,0:T(8,128)(2,1)} %collective-permute-done.16.refs_0_, bf16[512,512]{1,0:T(8,128)(2,1)} %collective-permute-done.20.refs_1_, ...), custom_call_target="tpu_custom_call" | custom-call | flops 1000 | bytes 1000 | tf_op jit(solution)/shard_map/grad_pieces/pallas_call | solution.py:148
  202.9 1.3 make.31.refs_1_
  204.2 1.4 collective-permute-start.25
  205.6 1.8 add_convert_fusion.high_ref
  208.4 9.3 %tile_part.3.refs_3_ = f32[1792,4096]{1,0:T(8,128)} custom-call(s32[4]{0:T(128)S(1)} %pad_add_fusion.6.place_ref, bf16[512,896]{1,0:T(8,128)(2,1)S(1)} %add_convert_fusion.1.low_ref, bf16[512,896]{1,0:T(8,128)(2,1)S(1)} %add_convert_fusion.high_ref, bf16[512,512]{1,0:T(8,128)(2,1)} %make.28.refs_0_, bf16[512,512]{1,0:T(8,128)(2,1)} %make.29.refs_1_, ...), custom_call_target="tpu_custom_call" | custom-call | flops 1000 | bytes 1000 | tf_op jit(solution)/shard_map/tile_part/pallas_call | solution.py:285
  217.7 6.6 %tile_part.4.refs_1_ = f32[1792,4096]{1,0:T(8,128)} custom-call(s32[3]{0:T(128)S(1)} %pad_add_fusion.5.place_ref, bf16[512,896]{1,0:T(8,128)(2,1)S(1)} %add_convert_fusion.1.low_ref, bf16[512,896]{1,0:T(8,128)(2,1)S(1)} %add_convert_fusion.high_ref, bf16[512,512]{1,0:T(8,128)(2,1)S(1)} %make.30.refs_0_, ...), custom_call_target="tpu_custom_call", output_to_operand_aliasing={{}: (6, {})} | custom-call | flops 1000 | bytes 1000 | tf_op jit(solution)/shard_map/tile_part/pallas_call | solution.py:285
  224.2 3.1 %collective-permute-done.25.refs_0_ = bf16[512,512]{1,0:T(8,128)(2,1)S(1)} collective-permute-done((bf16[512,512]{1,0:T(8,128)(2,1)S(1)}, bf16[512,512]{1,0:T(8,128)(2,1)S(1)}, u32[]{:S(2)}, u32[]{:S(2)}) %collective-permute-start.25) | collective-permute-done | bytes 524320 | tf_op jit(solution)/shard_map/all_x_1b/ppermute | solution.py:60
  227.3 3.0 %tile_part.5 = f32[1792,4096]{1,0:T(8,128)} custom-call(s32[1]{0:T(128)} %bitcast.place_ref, bf16[512,896]{1,0:T(8,128)(2,1)S(1)} %add_convert_fusion.1.low_ref, bf16[512,896]{1,0:T(8,128)(2,1)S(1)} %add_convert_fusion.high_ref, bf16[512,512]{1,0:T(8,128)(2,1)S(1)} %collective-permute-done.25.refs_0_, ...), custom_call_target="tpu_custom_call", output_to_operand_aliasing={{}: (4, {})} | custom-call | flops 1000 | bytes 1000 | tf_op jit(solution)/shard_map/tile_part/pallas_call | solution.py:285
  (61 shorter events, 14.0 us)
Async XLA Ops:
  0.0 43.3 %collective-permute-start.2 = (bf16[512,1792]{1,0:T(8,128)(2,1)}, bf16[512,1792]{1,0:T(8,128)(2,1)}, u32[]{:S(2)}, u32[]{:S(2)}) collective-permute-start(bf16[512,1792]{1,0:T(8,128)(2,1)} %refs_0_), channel_id=1, source_target_pairs={{0,4},{2,6},{4,0},{6,2},{8,12},{10,14},{12,8},{14,10},{1,5},{3,7},... | collective-permute-start | bytes 5505032 | tf_op jit(solution)/shard_map/near/ppermute | solution.py:60
  3.0 42.0 %collective-permute-start.1 = (bf16[512,1792]{1,0:T(8,128)(2,1)}, bf16[512,1792]{1,0:T(8,128)(2,1)}, u32[]{:S(2)}, u32[]{:S(2)}) collective-permute-start(bf16[512,1792]{1,0:T(8,128)(2,1)} %refs_0_), channel_id=1, source_target_pairs={{4,8},{6,10},{8,4},{10,6},{20,24},{22,26},{24,20},{26,22},{0,16},{... | collective-permute-start | bytes 5505032 | tf_op jit(solution)/shard_map/mid_own/ppermute | solution.py:60
  4.5 46.5 %collective-permute-start = (bf16[512,1792]{1,0:T(8,128)(2,1)}, bf16[512,1792]{1,0:T(8,128)(2,1)}, u32[]{:S(2)}, u32[]{:S(2)}) collective-permute-start(bf16[512,1792]{1,0:T(8,128)(2,1)} %refs_0_), channel_id=1, source_target_pairs={{0,2},{2,0},{4,6},{6,4},{8,10},{10,8},{12,14},{14,12},{1,3},{3,1},... | collective-permute-start | bytes 5505032 | tf_op jit(solution)/shard_map/own_x/ppermute | solution.py:60
  43.3 41.9 %collective-permute-start.4 = (bf16[512,1792]{1,0:T(8,128)(2,1)}, bf16[512,1792]{1,0:T(8,128)(2,1)S(1)}, u32[]{:S(2)}, u32[]{:S(2)}) collective-permute-start(bf16[512,1792]{1,0:T(8,128)(2,1)} %collective-permute-done.2.refs_0_.refs_1_), channel_id=1, source_target_pairs={{0,2},{2,0},{4,8},{6,10},{8,4},{10,6},{12,14},{14,12},{1,3},{3,1},... | collective-permute-start | bytes 5505032 | tf_op jit(solution)/shard_map/near_on/ppermute | solution.py:60
  47.8 42.1 %collective-permute-start.3 = (bf16[512,1792]{1,0:T(8,128)(2,1)}, bf16[512,1792]{1,0:T(8,128)(2,1)}, u32[]{:S(2)}, u32[]{:S(2)}) collective-permute-start(bf16[512,1792]{1,0:T(8,128)(2,1)} %make.16), channel_id=1, source_target_pairs={{0,4},{2,6},{4,0},{6,2},{8,12},{10,14},{12,8},{14,10},{1,5},{3,7},... | collective-permute-start | bytes 5505032 | tf_op jit(solution)/shard_map/r1/ppermute | solution.py:60
  49.4 53.4 %collective-permute-start.7 = (bf16[512,1792]{1,0:T(8,128)(2,1)}, bf16[512,1792]{1,0:T(8,128)(2,1)}, u32[]{:S(2)}, u32[]{:S(2)}) collective-permute-start(bf16[512,1792]{1,0:T(8,128)(2,1)} %collective-permute-done.1.refs_1_), channel_id=1, source_target_pairs={{4,6},{6,4},{8,10},{10,8},{20,22},{22,20},{24,26},{26,24},{0,16},{... | collective-permute-start | bytes 5505032 | tf_op jit(solution)/shard_map/mid_own_x/ppermute | solution.py:60
  85.3 1.3 copy-start
  89.0 32.5 %collective-permute-start.6 = (bf16[512,1280]{1,0:T(8,128)(2,1)}, bf16[512,1280]{1,0:T(8,128)(2,1)}, u32[]{:S(2)}, u32[]{:S(2)}) collective-permute-start(bf16[512,1280]{1,0:T(8,128)(2,1)} %make.17), channel_id=1, source_target_pairs={{0,4},{2,6},{4,0},{6,2},{8,12},{10,14},{12,8},{14,10},{1,5},{3,7},... | collective-permute-start | bytes 3932168 | tf_op jit(solution)/shard_map/r2_h/ppermute | solution.py:60
  92.7 43.3 %collective-permute-start.10 = (bf16[512,1792]{1,0:T(8,128)(2,1)}, bf16[512,1792]{1,0:T(8,128)(2,1)}, u32[]{:S(2)}, u32[]{:S(2)}) collective-permute-start(bf16[512,1792]{1,0:T(8,128)(2,1)} %make.18), channel_id=1, source_target_pairs={{0,2},{2,0},{4,6},{6,4},{8,10},{10,8},{12,14},{14,12},{1,3},{3,1},... | collective-permute-start | bytes 5505032 | tf_op jit(solution)/shard_map/x2/ppermute | solution.py:60
  96.5 29.4 %collective-permute-start.5 = (bf16[512,1024]{1,0:T(8,128)(2,1)}, bf16[512,1024]{1,0:T(8,128)(2,1)}, u32[]{:S(2)}, u32[]{:S(2)}) collective-permute-start(bf16[512,1024]{1,0:T(8,128)(2,1)} %make.19), channel_id=1, source_target_pairs={{4,8},{6,10},{8,4},{10,6},{20,24},{22,26},{24,20},{26,22},{0,16},{... | collective-permute-start | bytes 3145736 | tf_op jit(solution)/shard_map/mid_a/ppermute | solution.py:60
  98.1 4.7 %copy-start.1 = (bf16[512,1792]{1,0:T(8,128)(2,1)S(1)}, bf16[512,1792]{1,0:T(8,128)(2,1)}, u32[]{:S(2)}) copy-start(bf16[512,1792]{1,0:T(8,128)(2,1)} %copy-done) | copy-start | bytes 5505028
  100.6 43.8 %collective-permute-start.9 = (bf16[512,1024]{1,0:T(8,128)(2,1)}, bf16[512,1024]{1,0:T(8,128)(2,1)S(1)}, u32[]{:S(2)}, u32[]{:S(2)}) collective-permute-start(bf16[512,1024]{1,0:T(8,128)(2,1)} %make.20), channel_id=1, source_target_pairs={{0,4},{2,6},{4,0},{6,2},{8,12},{10,14},{12,8},{14,10},{1,5},{3,7},... | collective-permute-start | bytes 3145736 | tf_op jit(solution)/shard_map/r2_t/ppermute | solution.py:60
  123.9 24.7 %collective-permute-start.13 = (bf16[512,1024]{1,0:T(8,128)(2,1)}, bf16[512,1024]{1,0:T(8,128)(2,1)}, u32[]{:S(2)}, u32[]{:S(2)}) collective-permute-start(bf16[512,1024]{1,0:T(8,128)(2,1)} %make.21), channel_id=1, source_target_pairs={{4,8},{6,10},{8,4},{10,6},{20,24},{22,26},{24,20},{26,22},{0,16},{... | collective-permute-start | bytes 3145736 | tf_op jit(solution)/shard_map/mid_b/ppermute | solution.py:60
  125.4 38.1 %collective-permute-start.16 = (bf16[512,1280]{1,0:T(8,128)(2,1)}, bf16[512,1280]{1,0:T(8,128)(2,1)}, u32[]{:S(2)}, u32[]{:S(2)}) collective-permute-start(bf16[512,1280]{1,0:T(8,128)(2,1)} %collective-permute-done.6.refs_1_.refs_5_.refs_0_), channel_id=1, source_target_pairs={{0,2},{2,0},{12,14},{14,12},{16,18},{18,16},{28,30},{30,28},{4,20}... | collective-permute-start | bytes 3932168 | tf_op jit(solution)/shard_map/x3_h/ppermute | solution.py:60
  128.2 16.2 %collective-permute-start.8 = (bf16[512,512]{1,0:T(8,128)(2,1)}, bf16[512,512]{1,0:T(8,128)(2,1)S(1)}, u32[]{:S(2)}, u32[]{:S(2)}) collective-permute-start(bf16[512,512]{1,0:T(8,128)(2,1)} %make.22), channel_id=1, source_target_pairs={{4,6},{6,4},{8,10},{10,8},{5,7},{7,5},{9,11},{11,9},{20,22},{22,20... | collective-permute-start | bytes 1572872 | tf_op jit(solution)/shard_map/sum_x_a/ppermute | solution.py:60
  144.4 2.1 copy-start.2
  146.6 3.6 %copy-start.4 = (bf16[512,512]{1,0:T(8,128)(2,1)}, bf16[512,512]{1,0:T(8,128)(2,1)S(1)}, u32[]{:S(2)}) copy-start(bf16[512,512]{1,0:T(8,128)(2,1)S(1)} %make.23.refs_1_) | copy-start | bytes 1572868
  146.6 11.2 %collective-permute-start.12 = (bf16[512,512]{1,0:T(8,128)(2,1)S(1)}, bf16[512,512]{1,0:T(8,128)(2,1)S(1)}, u32[]{:S(2)}, u32[]{:S(2)}) collective-permute-start(bf16[512,512]{1,0:T(8,128)(2,1)S(1)} %make.23.refs_1_), channel_id=1, source_target_pairs={{0,4},{2,6},{4,0},{6,2},{8,12},{10,14},{12,8},{14,10},{1,5},{3,7},... | collective-permute-start | bytes 1572872 | tf_op jit(solution)/shard_map/all_in_0a/ppermute | solution.py:60
  147.9 9.9 %collective-permute-start.11 = (bf16[512,512]{1,0:T(8,128)(2,1)S(1)}, bf16[512,512]{1,0:T(8,128)(2,1)S(1)}, u32[]{:S(2)}, u32[]{:S(2)}) collective-permute-start(bf16[512,512]{1,0:T(8,128)(2,1)S(1)} %make.23.refs_1_), channel_id=1, source_target_pairs={{4,8},{6,10},{8,4},{10,6},{5,9},{7,11},{9,5},{11,7},{20,24},{22,26... | collective-permute-start | bytes 1572872 | tf_op jit(solution)/shard_map/all_mid_a/ppermute | solution.py:60
  150.1 14.6 %collective-permute-start.15 = (bf16[512,512]{1,0:T(8,128)(2,1)S(1)}, bf16[512,512]{1,0:T(8,128)(2,1)S(1)}, u32[]{:S(2)}, u32[]{:S(2)}) collective-permute-start(bf16[512,512]{1,0:T(8,128)(2,1)S(1)} %make.24), channel_id=1, source_target_pairs={{4,6},{6,4},{8,10},{10,8},{5,7},{7,5},{9,11},{11,9},{20,22},{22,20... | collective-permute-start | bytes 1572872 | tf_op jit(solution)/shard_map/sum_x_b/ppermute | solution.py:60
  157.8 6.9 %copy-start.6 = (bf16[512,512]{1,0:T(8,128)(2,1)}, bf16[512,512]{1,0:T(8,128)(2,1)S(1)}, u32[]{:S(2)}) copy-start(bf16[512,512]{1,0:T(8,128)(2,1)S(1)} %collective-permute-done.11.refs_1_) | copy-start | bytes 1572868
  159.9 16.8 %collective-permute-start.14 = (bf16[512,512]{1,0:T(8,128)(2,1)}, bf16[512,512]{1,0:T(8,128)(2,1)}, u32[]{:S(2)}, u32[]{:S(2)}) collective-permute-start(bf16[512,512]{1,0:T(8,128)(2,1)} %make.26), channel_id=1, source_target_pairs={{0,4},{2,6},{4,0},{6,2},{8,12},{10,14},{12,8},{14,10},{1,5},{3,7},... | collective-permute-start | bytes 1572872 | tf_op jit(solution)/shard_map/all_in_1a/ppermute | solution.py:60
  163.5 25.0 %collective-permute-start.20 = (bf16[512,512]{1,0:T(8,128)(2,1)}, bf16[512,512]{1,0:T(8,128)(2,1)}, u32[]{:S(2)}, u32[]{:S(2)}) collective-permute-start(bf16[512,512]{1,0:T(8,128)(2,1)} %make.25), channel_id=1, source_target_pairs={{0,2},{2,0},{4,6},{6,4},{8,10},{10,8},{12,14},{14,12},{1,3},{3,1},... | collective-permute-start | bytes 1572872 | tf_op jit(solution)/shard_map/x3_t/ppermute | solution.py:60
  167.1 12.6 %copy-start.3 = (bf16[512,1024]{1,0:T(8,128)(2,1)S(1)}, bf16[512,1024]{1,0:T(8,128)(2,1)}, u32[]{:S(2)}) copy-start(bf16[512,1024]{1,0:T(8,128)(2,1)} %copy-done.2) | copy-start | bytes 3145732
  167.1 21.4 %collective-permute-start.19 = (bf16[512,512]{1,0:T(8,128)(2,1)}, bf16[512,512]{1,0:T(8,128)(2,1)}, u32[]{:S(2)}, u32[]{:S(2)}) collective-permute-start(bf16[512,512]{1,0:T(8,128)(2,1)} %make.27.refs_1_), channel_id=1, source_target_pairs={{0,4},{2,6},{4,0},{6,2},{8,12},{10,14},{12,8},{14,10},{1,5},{3,7},... | collective-permute-start | bytes 1572872 | tf_op jit(solution)/shard_map/all_in_0b/ppermute | solution.py:60
  170.4 18.1 %collective-permute-start.18 = (bf16[512,512]{1,0:T(8,128)(2,1)}, bf16[512,512]{1,0:T(8,128)(2,1)}, u32[]{:S(2)}, u32[]{:S(2)}) collective-permute-start(bf16[512,512]{1,0:T(8,128)(2,1)} %make.27.refs_1_), channel_id=1, source_target_pairs={{4,8},{6,10},{8,4},{10,6},{5,9},{7,11},{9,5},{11,7},{20,24},{22,26... | collective-permute-start | bytes 1572872 | tf_op jit(solution)/shard_map/all_mid_b/ppermute | solution.py:60
  172.0 1.0 copy-start.5
  173.0 3.7 %copy-start.7 = (bf16[512,512]{1,0:T(8,128)(2,1)S(1)}, bf16[512,512]{1,0:T(8,128)(2,1)}, u32[]{:S(2)}) copy-start(bf16[512,512]{1,0:T(8,128)(2,1)} %copy-done.6) | copy-start | bytes 1572868
  173.9 17.4 %collective-permute-start.22 = (bf16[512,512]{1,0:T(8,128)(2,1)}, bf16[512,512]{1,0:T(8,128)(2,1)}, u32[]{:S(2)}, u32[]{:S(2)}) collective-permute-start(bf16[512,512]{1,0:T(8,128)(2,1)} %make.28.refs_0_), channel_id=1, source_target_pairs={{0,2},{2,0},{4,6},{6,4},{8,10},{10,8},{12,14},{14,12},{1,3},{3,1},... | collective-permute-start | bytes 1572872 | tf_op jit(solution)/shard_map/all_x_0a/ppermute | solution.py:60
  178.6 22.9 %collective-permute-start.17 = (bf16[512,512]{1,0:T(8,128)(2,1)}, bf16[512,512]{1,0:T(8,128)(2,1)}, u32[]{:S(2)}, u32[]{:S(2)}) collective-permute-start(bf16[512,512]{1,0:T(8,128)(2,1)} %make.29.refs_1_), channel_id=1, source_target_pairs={{0,2},{2,0},{4,6},{6,4},{8,10},{10,8},{12,14},{14,12},{1,3},{3,1},... | collective-permute-start | bytes 1572872 | tf_op jit(solution)/shard_map/all_x_1a/ppermute | solution.py:60
  188.6 12.9 %collective-permute-start.21 = (bf16[512,512]{1,0:T(8,128)(2,1)}, bf16[512,512]{1,0:T(8,128)(2,1)S(1)}, u32[]{:S(2)}, u32[]{:S(2)}) collective-permute-start(bf16[512,512]{1,0:T(8,128)(2,1)} %collective-permute-done.18.refs_1_), channel_id=1, source_target_pairs={{4,0},{6,2},{8,12},{10,14},{5,1},{7,3},{9,13},{11,15},{20,16},{22,... | collective-permute-start | bytes 1572872 | tf_op jit(solution)/shard_map/all_in_1b/ppermute | solution.py:60
  201.4 4.1 %collective-permute-start.24 = (f32[512,896]{1,0:T(8,128)}, f32[512,896]{1,0:T(8,128)S(1)}, u32[]{:S(2)}, u32[]{:S(2)}) collective-permute-start(f32[512,896]{1,0:T(8,128)} %get-tuple-element.134), channel_id=1, source_target_pairs={{0,1},{1,0},{2,3},{3,2},{4,5},{5,4},{6,7},{7,6},{8,9},{9,8},{10,11... | collective-permute-start | bytes 5505032 | tf_op jit(solution)/shard_map/core_high/ppermute | solution.py:60
  201.5 6.6 %collective-permute-start.23 = (f32[512,896]{1,0:T(8,128)}, f32[512,896]{1,0:T(8,128)S(1)}, u32[]{:S(2)}, u32[]{:S(2)}) collective-permute-start(f32[512,896]{1,0:T(8,128)} %get-tuple-element.132), channel_id=1, source_target_pairs={{0,1},{1,0},{2,3},{3,2},{4,5},{5,4},{6,7},{7,6},{8,9},{9,8},{10,11... | collective-permute-start | bytes 5505032 | tf_op jit(solution)/shard_map/core_low/ppermute | solution.py:60
  202.2 15.5 %collective-permute-start.26 = (bf16[512,512]{1,0:T(8,128)(2,1)S(1)}, bf16[512,512]{1,0:T(8,128)(2,1)S(1)}, u32[]{:S(2)}, u32[]{:S(2)}) collective-permute-start(bf16[512,512]{1,0:T(8,128)(2,1)S(1)} %make.30.refs_0_), channel_id=1, source_target_pairs={{0,2},{2,0},{4,6},{6,4},{8,10},{10,8},{12,14},{14,12},{1,3},{3,1},... | collective-permute-start | bytes 1572872 | tf_op jit(solution)/shard_map/all_x_0b/ppermute | solution.py:60
  204.2 4.0 %copy-start.8 = (f32[512,896]{1,0:T(8,128)S(1)}, f32[512,896]{1,0:T(8,128)}, u32[]{:S(2)}) copy-start(f32[512,896]{1,0:T(8,128)} %get-tuple-element.132) | copy-start | bytes 5505028
  204.2 23.1 %collective-permute-start.25 = (bf16[512,512]{1,0:T(8,128)(2,1)S(1)}, bf16[512,512]{1,0:T(8,128)(2,1)S(1)}, u32[]{:S(2)}, u32[]{:S(2)}) collective-permute-start(bf16[512,512]{1,0:T(8,128)(2,1)S(1)} %make.31.refs_1_), channel_id=1, source_target_pairs={{0,2},{2,0},{4,6},{6,4},{8,10},{10,8},{12,14},{14,12},{1,3},{3,1},... | collective-permute-start | bytes 1572872 | tf_op jit(solution)/shard_map/all_x_1b/ppermute | solution.py:60
